TPU v7x, 512 devices: a whole 4x4x16 slice. The times are simulated.
512 devices in a mesh: replica: 32 (over z_lo, y), fsdp: 8 (over z_hi, x), tensor: 2 (over core).
Axes of the slice: x: 4, y: 4, z: 16 (z_hi: 2, z_lo: 8; z = z_hi * 8 + z_lo), core: 2. Of those that a mesh axis runs over, the one named last changes fastest.
Arguments:
- w_local: bfloat16 [32, 10240, 512], P('replica', 'fsdp', 'tensor'), may hold values from -24 to 24
- anchor: bfloat16 [10240, 512], P('fsdp', 'tensor'), may hold values from -20 to 20
- momentum: float32 [8, 32, 40, 512], P('fsdp', 'replica', None, 'tensor'), may hold values from -4 to 4
- key_grad: bfloat16 [32, 2304, 512], P('replica', 'fsdp', 'tensor'), may hold values from -0.25 to 0.25
Outputs:
- new_weights: bfloat16 [10240, 512], P('fsdp', 'tensor')
- new_momentum: float32 [8, 32, 40, 512], P('fsdp', 'replica', None, 'tensor')
- input_grad: bfloat16 [32, 8, 288, 10240], P('replica', None, 'tensor', 'fsdp')
- max_scale: float32 [1], replicated
All inputs are finite; a program needn't handle non-finite values.
Results may differ from a plain program's by a relative error of at most 0.006.
Values may be sent and summed in bfloat16 or wider, within the bound.
No kernel may reach another device: no remote copies, remote signals or barrier semaphores. Data moves between devices by JAX's collectives and lax.ppermute only.
A program may use at most 64 MiB of HBM per device.

v0:
```python
import jax
import jax.numpy as jnp
from jax import lax
from jax.sharding import PartitionSpec as P

OUTER_MOMENTUM = 0.9
OUTER_RATE = 0.7
EPSILON = 1e-06


def project_rows(segment, key_weight):
    product = lax.dot_general(
        segment,
        key_weight,
        (((segment.ndim - 1,), (1,)), ((), ())),
        preferred_element_type=jnp.float32,
    )
    return product.astype(jnp.bfloat16)


def body(w_local, anchor, momentum, key_grad):
    key_weight = lax.all_gather(w_local, "tensor", axis=2, tiled=True)[0]
    fsdp_count = lax.axis_size("fsdp")
    halves = lax.all_to_all(key_grad, "tensor", split_axis=1, concat_axis=2, tiled=True)
    projected = project_rows(lax.all_gather(halves, "fsdp", axis=1, tiled=True), key_weight)
    input_grad = projected.reshape(1, fsdp_count, halves.shape[1], projected.shape[2])
    pseudo_grad = anchor.astype(jnp.float32) - w_local[0].astype(jnp.float32)
    max_scale = lax.pmax(jnp.max(jnp.abs(pseudo_grad)), ("replica", "fsdp", "tensor")) + EPSILON
    coded_grad = (pseudo_grad / max_scale).astype(jnp.bfloat16)
    shard_rows = momentum.shape[2]
    row_start = lax.axis_index("replica") * shard_rows
    replica_count = lax.axis_size("replica")
    summed = lax.psum_scatter(
        coded_grad.astype(jnp.float32), "replica", scatter_dimension=0, tiled=True
    )
    mean_drift = summed * max_scale / replica_count
    moment_new = OUTER_MOMENTUM * momentum[0, 0] + mean_drift
    anchor_rows = lax.dynamic_slice_in_dim(anchor, row_start, shard_rows, 0).astype(jnp.float32)
    updated = (anchor_rows - OUTER_RATE * (mean_drift + OUTER_MOMENTUM * moment_new)).astype(
        jnp.bfloat16
    )
    new_weights = lax.all_gather(updated, "replica", axis=0, tiled=True)
    new_momentum = moment_new[None, None]
    scale_out = jnp.reshape(max_scale, (1,))
    return (new_weights, new_momentum, input_grad, scale_out)


def solution(mesh):
    return jax.shard_map(
        body,
        mesh=mesh,
        in_specs=(
            P("replica", "fsdp", "tensor"),
            P("fsdp", "tensor"),
            P("fsdp", "replica", None, "tensor"),
            P("replica", "fsdp", "tensor"),
        ),
        out_specs=(
            P("fsdp", "tensor"),
            P("fsdp", "replica", None, "tensor"),
            P("replica", None, "tensor", "fsdp"),
            P(),
        ),
        check_vma=False,
    )
```

profile of v0, /device:TPU:2, one launch (start us, length us, event | category | flops | bytes accessed | tf_op | source)
XLA Modules:
  0.0 514.1 jit_solution(1385163301425100671)
XLA Ops:
  8.0 0.0 all-gather.5.cloned.1.call-start
  8.0 0.7 all-gather.5.cloned.1.call-update
  8.7 0.0 copy-start
  8.7 0.0 copy-start.1
  8.8 0.0 all-gather.3.cloned.1.call-start
  8.8 1.2 copy.16
  10.0 0.5 broadcast.13
  10.5 1.5 reduce
  12.1 3.8 all_to_all.18
  15.9 0.1 reshape.29
  16.1 0.7 copy.14
  16.8 0.0 all-gather.3.cloned.1.call-update
  16.8 0.0 reduce-scatter.2.cloned.1.call-start
  16.8 0.0 copy-done
  16.9 0.0 copy-done.1
  16.9 0.7 abs_reduce_fusion
  17.6 129.3 %pmax.7 = f32[]{:T(128)} all-reduce(f32[]{:T(128)} %abs_reduce_fusion), channel_id=1, replica_groups=mesh['replica'=32,'fsdp'=8,'tensor'=2] {'replica','fsdp','tensor'}, use_global_device_ids=true, to_apply=%region_1.0 | all-reduce | flops 1 | bytes 8 | tf_op jit(solution)/shard_map/pmax | solution.py:28
  147.5 1.3 fusion.2
  148.8 0.0 reduce-scatter.2.cloned.1.call-update
  148.8 0.0 copy-start.2
  148.8 0.0 all-gather.5.cloned.1.call-done
  148.9 0.0 all-gather.3.cloned.1.call-done
  148.9 5.0 convolution_convert_fusion
  153.9 233.9 %reduce-scatter.2.cloned.1.call-done = f32[40,256]{1,0:T(8,128)} async-done(((f32[1280,256]{1,0:T(8,128)}), f32[40,256]{1,0:T(8,128)}) %reduce-scatter.2.cloned.1.call-update) | async-done | bytes 40976 | tf_op jit(solution)/shard_map/reduce_scatter | solution.py:33
  387.8 0.0 copy-done.2
  387.8 1.4 fusion.3
  389.2 115.5 %all_gather.9 = bf16[1280,256]{1,0:T(8,128)(2,1)S(1)} all-gather(bf16[40,256]{1,0:T(8,128)(2,1)S(1)} %get-tuple-element.5), channel_id=1, replica_groups=mesh['replica'=32,'fsdp'=8,'tensor'=2] {'replica'}, dimensions={0}, use_global_device_ids=true | all-gather | bytes 675840 | tf_op jit(solution)/shard_map/all_gather | solution.py:42
  504.7 0.8 copy.18
  (2 shorter events, 0.1 us)
Async XLA Ops:
  8.0 140.9 %all-gather.5.cloned.1.call-start = ((), (), s32[]{:S(2)}) async-start(), calls=%async_computation.4 | async-start | bytes 1966080 | tf_op jit(solution)/shard_map/all_gather | solution.py:22
  8.7 8.1 %copy-start = (bf16[1,1280,256]{2,1,0:T(8,128)(2,1)S(1)}, bf16[1,1280,256]{2,1,0:T(8,128)(2,1)}, u32[]{:S(2)}) copy-start(bf16[1,1280,256]{2,1,0:T(8,128)(2,1)} %param.4) | copy-start | bytes 1966084
  8.7 8.1 %copy-start.1 = (bf16[1280,256]{1,0:T(8,128)(2,1)S(1)}, bf16[1280,256]{1,0:T(8,128)(2,1)}, u32[]{:S(2)}) copy-start(bf16[1280,256]{1,0:T(8,128)(2,1)} %param.5) | copy-start | bytes 1966084
  8.8 140.1 %all-gather.3.cloned.1.call-start = ((), (), s32[]{:S(2)}) async-start(), calls=%async_computation.3 | async-start | bytes 1327104 | tf_op jit(solution)/shard_map/all_gather | solution.py:25
  16.8 371.0 %reduce-scatter.2.cloned.1.call-start = ((), (), s32[]{:S(2)}) async-start(), calls=%async_computation.2 | async-start | bytes 1351680 | tf_op jit(solution)/shard_map/reduce_scatter | solution.py:33
  148.8 238.9 %copy-start.2 = (f32[1,1,40,256]{3,2,1,0:T(8,128)S(1)}, f32[1,1,40,256]{3,2,1,0:T(8,128)}, u32[]{:S(2)}) copy-start(f32[1,1,40,256]{3,2,1,0:T(8,128)} %param.6) | copy-start | bytes 122884
Sparse Core Ops, SparseCore 0:
  11.1 24.2 all-gather.4
  39.7 96.3 all-gather.2
Sparse Core Ops, SparseCore 1:
  148.9 238.8 reduce-scatter.1
where the time goes:
time: 514 us
  blocking collectives  249 us (48%)
  waiting for transfers between devices  235 us (46%)
  between operations  17.4 us (3%)
    reduce_scatter x1, waiting for transfers between devices, body(): lax.psum_scatter(coded_grad.astype(jnp.float32), 'replica', scatter_dimen...  234 us
    pmax x1, blocking collectives, body(): lax.pmax(jnp.max(jnp.abs(pseudo_grad)), ('replica', 'fsdp', 'tensor'))  129 us
    all_gather x1, blocking collectives, body(): new_weights = lax.all_gather(updated, 'replica', axis=0, tiled=True)  115 us
  transfers between devices with their start and end apart: 3, of which 1 were waited for; matrix products, arithmetic and copies ran while one was open for 2% of the time, Pallas kernels for 0%

commit v1 on v0

v1 whole, which is shorter than its diff:
```python
import jax
import jax.numpy as jnp
from jax import lax
from jax.sharding import PartitionSpec as P

OUTER_MOMENTUM = 0.9
OUTER_RATE = 0.7
EPSILON = 1e-06
N_REPLICA = 32
STEP_GAIN = OUTER_RATE * (1.0 + OUTER_MOMENTUM) / N_REPLICA
MOMENTUM_GAIN = OUTER_MOMENTUM * OUTER_MOMENTUM * N_REPLICA / (1.0 + OUTER_MOMENTUM)
F32, BF16 = jnp.float32, jnp.bfloat16


def swap(x, axis, bit):
    n = lax.axis_size(axis)
    return lax.ppermute(x, axis, [(i, i ^ bit) for i in range(n)])


def pick(x, index, axis):
    return lax.dynamic_index_in_dim(x, index, axis, keepdims=False)


def body(w_local, anchor, momentum, key_grad):
    r = lax.axis_index("replica")
    y, hi, lo = r & 3, r >> 4, (r >> 2) & 3
    f = lax.axis_index("fsdp")
    t = lax.axis_index("tensor")
    w = w_local[0]
    cols = w.shape[1]

    kg = key_grad[0]
    tokens = kg.shape[0]
    half = tokens // 2
    pair = jnp.stack([kg, swap(kg, "fsdp", 4)])
    rows = jnp.concatenate([pair] + [swap(pair, "fsdp", d) for d in (1, 2, 3)])
    rows = rows.reshape(8, 2, half, cols)
    mine, theirs = pick(rows, t, 1), pick(rows, 1 - t, 1)
    other = swap(theirs, "tensor", 1)
    w_other = swap(w, "tensor", 1)
    dims = (((2,), (1,)), ((), ()))

    w4 = w.reshape(8, 4, 40, cols)
    a4 = anchor.reshape(8, 4, 40, cols)
    a_y = pick(a4, y, 1).astype(F32)
    parts = [pick(w4, y, 1)] + [swap(pick(w4, y ^ d, 1), "replica", d) for d in (1, 2, 3)]
    p1 = sum(a_y - p.astype(F32) for p in parts)
    p1 = p1.reshape(2, 4, 40, cols)
    send = pick(p1, 1 - hi, 0).astype(BF16)
    p2 = pick(p1, hi, 0) + swap(send, "replica", 16).astype(F32)
    m = momentum[0, 0]
    own = lax.broadcasted_iota(jnp.int32, (4, 1, 1), 0) == lo
    q = (p2 + jnp.where(own, MOMENTUM_GAIN * m[None], 0.0)).astype(BF16)
    got = [swap(q, "replica", 4 * d).astype(F32) for d in (1, 2, 3)]
    total = (q.astype(F32) + got[0]) + (got[1] + got[2])
    summed = pick(p2, lo, 0) + sum(pick(g, lo, 0) for g in got)
    moment_new = OUTER_MOMENTUM * m + summed / N_REPLICA
    a_hi = pick(a_y.reshape(2, 4, 40, cols), hi, 0)
    fresh = (a_hi - STEP_GAIN * total).astype(BF16)
    far = swap(fresh, "replica", 16)
    eight = jnp.where(hi == 0, jnp.stack([fresh, far]), jnp.stack([far, fresh])).reshape(8, 40, cols)
    pieces = [eight] + [swap(eight, "replica", d) for d in (1, 2, 3)]
    out = jnp.zeros((8, 4, 40, cols), BF16)
    for d in range(4):
        out = lax.dynamic_update_index_in_dim(out, pieces[d], y ^ d, 1)
    new_weights = out.reshape(1280, cols)

    scale = jnp.max(jnp.abs(anchor.astype(F32) - w.astype(F32)))
    scale = jnp.full((8, 128), scale, F32)
    for axis, masks in (("tensor", (1,)), ("replica", (1, 2, 3)), ("replica", (4, 8, 12)), ("replica", (16,)), ("fsdp", (4,)), ("fsdp", (1, 2, 3))):
        got_s = [swap(scale, axis, k) for k in masks]
        for g in got_s:
            scale = jnp.maximum(scale, g)
    max_scale = scale[0, :1] + EPSILON

    where = jnp.array([0, 2, 4, 6, 1, 3, 5, 7])[jnp.arange(8) ^ f]
    a_in = jnp.take(jnp.concatenate([mine, other], axis=2), where, axis=0)
    w_in = jnp.concatenate([w, w_other], axis=1)
    prod = lax.dot_general(a_in, w_in, dims, preferred_element_type=F32).astype(BF16)
    input_grad = prod[None]
    return new_weights, moment_new[None, None], input_grad, max_scale


def solution(mesh):
    return jax.shard_map(
        body,
        mesh=mesh,
        in_specs=(
            P("replica", "fsdp", "tensor"),
            P("fsdp", "tensor"),
            P("fsdp", "replica", None, "tensor"),
            P("replica", "fsdp", "tensor"),
        ),
        out_specs=(
            P("fsdp", "tensor"),
            P("fsdp", "replica", None, "tensor"),
            P("replica", None, "tensor", "fsdp"),
            P(),
        ),
        check_vma=False,
    )
```

time: 514 us -> 175 us (0.34)
  the two profiles are of different devices: /device:TPU:2 before, /device:TPU:24 now
where the time goes in v1:
time: 175 us; the launch traced here: 172 us
  starting transfers between devices  123 us (70%)
  waiting for transfers between devices  29.1 us (17%)
  other arithmetic  8.22 us (5%)
  local copies, waits for them, and re-layouts  4.77 us (3%)
  matrix products  4.43 us (3%)
  between operations  3.13 us (2%)
    ppermute x29, starting transfers between devices, swap(): return lax.ppermute(x, axis, [(i, i ^ bit) for i in range(n)])  123 us
    ppermute x29, waiting for transfers between devices, swap(): return lax.ppermute(x, axis, [(i, i ^ bit) for i in range(n)])  29.1 us
    dot_general x1, matrix products, body(): lax.dot_general(a_in, w_in, dims, preferred_element_type=F32).astype(BF16)  4.43 us
  transfers between devices with their start and end apart: 29, of which 7 were waited for; matrix products, arithmetic and copies ran while one was open for 6% of the time, Pallas kernels for 0%

profile of v1, /device:TPU:24, one launch (start us, length us, event | category | flops | bytes accessed | tf_op | source)
XLA Modules:
  0.0 172.5 jit_solution(6808836973073326689)
XLA Ops:
  1.9 7.6 %collective-permute-start.2 = (bf16[8,40,256]{2,1,0:T(8,128)(2,1)S(1)}, bf16[8,40,256]{2,1,0:T(8,128)(2,1)}, u32[]{:S(2)}, u32[]{:S(2)}) collective-permute-start(bf16[8,40,256]{2,1,0:T(8,128)(2,1)S(1)} %get-tuple-element.9), channel_id=1, source_target_pairs={{0,48},{16,32},{32,16},{48,0},{64,112},{80,96},{96,80},{112,64},{1... | collective-permute-start | bytes 491528 | tf_op jit(solution)/shard_map/ppermute | solution.py:17
  9.5 2.1 %collective-permute-start.1 = (bf16[8,40,256]{2,1,0:T(8,128)(2,1)S(1)}, bf16[8,40,256]{2,1,0:T(8,128)(2,1)}, u32[]{:S(2)}, u32[]{:S(2)}) collective-permute-start(bf16[8,40,256]{2,1,0:T(8,128)(2,1)S(1)} %get-tuple-element.10), channel_id=1, source_target_pairs={{0,32},{16,48},{32,0},{48,16},{64,96},{80,112},{96,64},{112,80},{1... | collective-permute-start | bytes 491528 | tf_op jit(solution)/shard_map/ppermute | solution.py:17
  14.1 1.9 %collective-permute-start.17 = (f32[8,128]{1,0:T(8,128)S(1)}, f32[8,128]{1,0:T(8,128)S(1)}, u32[]{:S(2)}, u32[]{:S(2)}) collective-permute-start(f32[8,128]{1,0:T(8,128)S(1)} %broadcast_in_dim.62), channel_id=1, source_target_pairs={{0,1},{1,0},{2,3},{3,2},{4,5},{5,4},{6,7},{7,6},{8,9},{9,8},{10,11... | collective-permute-start | bytes 12296 | tf_op jit(solution)/shard_map/ppermute | solution.py:17
  17.9 1.9 %collective-permute-start.20 = (f32[8,128]{1,0:T(8,128)S(1)}, f32[8,128]{1,0:T(8,128)S(1)}, u32[]{:S(2)}, u32[]{:S(2)}) collective-permute-start(f32[8,128]{1,0:T(8,128)S(1)} %broadcast_maximum_fusion), channel_id=1, source_target_pairs={{0,48},{16,32},{32,16},{48,0},{64,112},{80,96},{96,80},{112,64},{1... | collective-permute-start | bytes 12296 | tf_op jit(solution)/shard_map/ppermute | solution.py:17
  19.8 5.4 %collective-permute-start.19 = (f32[8,128]{1,0:T(8,128)S(1)}, f32[8,128]{1,0:T(8,128)S(1)}, u32[]{:S(2)}, u32[]{:S(2)}) collective-permute-start(f32[8,128]{1,0:T(8,128)S(1)} %broadcast_maximum_fusion), channel_id=1, source_target_pairs={{0,32},{16,48},{32,0},{48,16},{64,96},{80,112},{96,64},{112,80},{1... | collective-permute-start | bytes 12296 | tf_op jit(solution)/shard_map/ppermute | solution.py:17
  25.3 2.5 %collective-permute-start.18 = (f32[8,128]{1,0:T(8,128)S(1)}, f32[8,128]{1,0:T(8,128)S(1)}, u32[]{:S(2)}, u32[]{:S(2)}) collective-permute-start(f32[8,128]{1,0:T(8,128)S(1)} %broadcast_maximum_fusion), channel_id=1, source_target_pairs={{0,16},{16,0},{32,48},{48,32},{64,80},{80,64},{96,112},{112,96},{1... | collective-permute-start | bytes 12296 | tf_op jit(solution)/shard_map/ppermute | solution.py:17
  28.3 2.5 %collective-permute-done.18 = f32[8,128]{1,0:T(8,128)S(1)} collective-permute-done((f32[8,128]{1,0:T(8,128)S(1)}, f32[8,128]{1,0:T(8,128)S(1)}, u32[]{:S(2)}, u32[]{:S(2)}) %collective-permute-start.18) | collective-permute-done | bytes 4128 | tf_op jit(solution)/shard_map/ppermute | solution.py:17
  31.4 3.6 %collective-permute-start.23 = (f32[8,128]{1,0:T(8,128)S(1)}, f32[8,128]{1,0:T(8,128)S(1)}, u32[]{:S(2)}, u32[]{:S(2)}) collective-permute-start(f32[8,128]{1,0:T(8,128)S(1)} %maximum_maximum_fusion.2), channel_id=1, source_target_pairs={{0,192},{16,208},{32,224},{48,240},{64,128},{80,144},{96,160},{112... | collective-permute-start | bytes 12296 | tf_op jit(solution)/shard_map/ppermute | solution.py:17
  35.0 1.9 %collective-permute-start.22 = (f32[8,128]{1,0:T(8,128)S(1)}, f32[8,128]{1,0:T(8,128)S(1)}, u32[]{:S(2)}, u32[]{:S(2)}) collective-permute-start(f32[8,128]{1,0:T(8,128)S(1)} %maximum_maximum_fusion.2), channel_id=1, source_target_pairs={{0,128},{16,144},{32,160},{48,176},{64,192},{80,208},{96,224},{112... | collective-permute-start | bytes 12296 | tf_op jit(solution)/shard_map/ppermute | solution.py:17
  36.9 4.6 %collective-permute-start.21 = (f32[8,128]{1,0:T(8,128)S(1)}, f32[8,128]{1,0:T(8,128)S(1)}, u32[]{:S(2)}, u32[]{:S(2)}) collective-permute-start(f32[8,128]{1,0:T(8,128)S(1)} %maximum_maximum_fusion.2), channel_id=1, source_target_pairs={{0,64},{16,80},{32,96},{48,112},{64,0},{80,16},{96,32},{112,48},{1... | collective-permute-start | bytes 12296 | tf_op jit(solution)/shard_map/ppermute | solution.py:17
  43.2 8.4 %collective-permute-start.24 = (f32[8,128]{1,0:T(8,128)S(1)}, f32[8,128]{1,0:T(8,128)S(1)}, u32[]{:S(2)}, u32[]{:S(2)}) collective-permute-start(f32[8,128]{1,0:T(8,128)S(1)} %maximum_maximum_fusion.1), channel_id=1, source_target_pairs={{0,256},{16,272},{32,288},{48,304},{64,320},{80,336},{96,352},{112... | collective-permute-start | bytes 12296 | tf_op jit(solution)/shard_map/ppermute | solution.py:17
  53.1 12.3 %collective-permute-start.25 = (f32[8,128]{1,0:T(8,128)S(1)}, f32[8,128]{1,0:T(8,128)S(1)}, u32[]{:S(2)}, u32[]{:S(2)}) collective-permute-start(f32[8,128]{1,0:T(8,128)S(1)} %max.43), channel_id=1, source_target_pairs={{0,8},{2,10},{4,12},{6,14},{8,0},{10,2},{12,4},{14,6},{1,9},{3,11}... | collective-permute-start | bytes 12296 | tf_op jit(solution)/shard_map/ppermute | solution.py:17
  67.3 4.7 %collective-permute-start.28 = (f32[8,128]{1,0:T(8,128)S(1)}, f32[8,128]{1,0:T(8,128)S(1)}, u32[]{:S(2)}, u32[]{:S(2)}) collective-permute-start(f32[8,128]{1,0:T(8,128)S(1)} %max.44), channel_id=1, source_target_pairs={{0,6},{2,4},{4,2},{6,0},{8,14},{10,12},{12,10},{14,8},{1,7},{3,5},... | collective-permute-start | bytes 12296 | tf_op jit(solution)/shard_map/ppermute | solution.py:17
  72.0 2.7 %collective-permute-start.27 = (f32[8,128]{1,0:T(8,128)S(1)}, f32[8,128]{1,0:T(8,128)S(1)}, u32[]{:S(2)}, u32[]{:S(2)}) collective-permute-start(f32[8,128]{1,0:T(8,128)S(1)} %max.44), channel_id=1, source_target_pairs={{0,4},{2,6},{4,0},{6,2},{8,12},{10,14},{12,8},{14,10},{1,5},{3,7},... | collective-permute-start | bytes 12296 | tf_op jit(solution)/shard_map/ppermute | solution.py:17
  74.7 2.4 %collective-permute-start.26 = (f32[8,128]{1,0:T(8,128)S(1)}, f32[8,128]{1,0:T(8,128)}, u32[]{:S(2)}, u32[]{:S(2)}) collective-permute-start(f32[8,128]{1,0:T(8,128)S(1)} %max.44), channel_id=1, source_target_pairs={{0,2},{2,0},{4,6},{6,4},{8,10},{10,8},{12,14},{14,12},{1,3},{3,1},... | collective-permute-start | bytes 12296 | tf_op jit(solution)/shard_map/ppermute | solution.py:17
  77.7 2.8 %collective-permute-start = (bf16[8,40,256]{2,1,0:T(8,128)(2,1)S(1)}, bf16[8,40,256]{2,1,0:T(8,128)(2,1)S(1)}, u32[]{:S(2)}, u32[]{:S(2)}) collective-permute-start(bf16[8,40,256]{2,1,0:T(8,128)(2,1)S(1)} %get-tuple-element.8), channel_id=1, source_target_pairs={{0,16},{16,0},{32,48},{48,32},{64,80},{80,64},{96,112},{112,96},{1... | collective-permute-start | bytes 491528 | tf_op jit(solution)/shard_map/ppermute | solution.py:17
  80.5 1.9 %collective-permute-start.16 = (bf16[1280,256]{1,0:T(8,128)(2,1)S(1)}, bf16[1280,256]{1,0:T(8,128)(2,1)}, u32[]{:S(2)}, u32[]{:S(2)}) collective-permute-start(bf16[1280,256]{1,0:T(8,128)(2,1)S(1)} %bitcast.88), channel_id=1, source_target_pairs={{0,1},{1,0},{2,3},{3,2},{4,5},{5,4},{6,7},{7,6},{8,9},{9,8},{10,11... | collective-permute-start | bytes 1966088 | tf_op jit(solution)/shard_map/ppermute | solution.py:17
  82.4 12.3 %collective-permute-start.11 = (bf16[288,256]{1,0:T(8,128)(2,1)S(1)}, bf16[288,256]{1,0:T(8,128)(2,1)S(1)}, u32[]{:S(2)}, u32[]{:S(2)}) collective-permute-start(bf16[288,256]{1,0:T(8,128)(2,1)S(1)} %bitcast.102), channel_id=1, source_target_pairs={{0,8},{2,10},{4,12},{6,14},{8,0},{10,2},{12,4},{14,6},{1,9},{3,11}... | collective-permute-start | bytes 442376 | tf_op jit(solution)/shard_map/ppermute | solution.py:17
  97.7 4.3 %collective-permute-start.3 = (bf16[4,40,256]{2,1,0:T(8,128)(2,1)S(1)}, bf16[4,40,256]{2,1,0:T(8,128)(2,1)S(1)}, u32[]{:S(2)}, u32[]{:S(2)}) collective-permute-start(bf16[4,40,256]{2,1,0:T(8,128)(2,1)S(1)} %fusion.10), channel_id=1, source_target_pairs={{0,256},{16,272},{32,288},{48,304},{64,320},{80,336},{96,352},{112... | collective-permute-start | bytes 245768 | tf_op jit(solution)/shard_map/ppermute | solution.py:17
  102.1 3.4 %collective-permute-start.12 = (bf16[2,288,256]{2,1,0:T(8,128)(2,1)S(1)}, bf16[2,288,256]{2,1,0:T(8,128)(2,1)S(1)}, u32[]{:S(2)}, u32[]{:S(2)}) collective-permute-start(bf16[2,288,256]{2,1,0:T(8,128)(2,1)S(1)} %pad_maximum_fusion.1), channel_id=1, source_target_pairs={{0,2},{2,0},{4,6},{6,4},{8,10},{10,8},{12,14},{14,12},{1,3},{3,1},... | collective-permute-start | bytes 884744 | tf_op jit(solution)/shard_map/ppermute | solution.py:17
  105.5 11.6 %collective-permute-done.3 = bf16[4,40,256]{2,1,0:T(8,128)(2,1)S(1)} collective-permute-done((bf16[4,40,256]{2,1,0:T(8,128)(2,1)S(1)}, bf16[4,40,256]{2,1,0:T(8,128)(2,1)S(1)}, u32[]{:S(2)}, u32[]{:S(2)}) %collective-permute-start.3) | collective-permute-done | bytes 81952 | tf_op jit(solution)/shard_map/ppermute | solution.py:17
  117.2 3.1 %collective-permute-start.6 = (bf16[4,40,256]{2,1,0:T(8,128)(2,1)S(1)}, bf16[4,40,256]{2,1,0:T(8,128)(2,1)S(1)}, u32[]{:S(2)}, u32[]{:S(2)}) collective-permute-start(bf16[4,40,256]{2,1,0:T(8,128)(2,1)S(1)} %get-tuple-element.4), channel_id=1, source_target_pairs={{0,192},{16,208},{32,224},{48,240},{64,128},{80,144},{96,160},{112... | collective-permute-start | bytes 245768 | tf_op jit(solution)/shard_map/ppermute | solution.py:17
  122.2 5.1 %collective-permute-start.4 = (bf16[4,40,256]{2,1,0:T(8,128)(2,1)S(1)}, bf16[4,40,256]{2,1,0:T(8,128)(2,1)S(1)}, u32[]{:S(2)}, u32[]{:S(2)}) collective-permute-start(bf16[4,40,256]{2,1,0:T(8,128)(2,1)S(1)} %get-tuple-element.4), channel_id=1, source_target_pairs={{0,64},{16,80},{32,96},{48,112},{64,0},{80,16},{96,32},{112,48},{1... | collective-permute-start | bytes 245768 | tf_op jit(solution)/shard_map/ppermute | solution.py:17
  127.3 4.9 %collective-permute-start.13 = (bf16[2,288,256]{2,1,0:T(8,128)(2,1)S(1)}, bf16[2,288,256]{2,1,0:T(8,128)(2,1)S(1)}, u32[]{:S(2)}, u32[]{:S(2)}) collective-permute-start(bf16[2,288,256]{2,1,0:T(8,128)(2,1)S(1)} %pad_maximum_fusion.1), channel_id=1, source_target_pairs={{0,4},{2,6},{4,0},{6,2},{8,12},{10,14},{12,8},{14,10},{1,5},{3,7},... | collective-permute-start | bytes 884744 | tf_op jit(solution)/shard_map/ppermute | solution.py:17
  132.3 3.0 %collective-permute-start.14 = (bf16[2,288,256]{2,1,0:T(8,128)(2,1)S(1)}, bf16[2,288,256]{2,1,0:T(8,128)(2,1)S(1)}, u32[]{:S(2)}, u32[]{:S(2)}) collective-permute-start(bf16[2,288,256]{2,1,0:T(8,128)(2,1)S(1)} %pad_maximum_fusion.1), channel_id=1, source_target_pairs={{0,6},{2,4},{4,2},{6,0},{8,14},{10,12},{12,10},{14,8},{1,7},{3,5},... | collective-permute-start | bytes 884744 | tf_op jit(solution)/shard_map/ppermute | solution.py:17
  135.4 5.6 %collective-permute-start.7 = (bf16[4,40,256]{2,1,0:T(8,128)(2,1)S(1)}, bf16[4,40,256]{2,1,0:T(8,128)(2,1)S(1)}, u32[]{:S(2)}, u32[]{:S(2)}) collective-permute-start(bf16[4,40,256]{2,1,0:T(8,128)(2,1)S(1)} %fusion.9), channel_id=1, source_target_pairs={{0,256},{16,272},{32,288},{48,304},{64,320},{80,336},{96,352},{112... | collective-permute-start | bytes 245768 | tf_op jit(solution)/shard_map/ppermute | solution.py:17
  141.8 7.4 %collective-permute-done.7 = bf16[4,40,256]{2,1,0:T(8,128)(2,1)S(1)} collective-permute-done((bf16[4,40,256]{2,1,0:T(8,128)(2,1)S(1)}, bf16[4,40,256]{2,1,0:T(8,128)(2,1)S(1)}, u32[]{:S(2)}, u32[]{:S(2)}) %collective-permute-start.7) | collective-permute-done | bytes 81952 | tf_op jit(solution)/shard_map/ppermute | solution.py:17
  149.2 3.2 %collective-permute-start.8 = (bf16[8,40,256]{2,1,0:T(8,128)(2,1)S(1)}, bf16[8,40,256]{2,1,0:T(8,128)(2,1)S(1)}, u32[]{:S(2)}, u32[]{:S(2)}) collective-permute-start(bf16[8,40,256]{2,1,0:T(8,128)(2,1)S(1)} %bitcast.97), channel_id=1, source_target_pairs={{0,16},{16,0},{32,48},{48,32},{64,80},{80,64},{96,112},{112,96},{1... | collective-permute-start | bytes 491528 | tf_op jit(solution)/shard_map/ppermute | solution.py:17
  152.5 3.1 %collective-permute-start.9 = (bf16[8,40,256]{2,1,0:T(8,128)(2,1)S(1)}, bf16[8,40,256]{2,1,0:T(8,128)(2,1)S(1)}, u32[]{:S(2)}, u32[]{:S(2)}) collective-permute-start(bf16[8,40,256]{2,1,0:T(8,128)(2,1)S(1)} %bitcast.99), channel_id=1, source_target_pairs={{0,32},{16,48},{32,0},{48,16},{64,96},{80,112},{96,64},{112,80},{1... | collective-permute-start | bytes 491528 | tf_op jit(solution)/shard_map/ppermute | solution.py:17
  155.7 4.1 %collective-permute-start.10 = (bf16[8,40,256]{2,1,0:T(8,128)(2,1)S(1)}, bf16[8,40,256]{2,1,0:T(8,128)(2,1)S(1)}, u32[]{:S(2)}, u32[]{:S(2)}) collective-permute-start(bf16[8,40,256]{2,1,0:T(8,128)(2,1)S(1)} %bitcast.100), channel_id=1, source_target_pairs={{0,48},{16,32},{32,16},{48,0},{64,112},{80,96},{96,80},{112,64},{1... | collective-permute-start | bytes 491528 | tf_op jit(solution)/shard_map/ppermute | solution.py:17
  162.0 3.3 %collective-permute-done.10 = bf16[8,40,256]{2,1,0:T(8,128)(2,1)S(1)} collective-permute-done((bf16[8,40,256]{2,1,0:T(8,128)(2,1)S(1)}, bf16[8,40,256]{2,1,0:T(8,128)(2,1)S(1)}, u32[]{:S(2)}, u32[]{:S(2)}) %collective-permute-start.10) | collective-permute-done | bytes 163872 | tf_op jit(solution)/shard_map/ppermute | solution.py:17
  166.9 4.4 %fusion = bf16[1,8,144,1280]{3,2,1,0:T(8,128)(2,1)} fusion(bf16[1280,256]{1,0:T(8,128)(2,1)} %collective-permute-done.16, bf16[1280,256]{1,0:T(8,128)(2,1)S(1)} %bitcast.90, bf16[8,144,512]{2,1,0:T(8,128)(2,1)S(1)} %gather_fusion.1, pred[8]{0:T(512)(128)(4,1)S(1)} %copy-done.7), kind=kOutput, calls=%fused_computation.3 | convolution fusion | flops 1514635264 | bytes 5439496 | tf_op jit(solution)/shard_map/dot_general | solution.py:79
  (85 shorter events, 21.2 us)
Async XLA Ops:
  1.9 39.7 %copy-start.2 = (bf16[1280,256]{1,0:T(8,128)(2,1)S(1)}, bf16[1280,256]{1,0:T(8,128)(2,1)}, u32[]{:S(2)}) copy-start(bf16[1280,256]{1,0:T(8,128)(2,1)} %param.6) | copy-start | bytes 1966084
  1.9 94.7 %collective-permute-start.2 = (bf16[8,40,256]{2,1,0:T(8,128)(2,1)S(1)}, bf16[8,40,256]{2,1,0:T(8,128)(2,1)}, u32[]{:S(2)}, u32[]{:S(2)}) collective-permute-start(bf16[8,40,256]{2,1,0:T(8,128)(2,1)S(1)} %get-tuple-element.9), channel_id=1, source_target_pairs={{0,48},{16,32},{32,16},{48,0},{64,112},{80,96},{96,80},{112,64},{1... | collective-permute-start | bytes 491528 | tf_op jit(solution)/shard_map/ppermute | solution.py:17
  9.5 42.0 %copy-start.4 = (bf16[1,288,256]{2,1,0:T(8,128)(2,1)S(1)}, bf16[1,288,256]{2,1,0:T(8,128)(2,1)}, u32[]{:S(2)}) copy-start(bf16[1,288,256]{2,1,0:T(8,128)(2,1)} %param.8) | copy-start | bytes 442372
  9.5 87.0 %collective-permute-start.1 = (bf16[8,40,256]{2,1,0:T(8,128)(2,1)S(1)}, bf16[8,40,256]{2,1,0:T(8,128)(2,1)}, u32[]{:S(2)}, u32[]{:S(2)}) collective-permute-start(bf16[8,40,256]{2,1,0:T(8,128)(2,1)S(1)} %get-tuple-element.10), channel_id=1, source_target_pairs={{0,32},{16,48},{32,0},{48,16},{64,96},{80,112},{96,64},{112,80},{1... | collective-permute-start | bytes 491528 | tf_op jit(solution)/shard_map/ppermute | solution.py:17
  14.1 3.2 %collective-permute-start.17 = (f32[8,128]{1,0:T(8,128)S(1)}, f32[8,128]{1,0:T(8,128)S(1)}, u32[]{:S(2)}, u32[]{:S(2)}) collective-permute-start(f32[8,128]{1,0:T(8,128)S(1)} %broadcast_in_dim.62), channel_id=1, source_target_pairs={{0,1},{1,0},{2,3},{3,2},{4,5},{5,4},{6,7},{7,6},{8,9},{9,8},{10,11... | collective-permute-start | bytes 12296 | tf_op jit(solution)/shard_map/ppermute | solution.py:17
  17.9 10.4 %collective-permute-start.20 = (f32[8,128]{1,0:T(8,128)S(1)}, f32[8,128]{1,0:T(8,128)S(1)}, u32[]{:S(2)}, u32[]{:S(2)}) collective-permute-start(f32[8,128]{1,0:T(8,128)S(1)} %broadcast_maximum_fusion), channel_id=1, source_target_pairs={{0,48},{16,32},{32,16},{48,0},{64,112},{80,96},{96,80},{112,64},{1... | collective-permute-start | bytes 12296 | tf_op jit(solution)/shard_map/ppermute | solution.py:17
  19.8 8.4 %collective-permute-start.19 = (f32[8,128]{1,0:T(8,128)S(1)}, f32[8,128]{1,0:T(8,128)S(1)}, u32[]{:S(2)}, u32[]{:S(2)}) collective-permute-start(f32[8,128]{1,0:T(8,128)S(1)} %broadcast_maximum_fusion), channel_id=1, source_target_pairs={{0,32},{16,48},{32,0},{48,16},{64,96},{80,112},{96,64},{112,80},{1... | collective-permute-start | bytes 12296 | tf_op jit(solution)/shard_map/ppermute | solution.py:17
  25.3 5.5 %collective-permute-start.18 = (f32[8,128]{1,0:T(8,128)S(1)}, f32[8,128]{1,0:T(8,128)S(1)}, u32[]{:S(2)}, u32[]{:S(2)}) collective-permute-start(f32[8,128]{1,0:T(8,128)S(1)} %broadcast_maximum_fusion), channel_id=1, source_target_pairs={{0,16},{16,0},{32,48},{48,32},{64,80},{80,64},{96,112},{112,96},{1... | collective-permute-start | bytes 12296 | tf_op jit(solution)/shard_map/ppermute | solution.py:17
  31.4 10.2 %collective-permute-start.23 = (f32[8,128]{1,0:T(8,128)S(1)}, f32[8,128]{1,0:T(8,128)S(1)}, u32[]{:S(2)}, u32[]{:S(2)}) collective-permute-start(f32[8,128]{1,0:T(8,128)S(1)} %maximum_maximum_fusion.2), channel_id=1, source_target_pairs={{0,192},{16,208},{32,224},{48,240},{64,128},{80,144},{96,160},{112... | collective-permute-start | bytes 12296 | tf_op jit(solution)/shard_map/ppermute | solution.py:17
  35.0 6.6 %collective-permute-start.22 = (f32[8,128]{1,0:T(8,128)S(1)}, f32[8,128]{1,0:T(8,128)S(1)}, u32[]{:S(2)}, u32[]{:S(2)}) collective-permute-start(f32[8,128]{1,0:T(8,128)S(1)} %maximum_maximum_fusion.2), channel_id=1, source_target_pairs={{0,128},{16,144},{32,160},{48,176},{64,192},{80,208},{96,224},{112... | collective-permute-start | bytes 12296 | tf_op jit(solution)/shard_map/ppermute | solution.py:17
  36.9 6.2 %collective-permute-start.21 = (f32[8,128]{1,0:T(8,128)S(1)}, f32[8,128]{1,0:T(8,128)S(1)}, u32[]{:S(2)}, u32[]{:S(2)}) collective-permute-start(f32[8,128]{1,0:T(8,128)S(1)} %maximum_maximum_fusion.2), channel_id=1, source_target_pairs={{0,64},{16,80},{32,96},{48,112},{64,0},{80,16},{96,32},{112,48},{1... | collective-permute-start | bytes 12296 | tf_op jit(solution)/shard_map/ppermute | solution.py:17
  43.2 10.0 %collective-permute-start.24 = (f32[8,128]{1,0:T(8,128)S(1)}, f32[8,128]{1,0:T(8,128)S(1)}, u32[]{:S(2)}, u32[]{:S(2)}) collective-permute-start(f32[8,128]{1,0:T(8,128)S(1)} %maximum_maximum_fusion.1), channel_id=1, source_target_pairs={{0,256},{16,272},{32,288},{48,304},{64,320},{80,336},{96,352},{112... | collective-permute-start | bytes 12296 | tf_op jit(solution)/shard_map/ppermute | solution.py:17
  53.1 14.2 %collective-permute-start.25 = (f32[8,128]{1,0:T(8,128)S(1)}, f32[8,128]{1,0:T(8,128)S(1)}, u32[]{:S(2)}, u32[]{:S(2)}) collective-permute-start(f32[8,128]{1,0:T(8,128)S(1)} %max.43), channel_id=1, source_target_pairs={{0,8},{2,10},{4,12},{6,14},{8,0},{10,2},{12,4},{14,6},{1,9},{3,11}... | collective-permute-start | bytes 12296 | tf_op jit(solution)/shard_map/ppermute | solution.py:17
  67.3 10.4 %collective-permute-start.28 = (f32[8,128]{1,0:T(8,128)S(1)}, f32[8,128]{1,0:T(8,128)S(1)}, u32[]{:S(2)}, u32[]{:S(2)}) collective-permute-start(f32[8,128]{1,0:T(8,128)S(1)} %max.44), channel_id=1, source_target_pairs={{0,6},{2,4},{4,2},{6,0},{8,14},{10,12},{12,10},{14,8},{1,7},{3,5},... | collective-permute-start | bytes 12296 | tf_op jit(solution)/shard_map/ppermute | solution.py:17
  72.0 8.4 %collective-permute-start.27 = (f32[8,128]{1,0:T(8,128)S(1)}, f32[8,128]{1,0:T(8,128)S(1)}, u32[]{:S(2)}, u32[]{:S(2)}) collective-permute-start(f32[8,128]{1,0:T(8,128)S(1)} %max.44), channel_id=1, source_target_pairs={{0,4},{2,6},{4,0},{6,2},{8,12},{10,14},{12,8},{14,10},{1,5},{3,7},... | collective-permute-start | bytes 12296 | tf_op jit(solution)/shard_map/ppermute | solution.py:17
  74.7 7.7 %collective-permute-start.26 = (f32[8,128]{1,0:T(8,128)S(1)}, f32[8,128]{1,0:T(8,128)}, u32[]{:S(2)}, u32[]{:S(2)}) collective-permute-start(f32[8,128]{1,0:T(8,128)S(1)} %max.44), channel_id=1, source_target_pairs={{0,2},{2,0},{4,6},{6,4},{8,10},{10,8},{12,14},{14,12},{1,3},{3,1},... | collective-permute-start | bytes 12296 | tf_op jit(solution)/shard_map/ppermute | solution.py:17
  77.7 39.4 %copy-start.6 = (pred[4]{0:T(512)(128)(4,1)S(1)}, pred[4]{0:T(512)(128)(4,1)}, u32[]{:S(2)}) copy-start(pred[4]{0:T(512)(128)(4,1)} %iota_compare_fusion) | copy-start | bytes 16
  77.7 18.9 %collective-permute-start = (bf16[8,40,256]{2,1,0:T(8,128)(2,1)S(1)}, bf16[8,40,256]{2,1,0:T(8,128)(2,1)S(1)}, u32[]{:S(2)}, u32[]{:S(2)}) collective-permute-start(bf16[8,40,256]{2,1,0:T(8,128)(2,1)S(1)} %get-tuple-element.8), channel_id=1, source_target_pairs={{0,16},{16,0},{32,48},{48,32},{64,80},{80,64},{96,112},{112,96},{1... | collective-permute-start | bytes 491528 | tf_op jit(solution)/shard_map/ppermute | solution.py:17
  80.5 86.4 %collective-permute-start.16 = (bf16[1280,256]{1,0:T(8,128)(2,1)S(1)}, bf16[1280,256]{1,0:T(8,128)(2,1)}, u32[]{:S(2)}, u32[]{:S(2)}) collective-permute-start(bf16[1280,256]{1,0:T(8,128)(2,1)S(1)} %bitcast.88), channel_id=1, source_target_pairs={{0,1},{1,0},{2,3},{3,2},{4,5},{5,4},{6,7},{7,6},{8,9},{9,8},{10,11... | collective-permute-start | bytes 1966088 | tf_op jit(solution)/shard_map/ppermute | solution.py:17
  82.4 19.6 %collective-permute-start.11 = (bf16[288,256]{1,0:T(8,128)(2,1)S(1)}, bf16[288,256]{1,0:T(8,128)(2,1)S(1)}, u32[]{:S(2)}, u32[]{:S(2)}) collective-permute-start(bf16[288,256]{1,0:T(8,128)(2,1)S(1)} %bitcast.102), channel_id=1, source_target_pairs={{0,8},{2,10},{4,12},{6,14},{8,0},{10,2},{12,4},{14,6},{1,9},{3,11}... | collective-permute-start | bytes 442376 | tf_op jit(solution)/shard_map/ppermute | solution.py:17
  97.7 19.3 %collective-permute-start.3 = (bf16[4,40,256]{2,1,0:T(8,128)(2,1)S(1)}, bf16[4,40,256]{2,1,0:T(8,128)(2,1)S(1)}, u32[]{:S(2)}, u32[]{:S(2)}) collective-permute-start(bf16[4,40,256]{2,1,0:T(8,128)(2,1)S(1)} %fusion.10), channel_id=1, source_target_pairs={{0,256},{16,272},{32,288},{48,304},{64,320},{80,336},{96,352},{112... | collective-permute-start | bytes 245768 | tf_op jit(solution)/shard_map/ppermute | solution.py:17
  102.1 50.4 %collective-permute-start.12 = (bf16[2,288,256]{2,1,0:T(8,128)(2,1)S(1)}, bf16[2,288,256]{2,1,0:T(8,128)(2,1)S(1)}, u32[]{:S(2)}, u32[]{:S(2)}) collective-permute-start(bf16[2,288,256]{2,1,0:T(8,128)(2,1)S(1)} %pad_maximum_fusion.1), channel_id=1, source_target_pairs={{0,2},{2,0},{4,6},{6,4},{8,10},{10,8},{12,14},{14,12},{1,3},{3,1},... | collective-permute-start | bytes 884744 | tf_op jit(solution)/shard_map/ppermute | solution.py:17
  117.2 10.2 %collective-permute-start.6 = (bf16[4,40,256]{2,1,0:T(8,128)(2,1)S(1)}, bf16[4,40,256]{2,1,0:T(8,128)(2,1)S(1)}, u32[]{:S(2)}, u32[]{:S(2)}) collective-permute-start(bf16[4,40,256]{2,1,0:T(8,128)(2,1)S(1)} %get-tuple-element.4), channel_id=1, source_target_pairs={{0,192},{16,208},{32,224},{48,240},{64,128},{80,144},{96,160},{112... | collective-permute-start | bytes 245768 | tf_op jit(solution)/shard_map/ppermute | solution.py:17
  120.2 12.0 %collective-permute-start.5 = (bf16[4,40,256]{2,1,0:T(8,128)(2,1)S(1)}, bf16[4,40,256]{2,1,0:T(8,128)(2,1)S(1)}, u32[]{:S(2)}, u32[]{:S(2)}) collective-permute-start(bf16[4,40,256]{2,1,0:T(8,128)(2,1)S(1)} %get-tuple-element.4), channel_id=1, source_target_pairs={{0,128},{16,144},{32,160},{48,176},{64,192},{80,208},{96,224},{112... | collective-permute-start | bytes 245768 | tf_op jit(solution)/shard_map/ppermute | solution.py:17
  122.2 13.2 %collective-permute-start.4 = (bf16[4,40,256]{2,1,0:T(8,128)(2,1)S(1)}, bf16[4,40,256]{2,1,0:T(8,128)(2,1)S(1)}, u32[]{:S(2)}, u32[]{:S(2)}) collective-permute-start(bf16[4,40,256]{2,1,0:T(8,128)(2,1)S(1)} %get-tuple-element.4), channel_id=1, source_target_pairs={{0,64},{16,80},{32,96},{48,112},{64,0},{80,16},{96,32},{112,48},{1... | collective-permute-start | bytes 245768 | tf_op jit(solution)/shard_map/ppermute | solution.py:17
  127.3 28.4 %collective-permute-start.13 = (bf16[2,288,256]{2,1,0:T(8,128)(2,1)S(1)}, bf16[2,288,256]{2,1,0:T(8,128)(2,1)S(1)}, u32[]{:S(2)}, u32[]{:S(2)}) collective-permute-start(bf16[2,288,256]{2,1,0:T(8,128)(2,1)S(1)} %pad_maximum_fusion.1), channel_id=1, source_target_pairs={{0,4},{2,6},{4,0},{6,2},{8,12},{10,14},{12,8},{14,10},{1,5},{3,7},... | collective-permute-start | bytes 884744 | tf_op jit(solution)/shard_map/ppermute | solution.py:17
  132.3 27.6 %collective-permute-start.14 = (bf16[2,288,256]{2,1,0:T(8,128)(2,1)S(1)}, bf16[2,288,256]{2,1,0:T(8,128)(2,1)S(1)}, u32[]{:S(2)}, u32[]{:S(2)}) collective-permute-start(bf16[2,288,256]{2,1,0:T(8,128)(2,1)S(1)} %pad_maximum_fusion.1), channel_id=1, source_target_pairs={{0,6},{2,4},{4,2},{6,0},{8,14},{10,12},{12,10},{14,8},{1,7},{3,5},... | collective-permute-start | bytes 884744 | tf_op jit(solution)/shard_map/ppermute | solution.py:17
  135.4 13.8 %collective-permute-start.7 = (bf16[4,40,256]{2,1,0:T(8,128)(2,1)S(1)}, bf16[4,40,256]{2,1,0:T(8,128)(2,1)S(1)}, u32[]{:S(2)}, u32[]{:S(2)}) collective-permute-start(bf16[4,40,256]{2,1,0:T(8,128)(2,1)S(1)} %fusion.9), channel_id=1, source_target_pairs={{0,256},{16,272},{32,288},{48,304},{64,320},{80,336},{96,352},{112... | collective-permute-start | bytes 245768 | tf_op jit(solution)/shard_map/ppermute | solution.py:17
  149.2 12.7 %collective-permute-start.8 = (bf16[8,40,256]{2,1,0:T(8,128)(2,1)S(1)}, bf16[8,40,256]{2,1,0:T(8,128)(2,1)S(1)}, u32[]{:S(2)}, u32[]{:S(2)}) collective-permute-start(bf16[8,40,256]{2,1,0:T(8,128)(2,1)S(1)} %bitcast.97), channel_id=1, source_target_pairs={{0,16},{16,0},{32,48},{48,32},{64,80},{80,64},{96,112},{112,96},{1... | collective-permute-start | bytes 491528 | tf_op jit(solution)/shard_map/ppermute | solution.py:17
  152.5 9.4 %collective-permute-start.9 = (bf16[8,40,256]{2,1,0:T(8,128)(2,1)S(1)}, bf16[8,40,256]{2,1,0:T(8,128)(2,1)S(1)}, u32[]{:S(2)}, u32[]{:S(2)}) collective-permute-start(bf16[8,40,256]{2,1,0:T(8,128)(2,1)S(1)} %bitcast.99), channel_id=1, source_target_pairs={{0,32},{16,48},{32,0},{48,16},{64,96},{80,112},{96,64},{112,80},{1... | collective-permute-start | bytes 491528 | tf_op jit(solution)/shard_map/ppermute | solution.py:17
  155.7 9.6 %collective-permute-start.10 = (bf16[8,40,256]{2,1,0:T(8,128)(2,1)S(1)}, bf16[8,40,256]{2,1,0:T(8,128)(2,1)S(1)}, u32[]{:S(2)}, u32[]{:S(2)}) collective-permute-start(bf16[8,40,256]{2,1,0:T(8,128)(2,1)S(1)} %bitcast.100), channel_id=1, source_target_pairs={{0,48},{16,32},{32,16},{48,0},{64,112},{80,96},{96,80},{112,64},{1... | collective-permute-start | bytes 491528 | tf_op jit(solution)/shard_map/ppermute | solution.py:17
  160.0 5.3 %collective-permute-start.15 = (bf16[8,144,256]{2,1,0:T(8,128)(2,1)S(1)}, bf16[8,144,256]{2,1,0:T(8,128)(2,1)S(1)}, u32[]{:S(2)}, u32[]{:S(2)}) collective-permute-start(bf16[8,144,256]{2,1,0:T(8,128)(2,1)S(1)} %get-tuple-element.7), channel_id=1, source_target_pairs={{0,1},{1,0},{2,3},{3,2},{4,5},{5,4},{6,7},{7,6},{8,9},{9,8},{10,11... | collective-permute-start | bytes 1769480 | tf_op jit(solution)/shard_map/ppermute | solution.py:17
  (5 other events, 43.3 us)

commit v2 on v0

v2 whole, which is shorter than its diff:
```python
import jax
import jax.numpy as jnp
from jax import lax
from jax.experimental import pallas as pl
from jax.experimental.pallas import tpu as pltpu
from jax.sharding import PartitionSpec as P

OUTER_MOMENTUM = 0.9
OUTER_RATE = 0.7
EPSILON = 1e-06
N_REPLICA = 32
STEP_GAIN = OUTER_RATE * (1.0 + OUTER_MOMENTUM) / N_REPLICA
MOMENTUM_GAIN = OUTER_MOMENTUM * OUTER_MOMENTUM * N_REPLICA / (1.0 + OUTER_MOMENTUM)
F32, BF16 = jnp.float32, jnp.bfloat16
ROWS, COLS, TAIL, TOK = 40, 256, 16, 144
TOP = (8, COLS)
VMEM = pl.BlockSpec(memory_space=pltpu.VMEM)
SMEM = pl.BlockSpec(memory_space=pltpu.SMEM)


def swap(x, axis, bit):
    n = lax.axis_size(axis)
    return lax.ppermute(x, axis, [(i, i ^ bit) for i in range(n)])


def tie(x, dep):
    return lax.optimization_barrier((x, dep))[0]


def call(kernel, outs, args, scratch=()):
    return pl.pallas_call(
        kernel,
        out_shape=[jax.ShapeDtypeStruct(s, d) for s, d in outs],
        in_specs=[SMEM] + [VMEM] * (len(args) - 1),
        out_specs=[VMEM] * len(outs),
        scratch_shapes=[pltpu.VMEM(s, d) for s, d in scratch],
        compiler_params=pltpu.CompilerParams(vmem_limit_bytes=24 * 1024 * 1024),
    )(*args)


def tail(m):
    a = m.astype(BF16).astype(F32)
    b = (m - a).astype(BF16).astype(F32)
    c = m - a - b
    row = lax.broadcasted_iota(jnp.int32, (TAIL, COLS), 0)
    return jnp.where(row == 0, a, jnp.where(row == 1, b, c)).astype(BF16)


def untail(ref, rows):
    p = ref[rows : rows + TAIL].astype(F32)
    return p[0:1] + p[1:2] + p[2:3]


def put(msg, rows, m):
    n = rows.shape[0]
    msg[0:n] = rows.astype(BF16)
    msg[n : n + TAIL] = tail(m)


def start_kernel(ix, w, a, kg, m1, m2, m3, own, a_y, kgm, mx):
    y = ix[0]
    top = jnp.zeros(TOP, F32)
    for i in range(8):
        d = jnp.abs(a[i].astype(F32) - w[i].astype(F32)).reshape(-1, 8, COLS)
        top = jnp.maximum(top, jnp.max(d, axis=0))
    m = jnp.broadcast_to(jnp.max(top), (1, COLS))
    kgm[0 : 2 * TOK] = kg[...]
    kgm[2 * TOK :] = tail(m)
    for d, msg in ((1, m1), (2, m2), (3, m3)):
        msg[...] = w[:, y ^ d].astype(F32).reshape(8 * ROWS, COLS).astype(BF16)
    mine = a[:, y].astype(F32).reshape(8 * ROWS, COLS)
    a_y[...] = mine
    own[...] = mine - w[:, y].astype(F32).reshape(8 * ROWS, COLS)
    mx[...] = jnp.broadcast_to(m, TOP)


def y_kernel(ix, own, a_y, g1, g2, g3, h, own4, s):
    lo = ix[2]
    mine = a_y[...]
    s[...] = own[...] + sum(mine - g[...].astype(F32) for g in (g1, g2, g3))

    def blocks(k):
        return [s[pl.ds((4 * b + k) * ROWS, ROWS)] for b in range(2)]

    h[...] = jnp.concatenate(blocks(lo ^ 1) + blocks(lo ^ 3)).astype(BF16)
    own4[...] = jnp.concatenate(blocks(lo) + blocks(lo ^ 2))


def near_kernel(ix, own4, g, h, own2):
    s = own4[...] + g[...].astype(F32)
    h[...] = s[2 * ROWS :].astype(BF16)
    own2[...] = s[: 2 * ROWS]


def lo_kernel(ix, own2, mom, h, mx, mr, q, p_own, mx2, s):
    hi = ix[1]
    m = jnp.maximum(mx[0:1], mr[0:1])
    s[...] = own2[...] + h[...].astype(F32)
    here = pl.ds(hi * ROWS, ROWS)
    p_own[...] = s[here]
    s[here] = s[here] + MOMENTUM_GAIN * mom[...]
    put(q, s[...], m)
    mx2[...] = jnp.broadcast_to(m, TOP)


def hi_kernel(ix, q, p_own, mom, a_y, mx, g, fresh, mom_new, mx2, s):
    hi, lo = ix[1], ix[2]
    m = jnp.maximum(mx[0:1], untail(g, 2 * ROWS))
    s[...] = g[0 : 2 * ROWS].astype(F32)
    total = q[0 : 2 * ROWS].astype(F32) + s[...]
    summed = p_own[...] + s[pl.ds(hi * ROWS, ROWS)]
    mom_new[...] = OUTER_MOMENTUM * mom[...] + summed * (1.0 / N_REPLICA)
    rows = jnp.concatenate([a_y[pl.ds((4 * b + lo) * ROWS, ROWS)] for b in range(2)])
    put(fresh, rows - STEP_GAIN * total, m)
    mx2[...] = jnp.broadcast_to(m, TOP)


def join_kernel(ix, a, b, mx, out, mx2):
    n = b.shape[0] - TAIL
    m = jnp.maximum(mx[0:1], untail(b, n))
    out[0:n] = a[0:n]
    out[n : 2 * n] = b[0:n]
    out[2 * n :] = tail(m)
    mx2[...] = jnp.broadcast_to(m, TOP)


def eight_kernel(ix, near, far, mx, eight, mx2, s):
    lo = ix[2]
    for j, ref in enumerate((near, far)):
        x = ref[0 : 4 * ROWS].astype(F32)
        for k in range(2):
            for b in range(2):
                at = (2 * k + b) * ROWS
                s[pl.ds((4 * b + (lo ^ (j + 2 * k))) * ROWS, ROWS)] = x[at : at + ROWS]
    m = jnp.maximum(mx[0:1], untail(far, 4 * ROWS))
    put(eight, s[...], m)
    mx2[...] = jnp.broadcast_to(m, TOP)


def out_kernel(ix, two, more, mx, out, scale):
    y = ix[0]
    n = 8 * ROWS
    for d, (ref, k) in enumerate(((two, 0), (two, 1), (more, 1), (more, 0))):
        out[:, y ^ d] = ref[k * n : (k + 1) * n].astype(F32).reshape(8, ROWS, COLS).astype(BF16)
    m = jnp.maximum(mx[0:1], untail(more, 2 * n))
    scale[...] = jnp.broadcast_to(m, TOP) + EPSILON


def pair_kernel(ix, a, b, mx, theirs, mine, mx2):
    t = ix[4]
    m = jnp.maximum(mx[0:1], untail(b, 2 * TOK))
    for i, ref in enumerate((a, b)):
        at = slice(i * TOK, (i + 1) * TOK)
        theirs[at] = ref[pl.ds(pl.multiple_of((1 - t) * TOK, 16), TOK)]
        mine[at] = ref[pl.ds(pl.multiple_of(t * TOK, 16), TOK)]
    theirs[2 * TOK :] = tail(m)
    mx2[...] = jnp.broadcast_to(m, TOP)


def core_kernel(ix, mine, g, mx, both, mx2):
    both[0 : 2 * TOK] = mine[...]
    both[2 * TOK :] = g[0 : 2 * TOK]
    mx2[...] = jnp.broadcast_to(jnp.maximum(mx[0:1], untail(g, 2 * TOK))[:, :128], (8, 128))


def quad_kernel(ix, a, b, quad):
    n = 2 * TOK
    for k in range(2):
        quad[2 * k * n : (2 * k + 1) * n] = a[k * n : (k + 1) * n]
        quad[(2 * k + 1) * n : (2 * k + 2) * n] = b[k * n : (k + 1) * n]


def product_kernel(place, a, b, wa, wb, out):
    dims = (((1,), (1,)), ((), ()))
    n = 4 * TOK
    for j, ref in enumerate((a, b)):
        x = lax.dot_general(ref[0:n], wa[...], dims, preferred_element_type=F32)
        x += lax.dot_general(ref[n:], wb[...], dims, preferred_element_type=F32)
        x = x.astype(BF16)
        for i in range(4):
            out[place[4 * j + i]] = x[i * TOK : (i + 1) * TOK]


def product(place, quad, more, w, w_other):
    width = w.shape[0]
    whole = pl.BlockSpec((8 * TOK, COLS), lambda i, s: (0, 0))
    part = pl.BlockSpec((COLS, COLS), lambda i, s: (i, 0))
    return pl.pallas_call(
        product_kernel,
        grid_spec=pltpu.PrefetchScalarGridSpec(
            num_scalar_prefetch=1,
            grid=(width // COLS,),
            in_specs=[whole, whole, part, part],
            out_specs=pl.BlockSpec((8, TOK, COLS), lambda i, s: (0, 0, i)),
        ),
        out_shape=jax.ShapeDtypeStruct((8, TOK, width), BF16),
        compiler_params=pltpu.CompilerParams(vmem_limit_bytes=24 * 1024 * 1024),
        cost_estimate=pl.CostEstimate(flops=16 * TOK * width * 2 * COLS, bytes_accessed=5_600_000, transcendentals=0),
    )(place, quad, more, w, w_other)


def body(w_local, anchor, momentum, key_grad):
    r = lax.axis_index("replica")
    f = lax.axis_index("fsdp")
    t = lax.axis_index("tensor")
    ix = jnp.stack([r & 3, r >> 4, (r >> 2) & 3, f, t])
    w = w_local[0]
    mom = momentum[0, 0]
    top = (TOP, F32)

    def bf(n):
        return ((n, COLS), BF16)

    def fl(n):
        return ((n, COLS), F32)

    w_other = swap(w, "tensor", 1)
    four = (8, 4, ROWS, COLS)
    m1, m2, m3, own, a_y, kgm, mx = call(
        start_kernel,
        [bf(320)] * 3 + [fl(320)] * 2 + [bf(304), top],
        (ix, w.reshape(four), anchor.reshape(four), key_grad[0]),
    )
    kg_far = swap(kgm, "fsdp", 4)
    g2, g1, g3 = (swap(m, "replica", d) for d, m in ((2, m2), (1, m1), (3, m3)))
    h, own4 = call(y_kernel, [bf(160), fl(160)], (ix, own, a_y, g1, g2, g3), [fl(320)])
    h = swap(h, "replica", 4)
    theirs, kg_mine, mx = call(pair_kernel, [bf(304), bf(288), top], (ix, kgm, kg_far, mx))
    kg_core = swap(theirs, "tensor", 1)
    h, own2 = call(near_kernel, [bf(80), fl(80)], (ix, own4, h))
    h = swap(h, "replica", 8)
    both, ms = call(core_kernel, [bf(576), ((8, 128), F32)], (ix, kg_mine, kg_core, mx))
    ms = jnp.maximum(ms, swap(ms, "fsdp", 1))
    mr = swap(ms, "fsdp", 3)
    wide = [jnp.concatenate([m, m], axis=1) for m in (ms, mr)]
    q, p_own, mx = call(lo_kernel, [bf(96), fl(40), top], (ix, own2, mom, h, *wide), [fl(80)])
    g = swap(q, "replica", 16)
    kg_x = swap(tie(both, q), "fsdp", 1)
    fresh, mom_new, mx = call(hi_kernel, [bf(96), fl(40), top], (ix, q, p_own, mom, a_y, mx, g), [fl(80)])
    near, mx = call(join_kernel, [bf(176), top], (ix, fresh, swap(fresh, "replica", 8), mx))
    far = swap(near, "replica", 4)
    quad = call(quad_kernel, [bf(1152)], (ix, both, tie(kg_x, near)))[0]
    more = swap(quad, "fsdp", 3)
    eight, mx = call(eight_kernel, [bf(336), top], (ix, near, far, mx), [fl(320)])
    two, mx = call(join_kernel, [bf(656), top], (ix, eight, swap(eight, "replica", 1), mx))
    last = swap(two, "replica", 3)
    place = jnp.array([0, 4, 1, 5, 3, 7, 2, 6], jnp.int32) ^ f
    prod = product(place, quad, tie(more, two), w, w_other)
    new_weights, scale = call(out_kernel, [(four, BF16), top], (ix, two, tie(last, prod), mx))
    return new_weights.reshape(anchor.shape), mom_new[None, None], prod[None], scale[0, :1]


def solution(mesh):
    return jax.shard_map(
        body,
        mesh=mesh,
        in_specs=(
            P("replica", "fsdp", "tensor"),
            P("fsdp", "tensor"),
            P("fsdp", "replica", None, "tensor"),
            P("replica", "fsdp", "tensor"),
        ),
        out_specs=(
            P("fsdp", "tensor"),
            P("fsdp", "replica", None, "tensor"),
            P("replica", None, "tensor", "fsdp"),
            P(),
        ),
        check_vma=False,
    )
```

time: 514 us -> 110 us (0.21)
  the two profiles are of different devices: /device:TPU:2 before, /device:TPU:24 now
where the time goes in v2:
time: 110 us; the launch traced here: 109 us
  starting transfers between devices  68.7 us (62%)
  waiting for transfers between devices  22.5 us (20%)
  Pallas kernels  13.3 us (12%)
  local copies, waits for them, and re-layouts  3.69 us (3%)
    ppermute x17, starting transfers between devices, swap(): return lax.ppermute(x, axis, [(i, i ^ bit) for i in range(n)])  68.7 us
    ppermute x17, waiting for transfers between devices, swap(): return lax.ppermute(x, axis, [(i, i ^ bit) for i in range(n)])  22.5 us
    pallas_call x12, Pallas kernels, call(): pl.pallas_call(kernel, out_shape=[jax.ShapeDtypeStruct(s, d) for s, d in...  8.77 us
    pallas_call x1, Pallas kernels, product(): pl.pallas_call(product_kernel, grid_spec=pltpu.PrefetchScalarGridSpec(num...  4.58 us
    unnamed x12, local copies, waits for them, and re-layouts  3.1 us
  transfers between devices with their start and end apart: 17, of which 7 were waited for; matrix products, arithmetic and copies ran while one was open for 0% of the time, Pallas kernels for 10%

profile of v2, /device:TPU:24, one launch (start us, length us, event | category | flops | bytes accessed | tf_op | source)
XLA Modules:
  0.0 109.2 jit_solution(3317473678947428463)
XLA Ops:
  0.7 1.1 copy-done
  1.8 1.1 copy-done.1
  2.9 0.9 copy-done.4
  3.8 0.8 shard_map.84
  4.7 15.7 %collective-permute-start.5 = (bf16[304,256]{1,0:T(8,128)(2,1)S(1)}, bf16[304,256]{1,0:T(8,128)(2,1)S(1)}, u32[]{:S(2)}, u32[]{:S(2)}) collective-permute-start(bf16[304,256]{1,0:T(8,128)(2,1)S(1)} %get-tuple-element.47.a), channel_id=1, source_target_pairs={{0,8},{2,10},{4,12},{6,14},{8,0},{10,2},{12,4},{14,6},{1,9},{3,11}... | collective-permute-start | bytes 466952 | tf_op jit(solution)/shard_map/ppermute | solution.py:23
  20.4 2.7 %collective-permute-start = (bf16[320,256]{1,0:T(8,128)(2,1)S(1)}, bf16[320,256]{1,0:T(8,128)(2,1)S(1)}, u32[]{:S(2)}, u32[]{:S(2)}) collective-permute-start(bf16[320,256]{1,0:T(8,128)(2,1)S(1)} %get-tuple-element.40), channel_id=1, source_target_pairs={{0,16},{16,0},{32,48},{48,32},{64,80},{80,64},{96,112},{112,96},{1... | collective-permute-start | bytes 491528 | tf_op jit(solution)/shard_map/ppermute | solution.py:23
  23.0 2.8 %collective-permute-start.1 = (bf16[320,256]{1,0:T(8,128)(2,1)S(1)}, bf16[320,256]{1,0:T(8,128)(2,1)S(1)}, u32[]{:S(2)}, u32[]{:S(2)}) collective-permute-start(bf16[320,256]{1,0:T(8,128)(2,1)S(1)} %get-tuple-element.41), channel_id=1, source_target_pairs={{0,32},{16,48},{32,0},{48,16},{64,96},{80,112},{96,64},{112,80},{1... | collective-permute-start | bytes 491528 | tf_op jit(solution)/shard_map/ppermute | solution.py:23
  25.9 4.9 %collective-permute-start.2 = (bf16[320,256]{1,0:T(8,128)(2,1)S(1)}, bf16[320,256]{1,0:T(8,128)(2,1)S(1)}, u32[]{:S(2)}, u32[]{:S(2)}) collective-permute-start(bf16[320,256]{1,0:T(8,128)(2,1)S(1)} %get-tuple-element.42), channel_id=1, source_target_pairs={{0,48},{16,32},{32,16},{48,0},{64,112},{80,96},{96,80},{112,64},{1... | collective-permute-start | bytes 491528 | tf_op jit(solution)/shard_map/ppermute | solution.py:23
  31.4 1.9 %collective-permute-start.6 = (bf16[304,256]{1,0:T(8,128)(2,1)S(1)}, bf16[304,256]{1,0:T(8,128)(2,1)S(1)}, u32[]{:S(2)}, u32[]{:S(2)}) collective-permute-start(bf16[304,256]{1,0:T(8,128)(2,1)S(1)} %get-tuple-element.50), channel_id=1, source_target_pairs={{0,1},{1,0},{2,3},{3,2},{4,5},{5,4},{6,7},{7,6},{8,9},{9,8},{10,11... | collective-permute-start | bytes 466952 | tf_op jit(solution)/shard_map/ppermute | solution.py:23
  33.4 2.0 %collective-permute-done.2.g3 = bf16[320,256]{1,0:T(8,128)(2,1)S(1)} collective-permute-done((bf16[320,256]{1,0:T(8,128)(2,1)S(1)}, bf16[320,256]{1,0:T(8,128)(2,1)S(1)}, u32[]{:S(2)}, u32[]{:S(2)}) %collective-permute-start.2) | collective-permute-done | bytes 163872 | tf_op jit(solution)/shard_map/ppermute | solution.py:23
  35.3 0.7 shard_map.85
  36.1 4.2 %collective-permute-start.3 = (bf16[160,256]{1,0:T(8,128)(2,1)S(1)}, bf16[160,256]{1,0:T(8,128)(2,1)S(1)}, u32[]{:S(2)}, u32[]{:S(2)}) collective-permute-start(bf16[160,256]{1,0:T(8,128)(2,1)S(1)} %get-tuple-element.44), channel_id=1, source_target_pairs={{0,64},{16,80},{32,96},{48,112},{64,0},{80,16},{96,32},{112,48},{1... | collective-permute-start | bytes 245768 | tf_op jit(solution)/shard_map/ppermute | solution.py:23
  40.9 3.4 %collective-permute-start.7 = (f32[8,128]{1,0:T(8,128)S(1)}, f32[8,128]{1,0:T(8,128)S(1)}, u32[]{:S(2)}, u32[]{:S(2)}) collective-permute-start(f32[8,128]{1,0:T(8,128)S(1)} %get-tuple-element.52), channel_id=1, source_target_pairs={{0,2},{2,0},{4,6},{6,4},{8,10},{10,8},{12,14},{14,12},{1,3},{3,1},... | collective-permute-start | bytes 12296 | tf_op jit(solution)/shard_map/ppermute | solution.py:23
  44.8 2.1 %collective-permute-start.4 = (bf16[80,256]{1,0:T(8,128)(2,1)S(1)}, bf16[80,256]{1,0:T(8,128)(2,1)S(1)}, u32[]{:S(2)}, u32[]{:S(2)}) collective-permute-start(bf16[80,256]{1,0:T(8,128)(2,1)S(1)} %get-tuple-element.46), channel_id=1, source_target_pairs={{0,128},{16,144},{32,160},{48,176},{64,192},{80,208},{96,224},{112... | collective-permute-start | bytes 122888 | tf_op jit(solution)/shard_map/ppermute | solution.py:23
  47.0 4.1 %collective-permute-start.8 = (f32[8,128]{1,0:T(8,128)S(1)}, f32[8,128]{1,0:T(8,128)S(1)}, u32[]{:S(2)}, u32[]{:S(2)}) collective-permute-start(f32[8,128]{1,0:T(8,128)S(1)} %max.3), channel_id=1, source_target_pairs={{0,6},{2,4},{4,2},{6,0},{8,14},{10,12},{12,10},{14,8},{1,7},{3,5},... | collective-permute-start | bytes 12296 | tf_op jit(solution)/shard_map/ppermute | solution.py:23
  51.1 2.6 %collective-permute-done.8 = f32[8,128]{1,0:T(8,128)S(1)} collective-permute-done((f32[8,128]{1,0:T(8,128)S(1)}, f32[8,128]{1,0:T(8,128)S(1)}, u32[]{:S(2)}, u32[]{:S(2)}) %collective-permute-start.8) | collective-permute-done | bytes 4128 | tf_op jit(solution)/shard_map/ppermute | solution.py:23
  54.3 1.9 %collective-permute-start.14 = (bf16[576,256]{1,0:T(8,128)(2,1)S(1)}, bf16[576,256]{1,0:T(8,128)(2,1)S(1)}, u32[]{:S(2)}, u32[]{:S(2)}) collective-permute-start(bf16[576,256]{1,0:T(8,128)(2,1)S(1)} %get-tuple-element.64.a), channel_id=1, source_target_pairs={{0,2},{2,0},{4,6},{6,4},{8,10},{10,8},{12,14},{14,12},{1,3},{3,1},... | collective-permute-start | bytes 884744 | tf_op jit(solution)/shard_map/ppermute | solution.py:23
  56.2 8.5 %collective-permute-start.9 = (bf16[96,256]{1,0:T(8,128)(2,1)S(1)}, bf16[96,256]{1,0:T(8,128)(2,1)S(1)}, u32[]{:S(2)}, u32[]{:S(2)}) collective-permute-start(bf16[96,256]{1,0:T(8,128)(2,1)S(1)} %get-tuple-element.53.q), channel_id=1, source_target_pairs={{0,256},{16,272},{32,288},{48,304},{64,320},{80,336},{96,352},{112... | collective-permute-start | bytes 147464 | tf_op jit(solution)/shard_map/ppermute | solution.py:23
  64.7 1.9 %collective-permute-start.16 = (bf16[1280,256]{1,0:T(8,128)(2,1)S(1)}, bf16[1280,256]{1,0:T(8,128)(2,1)S(1)}, u32[]{:S(2)}, u32[]{:S(2)}) collective-permute-start(bf16[1280,256]{1,0:T(8,128)(2,1)S(1)} %bitcast.16), channel_id=1, source_target_pairs={{0,1},{1,0},{2,3},{3,2},{4,5},{5,4},{6,7},{7,6},{8,9},{9,8},{10,11... | collective-permute-start | bytes 1966088 | tf_op jit(solution)/shard_map/ppermute | solution.py:23
  66.7 0.7 collective-permute-done.9.g
  67.4 1.2 %shard_map.90 = (bf16[96,256]{1,0:T(8,128)(2,1)S(1)}, f32[40,256]{1,0:T(8,128)}, f32[8,256]{1,0:T(8,128)S(1)}) custom-call(s32[5]{0:T(128)S(1)} %stack.23.ix, bf16[96,256]{1,0:T(8,128)(2,1)S(1)} %get-tuple-element.53.q, f32[40,256]{1,0:T(8,128)S(1)} %get-tuple-element.54.p_own, f32[40,256]{1,0:T(8,128)S(1)} %bitcast.19, ...), custom_call_target="tpu_custom_call" | custom-call | tf_op jit(solution)/shard_map/pallas_call | solution.py:31
  68.6 3.3 %collective-permute-start.10 = (bf16[96,256]{1,0:T(8,128)(2,1)S(1)}, bf16[96,256]{1,0:T(8,128)(2,1)S(1)}, u32[]{:S(2)}, u32[]{:S(2)}) collective-permute-start(bf16[96,256]{1,0:T(8,128)(2,1)S(1)} %get-tuple-element.56.a), channel_id=1, source_target_pairs={{0,128},{16,144},{32,160},{48,176},{64,192},{80,208},{96,224},{112... | collective-permute-start | bytes 147464 | tf_op jit(solution)/shard_map/ppermute | solution.py:23
  71.9 3.9 %collective-permute-done.10.b = bf16[96,256]{1,0:T(8,128)(2,1)S(1)} collective-permute-done((bf16[96,256]{1,0:T(8,128)(2,1)S(1)}, bf16[96,256]{1,0:T(8,128)(2,1)S(1)}, u32[]{:S(2)}, u32[]{:S(2)}) %collective-permute-start.10) | collective-permute-done | bytes 49184 | tf_op jit(solution)/shard_map/ppermute | solution.py:23
  77.0 4.4 %collective-permute-start.15 = (bf16[1152,256]{1,0:T(8,128)(2,1)S(1)}, bf16[1152,256]{1,0:T(8,128)(2,1)S(1)}, u32[]{:S(2)}, u32[]{:S(2)}) collective-permute-start(bf16[1152,256]{1,0:T(8,128)(2,1)S(1)} %shard_map.94.a), channel_id=1, source_target_pairs={{0,6},{2,4},{4,2},{6,0},{8,14},{10,12},{12,10},{14,8},{1,7},{3,5},... | collective-permute-start | bytes 1769480 | tf_op jit(solution)/shard_map/ppermute | solution.py:23
  81.4 1.9 %collective-permute-start.11 = (bf16[176,256]{1,0:T(8,128)(2,1)S(1)}, bf16[176,256]{1,0:T(8,128)(2,1)S(1)}, u32[]{:S(2)}, u32[]{:S(2)}) collective-permute-start(bf16[176,256]{1,0:T(8,128)(2,1)S(1)} %get-tuple-element.58.near), channel_id=1, source_target_pairs={{0,64},{16,80},{32,96},{48,112},{64,0},{80,16},{96,32},{112,48},{1... | collective-permute-start | bytes 270344 | tf_op jit(solution)/shard_map/ppermute | solution.py:23
  83.3 4.5 %collective-permute-done.11.far = bf16[176,256]{1,0:T(8,128)(2,1)S(1)} collective-permute-done((bf16[176,256]{1,0:T(8,128)(2,1)S(1)}, bf16[176,256]{1,0:T(8,128)(2,1)S(1)}, u32[]{:S(2)}, u32[]{:S(2)}) %collective-permute-start.11) | collective-permute-done | bytes 90144 | tf_op jit(solution)/shard_map/ppermute | solution.py:23
  88.4 2.6 %collective-permute-start.12 = (bf16[336,256]{1,0:T(8,128)(2,1)S(1)}, bf16[336,256]{1,0:T(8,128)(2,1)S(1)}, u32[]{:S(2)}, u32[]{:S(2)}) collective-permute-start(bf16[336,256]{1,0:T(8,128)(2,1)S(1)} %get-tuple-element.60.a), channel_id=1, source_target_pairs={{0,16},{16,0},{32,48},{48,32},{64,80},{80,64},{96,112},{112,96},{1... | collective-permute-start | bytes 516104 | tf_op jit(solution)/shard_map/ppermute | solution.py:23
  91.1 4.7 %collective-permute-done.12.b = bf16[336,256]{1,0:T(8,128)(2,1)S(1)} collective-permute-done((bf16[336,256]{1,0:T(8,128)(2,1)S(1)}, bf16[336,256]{1,0:T(8,128)(2,1)S(1)}, u32[]{:S(2)}, u32[]{:S(2)}) %collective-permute-start.12) | collective-permute-done | bytes 172064 | tf_op jit(solution)/shard_map/ppermute | solution.py:23
  96.3 2.2 %collective-permute-start.13 = (bf16[656,256]{1,0:T(8,128)(2,1)S(1)}, bf16[656,256]{1,0:T(8,128)(2,1)S(1)}, u32[]{:S(2)}, u32[]{:S(2)}) collective-permute-start(bf16[656,256]{1,0:T(8,128)(2,1)S(1)} %get-tuple-element.62.two), channel_id=1, source_target_pairs={{0,48},{16,32},{32,16},{48,0},{64,112},{80,96},{96,80},{112,64},{1... | collective-permute-start | bytes 1007624 | tf_op jit(solution)/shard_map/ppermute | solution.py:23
  98.6 4.6 %shard_map.95 = bf16[8,144,1280]{2,1,0:T(8,128)(2,1)} custom-call(s32[8]{0:T(128)S(1)} %broadcast_xor_fusion.place, bf16[1152,256]{1,0:T(8,128)(2,1)S(1)} %shard_map.94.a, bf16[1152,256]{1,0:T(8,128)(2,1)S(1)} %collective-permute-done.15.b, bf16[1280,256]{1,0:T(8,128)(2,1)S(1)} %bitcast.17, bf16[1280,256]{1,0:T(8,128)(2,1)S(1)} %collective-permute-done.16.wb), custom_call_target="tpu_custom_call" | custom-call | flops 1509949440 | bytes 5600000 | tf_op jit(solution)/shard_map/pallas_call | solution.py:188
  103.2 4.1 %collective-permute-done.13.more = bf16[656,256]{1,0:T(8,128)(2,1)S(1)} collective-permute-done((bf16[656,256]{1,0:T(8,128)(2,1)S(1)}, bf16[656,256]{1,0:T(8,128)(2,1)S(1)}, u32[]{:S(2)}, u32[]{:S(2)}) %collective-permute-start.13) | collective-permute-done | bytes 335904 | tf_op jit(solution)/shard_map/ppermute | solution.py:23
  107.2 1.4 %shard_map.96 = (bf16[8,4,40,256]{3,2,1,0:T(8,128)(2,1)}, f32[8,256]{1,0:T(8,128)S(1)}) custom-call(s32[5]{0:T(128)S(1)} %stack.23.ix, bf16[656,256]{1,0:T(8,128)(2,1)S(1)} %get-tuple-element.62.two, bf16[656,256]{1,0:T(8,128)(2,1)S(1)} %collective-permute-done.13.more, f32[8,256]{1,0:T(8,128)S(1)} %get-tuple-element.68.mx), custom_call_target="tpu_custom_call" | custom-call | tf_op jit(solution)/shard_map/pallas_call | solution.py:31
  (33 shorter events, 5.3 us)
Async XLA Ops:
  0.6 53.1 %copy-start.3 = (f32[1,1,40,256]{3,2,1,0:T(8,128)S(1)}, f32[1,1,40,256]{3,2,1,0:T(8,128)}, u32[]{:S(2)}) copy-start(f32[1,1,40,256]{3,2,1,0:T(8,128)} %param.7) | copy-start | bytes 122884
  0.7 1.1 copy-start
  1.8 1.1 copy-start.1
  2.9 0.9 copy-start.4
  3.8 60.9 %copy-start.2 = (bf16[1,1280,256]{2,1,0:T(8,128)(2,1)S(1)}, bf16[1,1280,256]{2,1,0:T(8,128)(2,1)}, u32[]{:S(2)}) copy-start(bf16[1,1280,256]{2,1,0:T(8,128)(2,1)} %param.5) | copy-start | bytes 1966084
  3.8 94.7 %copy-start.5 = (s32[8]{0:T(128)S(1)}, s32[8]{0:T(128)}, u32[]{:S(2)}) copy-start(s32[8]{0:T(128)} %constant.22.clone) | copy-start | bytes 100
  4.7 26.2 %collective-permute-start.5 = (bf16[304,256]{1,0:T(8,128)(2,1)S(1)}, bf16[304,256]{1,0:T(8,128)(2,1)S(1)}, u32[]{:S(2)}, u32[]{:S(2)}) collective-permute-start(bf16[304,256]{1,0:T(8,128)(2,1)S(1)} %get-tuple-element.47.a), channel_id=1, source_target_pairs={{0,8},{2,10},{4,12},{6,14},{8,0},{10,2},{12,4},{14,6},{1,9},{3,11}... | collective-permute-start | bytes 466952 | tf_op jit(solution)/shard_map/ppermute | solution.py:23
  20.4 13.0 %collective-permute-start = (bf16[320,256]{1,0:T(8,128)(2,1)S(1)}, bf16[320,256]{1,0:T(8,128)(2,1)S(1)}, u32[]{:S(2)}, u32[]{:S(2)}) collective-permute-start(bf16[320,256]{1,0:T(8,128)(2,1)S(1)} %get-tuple-element.40), channel_id=1, source_target_pairs={{0,16},{16,0},{32,48},{48,32},{64,80},{80,64},{96,112},{112,96},{1... | collective-permute-start | bytes 491528 | tf_op jit(solution)/shard_map/ppermute | solution.py:23
  23.0 10.3 %collective-permute-start.1 = (bf16[320,256]{1,0:T(8,128)(2,1)S(1)}, bf16[320,256]{1,0:T(8,128)(2,1)S(1)}, u32[]{:S(2)}, u32[]{:S(2)}) collective-permute-start(bf16[320,256]{1,0:T(8,128)(2,1)S(1)} %get-tuple-element.41), channel_id=1, source_target_pairs={{0,32},{16,48},{32,0},{48,16},{64,96},{80,112},{96,64},{112,80},{1... | collective-permute-start | bytes 491528 | tf_op jit(solution)/shard_map/ppermute | solution.py:23
  25.9 9.4 %collective-permute-start.2 = (bf16[320,256]{1,0:T(8,128)(2,1)S(1)}, bf16[320,256]{1,0:T(8,128)(2,1)S(1)}, u32[]{:S(2)}, u32[]{:S(2)}) collective-permute-start(bf16[320,256]{1,0:T(8,128)(2,1)S(1)} %get-tuple-element.42), channel_id=1, source_target_pairs={{0,48},{16,32},{32,16},{48,0},{64,112},{80,96},{96,80},{112,64},{1... | collective-permute-start | bytes 491528 | tf_op jit(solution)/shard_map/ppermute | solution.py:23
  31.4 8.9 %collective-permute-start.6 = (bf16[304,256]{1,0:T(8,128)(2,1)S(1)}, bf16[304,256]{1,0:T(8,128)(2,1)S(1)}, u32[]{:S(2)}, u32[]{:S(2)}) collective-permute-start(bf16[304,256]{1,0:T(8,128)(2,1)S(1)} %get-tuple-element.50), channel_id=1, source_target_pairs={{0,1},{1,0},{2,3},{3,2},{4,5},{5,4},{6,7},{7,6},{8,9},{9,8},{10,11... | collective-permute-start | bytes 466952 | tf_op jit(solution)/shard_map/ppermute | solution.py:23
  36.1 8.2 %collective-permute-start.3 = (bf16[160,256]{1,0:T(8,128)(2,1)S(1)}, bf16[160,256]{1,0:T(8,128)(2,1)S(1)}, u32[]{:S(2)}, u32[]{:S(2)}) collective-permute-start(bf16[160,256]{1,0:T(8,128)(2,1)S(1)} %get-tuple-element.44), channel_id=1, source_target_pairs={{0,64},{16,80},{32,96},{48,112},{64,0},{80,16},{96,32},{112,48},{1... | collective-permute-start | bytes 245768 | tf_op jit(solution)/shard_map/ppermute | solution.py:23
  40.9 6.1 %collective-permute-start.7 = (f32[8,128]{1,0:T(8,128)S(1)}, f32[8,128]{1,0:T(8,128)S(1)}, u32[]{:S(2)}, u32[]{:S(2)}) collective-permute-start(f32[8,128]{1,0:T(8,128)S(1)} %get-tuple-element.52), channel_id=1, source_target_pairs={{0,2},{2,0},{4,6},{6,4},{8,10},{10,8},{12,14},{14,12},{1,3},{3,1},... | collective-permute-start | bytes 12296 | tf_op jit(solution)/shard_map/ppermute | solution.py:23
  44.8 8.9 %collective-permute-start.4 = (bf16[80,256]{1,0:T(8,128)(2,1)S(1)}, bf16[80,256]{1,0:T(8,128)(2,1)S(1)}, u32[]{:S(2)}, u32[]{:S(2)}) collective-permute-start(bf16[80,256]{1,0:T(8,128)(2,1)S(1)} %get-tuple-element.46), channel_id=1, source_target_pairs={{0,128},{16,144},{32,160},{48,176},{64,192},{80,208},{96,224},{112... | collective-permute-start | bytes 122888 | tf_op jit(solution)/shard_map/ppermute | solution.py:23
  47.0 6.7 %collective-permute-start.8 = (f32[8,128]{1,0:T(8,128)S(1)}, f32[8,128]{1,0:T(8,128)S(1)}, u32[]{:S(2)}, u32[]{:S(2)}) collective-permute-start(f32[8,128]{1,0:T(8,128)S(1)} %max.3), channel_id=1, source_target_pairs={{0,6},{2,4},{4,2},{6,0},{8,14},{10,12},{12,10},{14,8},{1,7},{3,5},... | collective-permute-start | bytes 12296 | tf_op jit(solution)/shard_map/ppermute | solution.py:23
  54.3 22.1 %collective-permute-start.14 = (bf16[576,256]{1,0:T(8,128)(2,1)S(1)}, bf16[576,256]{1,0:T(8,128)(2,1)S(1)}, u32[]{:S(2)}, u32[]{:S(2)}) collective-permute-start(bf16[576,256]{1,0:T(8,128)(2,1)S(1)} %get-tuple-element.64.a), channel_id=1, source_target_pairs={{0,2},{2,0},{4,6},{6,4},{8,10},{10,8},{12,14},{14,12},{1,3},{3,1},... | collective-permute-start | bytes 884744 | tf_op jit(solution)/shard_map/ppermute | solution.py:23
  56.2 11.1 %collective-permute-start.9 = (bf16[96,256]{1,0:T(8,128)(2,1)S(1)}, bf16[96,256]{1,0:T(8,128)(2,1)S(1)}, u32[]{:S(2)}, u32[]{:S(2)}) collective-permute-start(bf16[96,256]{1,0:T(8,128)(2,1)S(1)} %get-tuple-element.53.q), channel_id=1, source_target_pairs={{0,256},{16,272},{32,288},{48,304},{64,320},{80,336},{96,352},{112... | collective-permute-start | bytes 147464 | tf_op jit(solution)/shard_map/ppermute | solution.py:23
  64.7 33.8 %collective-permute-start.16 = (bf16[1280,256]{1,0:T(8,128)(2,1)S(1)}, bf16[1280,256]{1,0:T(8,128)(2,1)S(1)}, u32[]{:S(2)}, u32[]{:S(2)}) collective-permute-start(bf16[1280,256]{1,0:T(8,128)(2,1)S(1)} %bitcast.16), channel_id=1, source_target_pairs={{0,1},{1,0},{2,3},{3,2},{4,5},{5,4},{6,7},{7,6},{8,9},{9,8},{10,11... | collective-permute-start | bytes 1966088 | tf_op jit(solution)/shard_map/ppermute | solution.py:23
  68.6 7.3 %collective-permute-start.10 = (bf16[96,256]{1,0:T(8,128)(2,1)S(1)}, bf16[96,256]{1,0:T(8,128)(2,1)S(1)}, u32[]{:S(2)}, u32[]{:S(2)}) collective-permute-start(bf16[96,256]{1,0:T(8,128)(2,1)S(1)} %get-tuple-element.56.a), channel_id=1, source_target_pairs={{0,128},{16,144},{32,160},{48,176},{64,192},{80,208},{96,224},{112... | collective-permute-start | bytes 147464 | tf_op jit(solution)/shard_map/ppermute | solution.py:23
  77.0 21.6 %collective-permute-start.15 = (bf16[1152,256]{1,0:T(8,128)(2,1)S(1)}, bf16[1152,256]{1,0:T(8,128)(2,1)S(1)}, u32[]{:S(2)}, u32[]{:S(2)}) collective-permute-start(bf16[1152,256]{1,0:T(8,128)(2,1)S(1)} %shard_map.94.a), channel_id=1, source_target_pairs={{0,6},{2,4},{4,2},{6,0},{8,14},{10,12},{12,10},{14,8},{1,7},{3,5},... | collective-permute-start | bytes 1769480 | tf_op jit(solution)/shard_map/ppermute | solution.py:23
  81.4 6.4 %collective-permute-start.11 = (bf16[176,256]{1,0:T(8,128)(2,1)S(1)}, bf16[176,256]{1,0:T(8,128)(2,1)S(1)}, u32[]{:S(2)}, u32[]{:S(2)}) collective-permute-start(bf16[176,256]{1,0:T(8,128)(2,1)S(1)} %get-tuple-element.58.near), channel_id=1, source_target_pairs={{0,64},{16,80},{32,96},{48,112},{64,0},{80,16},{96,32},{112,48},{1... | collective-permute-start | bytes 270344 | tf_op jit(solution)/shard_map/ppermute | solution.py:23
  88.4 7.3 %collective-permute-start.12 = (bf16[336,256]{1,0:T(8,128)(2,1)S(1)}, bf16[336,256]{1,0:T(8,128)(2,1)S(1)}, u32[]{:S(2)}, u32[]{:S(2)}) collective-permute-start(bf16[336,256]{1,0:T(8,128)(2,1)S(1)} %get-tuple-element.60.a), channel_id=1, source_target_pairs={{0,16},{16,0},{32,48},{48,32},{64,80},{80,64},{96,112},{112,96},{1... | collective-permute-start | bytes 516104 | tf_op jit(solution)/shard_map/ppermute | solution.py:23
  96.3 10.9 %collective-permute-start.13 = (bf16[656,256]{1,0:T(8,128)(2,1)S(1)}, bf16[656,256]{1,0:T(8,128)(2,1)S(1)}, u32[]{:S(2)}, u32[]{:S(2)}) collective-permute-start(bf16[656,256]{1,0:T(8,128)(2,1)S(1)} %get-tuple-element.62.two), channel_id=1, source_target_pairs={{0,48},{16,32},{32,16},{48,0},{64,112},{80,96},{96,80},{112,64},{1... | collective-permute-start | bytes 1007624 | tf_op jit(solution)/shard_map/ppermute | solution.py:23

commit v3 on v2

--- a/solution.py
+++ b/solution.py
@@ -27,7 +27,7 @@
     return lax.optimization_barrier((x, dep))[0]
 
 
-def call(kernel, outs, args, scratch=()):
+def call(kernel, outs, args, scratch=(), micros=0.5):
     return pl.pallas_call(
         kernel,
         out_shape=[jax.ShapeDtypeStruct(s, d) for s, d in outs],
@@ -35,6 +35,7 @@
         out_specs=[VMEM] * len(outs),
         scratch_shapes=[pltpu.VMEM(s, d) for s, d in scratch],
         compiler_params=pltpu.CompilerParams(vmem_limit_bytes=24 * 1024 * 1024),
+        cost_estimate=pl.CostEstimate(flops=int(micros * 1e9), bytes_accessed=0, transcendentals=0),
     )(*args)
 
 
@@ -137,12 +138,14 @@
     mx2[...] = jnp.broadcast_to(m, TOP)
 
 
-def out_kernel(ix, two, more, mx, out, scale):
+def out_kernel(ix, e0, e1, e2, e3, mx, out, scale):
     y = ix[0]
     n = 8 * ROWS
-    for d, (ref, k) in enumerate(((two, 0), (two, 1), (more, 1), (more, 0))):
-        out[:, y ^ d] = ref[k * n : (k + 1) * n].astype(F32).reshape(8, ROWS, COLS).astype(BF16)
-    m = jnp.maximum(mx[0:1], untail(more, 2 * n))
+    m = mx[0:1]
+    for d, e in enumerate((e0, e1, e2, e3)):
+        out[:, y ^ d] = e[0:n].astype(F32).reshape(8, ROWS, COLS).astype(BF16)
+        if d > 0:
+            m = jnp.maximum(m, untail(e, n))
     scale[...] = jnp.broadcast_to(m, TOP) + EPSILON
 
 
@@ -170,33 +173,42 @@
         quad[(2 * k + 1) * n : (2 * k + 2) * n] = b[k * n : (k + 1) * n]
 
 
-def product_kernel(place, a, b, wa, wb, out):
+def product_kernel(place, a, wa, wb, *rest):
+    out, buf, sem = rest[-3:]
     dims = (((1,), (1,)), ((), ()))
     n = 4 * TOK
-    for j, ref in enumerate((a, b)):
-        x = lax.dot_general(ref[0:n], wa[...], dims, preferred_element_type=F32)
-        x += lax.dot_general(ref[n:], wb[...], dims, preferred_element_type=F32)
-        x = x.astype(BF16)
+    copies = []
+    for j in range(wa.shape[0] // COLS):
+        at = slice(j * COLS, (j + 1) * COLS)
+        x = lax.dot_general(a[0:n], wa[at], dims, preferred_element_type=F32)
+        x += lax.dot_general(a[n:], wb[at], dims, preferred_element_type=F32)
+        buf[j] = x.astype(BF16)
         for i in range(4):
-            out[place[4 * j + i]] = x[i * TOK : (i + 1) * TOK]
-
-
-def product(place, quad, more, w, w_other):
+            src = buf.at[j, pl.ds(i * TOK, TOK)]
+            copy = pltpu.make_async_copy(src, out.at[place[i], :, pl.ds(j * COLS, COLS)], sem.at[j, i])
+            copy.start()
+            copies.append(copy)
+    for copy in copies:
+        copy.wait()
+
+
+def product(place, rows, w, w_other, prod=None):
     width = w.shape[0]
-    whole = pl.BlockSpec((8 * TOK, COLS), lambda i, s: (0, 0))
-    part = pl.BlockSpec((COLS, COLS), lambda i, s: (i, 0))
+    blocks = width // COLS
+    args = [place, rows, w, w_other] + ([] if prod is None else [prod])
     return pl.pallas_call(
         product_kernel,
-        grid_spec=pltpu.PrefetchScalarGridSpec(
-            num_scalar_prefetch=1,
-            grid=(width // COLS,),
-            in_specs=[whole, whole, part, part],
-            out_specs=pl.BlockSpec((8, TOK, COLS), lambda i, s: (0, 0, i)),
-        ),
+        in_specs=[SMEM, VMEM, VMEM, VMEM] + [pl.BlockSpec(memory_space=pl.ANY)] * (len(args) - 4),
+        out_specs=pl.BlockSpec(memory_space=pl.ANY),
         out_shape=jax.ShapeDtypeStruct((8, TOK, width), BF16),
+        scratch_shapes=[
+            pltpu.VMEM((blocks, 4 * TOK, COLS), BF16),
+            pltpu.SemaphoreType.DMA((blocks, 4)),
+        ],
+        input_output_aliases={} if prod is None else {4: 0},
         compiler_params=pltpu.CompilerParams(vmem_limit_bytes=24 * 1024 * 1024),
-        cost_estimate=pl.CostEstimate(flops=16 * TOK * width * 2 * COLS, bytes_accessed=5_600_000, transcendentals=0),
-    )(place, quad, more, w, w_other)
+        cost_estimate=pl.CostEstimate(flops=8 * TOK * width * 2 * COLS, bytes_accessed=3_500_000, transcendentals=0),
+    )(*args)
 
 
 def body(w_local, anchor, momentum, key_grad):
@@ -224,8 +236,8 @@
     kg_far = swap(kgm, "fsdp", 4)
     g2, g1, g3 = (swap(m, "replica", d) for d, m in ((2, m2), (1, m1), (3, m3)))
     h, own4 = call(y_kernel, [bf(160), fl(160)], (ix, own, a_y, g1, g2, g3), [fl(320)])
+    theirs, kg_mine, mx = call(pair_kernel, [bf(304), bf(288), top], (ix, kgm, kg_far, mx))
     h = swap(h, "replica", 4)
-    theirs, kg_mine, mx = call(pair_kernel, [bf(304), bf(288), top], (ix, kgm, kg_far, mx))
     kg_core = swap(theirs, "tensor", 1)
     h, own2 = call(near_kernel, [bf(80), fl(80)], (ix, own4, h))
     h = swap(h, "replica", 8)
@@ -236,17 +248,17 @@
     q, p_own, mx = call(lo_kernel, [bf(96), fl(40), top], (ix, own2, mom, h, *wide), [fl(80)])
     g = swap(q, "replica", 16)
     kg_x = swap(tie(both, q), "fsdp", 1)
-    fresh, mom_new, mx = call(hi_kernel, [bf(96), fl(40), top], (ix, q, p_own, mom, a_y, mx, g), [fl(80)])
+    fresh, mom_new, mx = call(hi_kernel, [bf(96), fl(40), top], (ix, q, p_own, mom, a_y, mx, g), [fl(80)], 6.0)
     near, mx = call(join_kernel, [bf(176), top], (ix, fresh, swap(fresh, "replica", 8), mx))
     far = swap(near, "replica", 4)
-    quad = call(quad_kernel, [bf(1152)], (ix, both, tie(kg_x, near)))[0]
+    quad = call(quad_kernel, [bf(1152)], (ix, both, tie(kg_x, fresh)))[0]
     more = swap(quad, "fsdp", 3)
-    eight, mx = call(eight_kernel, [bf(336), top], (ix, near, far, mx), [fl(320)])
-    two, mx = call(join_kernel, [bf(656), top], (ix, eight, swap(eight, "replica", 1), mx))
-    last = swap(two, "replica", 3)
     place = jnp.array([0, 4, 1, 5, 3, 7, 2, 6], jnp.int32) ^ f
-    prod = product(place, quad, tie(more, two), w, w_other)
-    new_weights, scale = call(out_kernel, [(four, BF16), top], (ix, two, tie(last, prod), mx))
+    prod = product(place[:4], quad, w, w_other)
+    eight, mx = call(eight_kernel, [bf(336), top], (ix, near, tie(far, prod), mx), [fl(320)])
+    e2, e1, e3 = (swap(eight, "replica", d) for d in (2, 1, 3))
+    prod = product(place[4:], tie(more, eight), w, w_other, prod)
+    new_weights, scale = call(out_kernel, [(four, BF16), top], (ix, eight, e1, tie(e2, prod), e3, mx))
     return new_weights.reshape(anchor.shape), mom_new[None, None], prod[None], scale[0, :1]
 
 

time: 110 us -> 106 us (0.964)
  waiting for transfers between devices: 22.5 us -> 14 us
  starting transfers between devices: 68.7 us -> 73.3 us
    ppermute x17 -> x18, waiting for transfers between devices: 22.5 us -> 14 us  [swap(): return lax.ppermute(x, axis, [(i, i ^ bit) for i in range(n)])]
    ppermute x17 -> x18, starting transfers between devices: 68.7 us -> 73.3 us  [swap(): return lax.ppermute(x, axis, [(i, i ^ bit) for i in range(n)])]
    pallas_call x12 -> x11, Pallas kernels: 8.77 us -> 8.19 us  [call(): pl.pallas_call(kernel, out_shape=[jax.ShapeDtypeStruct(s, d) for s, d in...]
    pallas_call x1 -> x2, Pallas kernels: 4.58 us -> 5.02 us  [product(): pl.pallas_call(product_kernel, in_specs=[SMEM, VMEM, VMEM, VMEM] + [pl.Bl...]
  transfers between devices with their start and end apart: 17 -> 18, of which waited for: 7 -> 6; matrix products, arithmetic and copies ran while one was open for 0% -> 0% of each run, Pallas kernels for 10% -> 10%
where the time goes in v3:
time: 106 us; the launch traced here: 105 us
  starting transfers between devices  73.3 us (69%)
  waiting for transfers between devices  14 us (13%)
  Pallas kernels  13.2 us (12%)
  local copies, waits for them, and re-layouts  3.77 us (4%)
    ppermute x18, starting transfers between devices, swap(): return lax.ppermute(x, axis, [(i, i ^ bit) for i in range(n)])  73.3 us
    ppermute x18, waiting for transfers between devices, swap(): return lax.ppermute(x, axis, [(i, i ^ bit) for i in range(n)])  14 us
    pallas_call x11, Pallas kernels, call(): pl.pallas_call(kernel, out_shape=[jax.ShapeDtypeStruct(s, d) for s, d in...  8.19 us
    pallas_call x2, Pallas kernels, product(): pl.pallas_call(product_kernel, in_specs=[SMEM, VMEM, VMEM, VMEM] + [pl.Bl...  5.02 us
    unnamed x12, local copies, waits for them, and re-layouts  3.1 us
  transfers between devices with their start and end apart: 18, of which 6 were waited for; matrix products, arithmetic and copies ran while one was open for 0% of the time, Pallas kernels for 10%

profile of v3, /device:TPU:24, one launch (start us, length us, event | category | flops | bytes accessed | tf_op | source)
XLA Modules:
  0.0 105.3 jit_solution(14352461181251964699)
XLA Ops:
  0.7 1.1 %copy-done = bf16[1,1280,256]{2,1,0:T(8,128)(2,1)S(1)} copy-done((bf16[1,1280,256]{2,1,0:T(8,128)(2,1)S(1)}, bf16[1,1280,256]{2,1,0:T(8,128)(2,1)}, u32[]{:S(2)}) %copy-start) | copy-done | bytes 655384
  1.8 1.1 %copy-done.2 = bf16[1280,256]{1,0:T(8,128)(2,1)S(1)} copy-done((bf16[1280,256]{1,0:T(8,128)(2,1)S(1)}, bf16[1280,256]{1,0:T(8,128)(2,1)}, u32[]{:S(2)}) %copy-start.2) | copy-done | bytes 655384
  2.9 0.9 copy-done.3
  3.8 0.8 shard_map.84
  4.6 15.7 %collective-permute-start.5 = (bf16[304,256]{1,0:T(8,128)(2,1)S(1)}, bf16[304,256]{1,0:T(8,128)(2,1)S(1)}, u32[]{:S(2)}, u32[]{:S(2)}) collective-permute-start(bf16[304,256]{1,0:T(8,128)(2,1)S(1)} %get-tuple-element.46.a), channel_id=1, source_target_pairs={{0,8},{2,10},{4,12},{6,14},{8,0},{10,2},{12,4},{14,6},{1,9},{3,11}... | collective-permute-start | bytes 466952 | tf_op jit(solution)/shard_map/ppermute | solution.py:23
  20.4 2.7 %collective-permute-start = (bf16[320,256]{1,0:T(8,128)(2,1)S(1)}, bf16[320,256]{1,0:T(8,128)(2,1)S(1)}, u32[]{:S(2)}, u32[]{:S(2)}) collective-permute-start(bf16[320,256]{1,0:T(8,128)(2,1)S(1)} %get-tuple-element.39), channel_id=1, source_target_pairs={{0,16},{16,0},{32,48},{48,32},{64,80},{80,64},{96,112},{112,96},{1... | collective-permute-start | bytes 491528 | tf_op jit(solution)/shard_map/ppermute | solution.py:23
  23.0 2.8 %collective-permute-start.1 = (bf16[320,256]{1,0:T(8,128)(2,1)S(1)}, bf16[320,256]{1,0:T(8,128)(2,1)S(1)}, u32[]{:S(2)}, u32[]{:S(2)}) collective-permute-start(bf16[320,256]{1,0:T(8,128)(2,1)S(1)} %get-tuple-element.40), channel_id=1, source_target_pairs={{0,32},{16,48},{32,0},{48,16},{64,96},{80,112},{96,64},{112,80},{1... | collective-permute-start | bytes 491528 | tf_op jit(solution)/shard_map/ppermute | solution.py:23
  25.9 4.9 %collective-permute-start.2 = (bf16[320,256]{1,0:T(8,128)(2,1)S(1)}, bf16[320,256]{1,0:T(8,128)(2,1)S(1)}, u32[]{:S(2)}, u32[]{:S(2)}) collective-permute-start(bf16[320,256]{1,0:T(8,128)(2,1)S(1)} %get-tuple-element.41), channel_id=1, source_target_pairs={{0,48},{16,32},{32,16},{48,0},{64,112},{80,96},{96,80},{112,64},{1... | collective-permute-start | bytes 491528 | tf_op jit(solution)/shard_map/ppermute | solution.py:23
  31.4 1.9 %collective-permute-start.6 = (bf16[304,256]{1,0:T(8,128)(2,1)S(1)}, bf16[304,256]{1,0:T(8,128)(2,1)S(1)}, u32[]{:S(2)}, u32[]{:S(2)}) collective-permute-start(bf16[304,256]{1,0:T(8,128)(2,1)S(1)} %get-tuple-element.49), channel_id=1, source_target_pairs={{0,1},{1,0},{2,3},{3,2},{4,5},{5,4},{6,7},{7,6},{8,9},{9,8},{10,11... | collective-permute-start | bytes 466952 | tf_op jit(solution)/shard_map/ppermute | solution.py:23
  33.4 1.9 %collective-permute-done.2.g3 = bf16[320,256]{1,0:T(8,128)(2,1)S(1)} collective-permute-done((bf16[320,256]{1,0:T(8,128)(2,1)S(1)}, bf16[320,256]{1,0:T(8,128)(2,1)S(1)}, u32[]{:S(2)}, u32[]{:S(2)}) %collective-permute-start.2) | collective-permute-done | bytes 163872 | tf_op jit(solution)/shard_map/ppermute | solution.py:23
  35.3 0.7 shard_map.85
  36.1 4.3 %collective-permute-start.3 = (bf16[160,256]{1,0:T(8,128)(2,1)S(1)}, bf16[160,256]{1,0:T(8,128)(2,1)S(1)}, u32[]{:S(2)}, u32[]{:S(2)}) collective-permute-start(bf16[160,256]{1,0:T(8,128)(2,1)S(1)} %get-tuple-element.43), channel_id=1, source_target_pairs={{0,64},{16,80},{32,96},{48,112},{64,0},{80,16},{96,32},{112,48},{1... | collective-permute-start | bytes 245768 | tf_op jit(solution)/shard_map/ppermute | solution.py:23
  41.0 3.4 %collective-permute-start.7 = (f32[8,128]{1,0:T(8,128)S(1)}, f32[8,128]{1,0:T(8,128)S(1)}, u32[]{:S(2)}, u32[]{:S(2)}) collective-permute-start(f32[8,128]{1,0:T(8,128)S(1)} %get-tuple-element.51), channel_id=1, source_target_pairs={{0,2},{2,0},{4,6},{6,4},{8,10},{10,8},{12,14},{14,12},{1,3},{3,1},... | collective-permute-start | bytes 12296 | tf_op jit(solution)/shard_map/ppermute | solution.py:23
  45.0 2.1 %collective-permute-start.4 = (bf16[80,256]{1,0:T(8,128)(2,1)S(1)}, bf16[80,256]{1,0:T(8,128)(2,1)S(1)}, u32[]{:S(2)}, u32[]{:S(2)}) collective-permute-start(bf16[80,256]{1,0:T(8,128)(2,1)S(1)} %get-tuple-element.45), channel_id=1, source_target_pairs={{0,128},{16,144},{32,160},{48,176},{64,192},{80,208},{96,224},{112... | collective-permute-start | bytes 122888 | tf_op jit(solution)/shard_map/ppermute | solution.py:23
  47.1 4.1 %collective-permute-start.8 = (f32[8,128]{1,0:T(8,128)S(1)}, f32[8,128]{1,0:T(8,128)S(1)}, u32[]{:S(2)}, u32[]{:S(2)}) collective-permute-start(f32[8,128]{1,0:T(8,128)S(1)} %max.3), channel_id=1, source_target_pairs={{0,6},{2,4},{4,2},{6,0},{8,14},{10,12},{12,10},{14,8},{1,7},{3,5},... | collective-permute-start | bytes 12296 | tf_op jit(solution)/shard_map/ppermute | solution.py:23
  51.2 2.6 %collective-permute-done.8 = f32[8,128]{1,0:T(8,128)S(1)} collective-permute-done((f32[8,128]{1,0:T(8,128)S(1)}, f32[8,128]{1,0:T(8,128)S(1)}, u32[]{:S(2)}, u32[]{:S(2)}) %collective-permute-start.8) | collective-permute-done | bytes 4128 | tf_op jit(solution)/shard_map/ppermute | solution.py:23
  54.4 8.2 %collective-permute-start.9 = (bf16[96,256]{1,0:T(8,128)(2,1)S(1)}, bf16[96,256]{1,0:T(8,128)(2,1)S(1)}, u32[]{:S(2)}, u32[]{:S(2)}) collective-permute-start(bf16[96,256]{1,0:T(8,128)(2,1)S(1)} %get-tuple-element.52.q), channel_id=1, source_target_pairs={{0,256},{16,272},{32,288},{48,304},{64,320},{80,336},{96,352},{112... | collective-permute-start | bytes 147464 | tf_op jit(solution)/shard_map/ppermute | solution.py:23
  62.7 1.9 %collective-permute-start.13 = (bf16[1280,256]{1,0:T(8,128)(2,1)S(1)}, bf16[1280,256]{1,0:T(8,128)(2,1)S(1)}, u32[]{:S(2)}, u32[]{:S(2)}) collective-permute-start(bf16[1280,256]{1,0:T(8,128)(2,1)S(1)} %bitcast.15), channel_id=1, source_target_pairs={{0,1},{1,0},{2,3},{3,2},{4,5},{5,4},{6,7},{7,6},{8,9},{9,8},{10,11... | collective-permute-start | bytes 1966088 | tf_op jit(solution)/shard_map/ppermute | solution.py:23
  64.6 2.2 %collective-permute-start.12 = (bf16[576,256]{1,0:T(8,128)(2,1)S(1)}, bf16[576,256]{1,0:T(8,128)(2,1)S(1)}, u32[]{:S(2)}, u32[]{:S(2)}) collective-permute-start(bf16[576,256]{1,0:T(8,128)(2,1)S(1)} %get-tuple-element.59.a), channel_id=1, source_target_pairs={{0,2},{2,0},{4,6},{6,4},{8,10},{10,8},{12,14},{14,12},{1,3},{3,1},... | collective-permute-start | bytes 884744 | tf_op jit(solution)/shard_map/ppermute | solution.py:23
  66.8 1.2 %shard_map.90 = (bf16[96,256]{1,0:T(8,128)(2,1)S(1)}, f32[40,256]{1,0:T(8,128)}, f32[8,256]{1,0:T(8,128)S(1)}) custom-call(s32[5]{0:T(128)S(1)} %stack.23.ix, bf16[96,256]{1,0:T(8,128)(2,1)S(1)} %get-tuple-element.52.q, f32[40,256]{1,0:T(8,128)S(1)} %get-tuple-element.53.p_own, f32[40,256]{1,0:T(8,128)S(1)} %bitcast.21, ...), custom_call_target="tpu_custom_call" | custom-call | flops 6000000000 | tf_op jit(solution)/shard_map/pallas_call | solution.py:31
  68.0 2.6 %collective-permute-start.10 = (bf16[96,256]{1,0:T(8,128)(2,1)S(1)}, bf16[96,256]{1,0:T(8,128)(2,1)S(1)}, u32[]{:S(2)}, u32[]{:S(2)}) collective-permute-start(bf16[96,256]{1,0:T(8,128)(2,1)S(1)} %get-tuple-element.55.a), channel_id=1, source_target_pairs={{0,128},{16,144},{32,160},{48,176},{64,192},{80,208},{96,224},{112... | collective-permute-start | bytes 147464 | tf_op jit(solution)/shard_map/ppermute | solution.py:23
  70.6 5.3 %collective-permute-done.12.b = bf16[576,256]{1,0:T(8,128)(2,1)S(1)} collective-permute-done((bf16[576,256]{1,0:T(8,128)(2,1)S(1)}, bf16[576,256]{1,0:T(8,128)(2,1)S(1)}, u32[]{:S(2)}, u32[]{:S(2)}) %collective-permute-start.12) | collective-permute-done | bytes 294944 | tf_op jit(solution)/shard_map/ppermute | solution.py:23
  76.5 4.7 %collective-permute-start.16 = (bf16[1152,256]{1,0:T(8,128)(2,1)S(1)}, bf16[1152,256]{1,0:T(8,128)(2,1)S(1)}, u32[]{:S(2)}, u32[]{:S(2)}) collective-permute-start(bf16[1152,256]{1,0:T(8,128)(2,1)S(1)} %shard_map.92.a), channel_id=1, source_target_pairs={{0,6},{2,4},{4,2},{6,0},{8,14},{10,12},{12,10},{14,8},{1,7},{3,5},... | collective-permute-start | bytes 1769480 | tf_op jit(solution)/shard_map/ppermute | solution.py:23
  81.8 2.4 %collective-permute-start.11 = (bf16[176,256]{1,0:T(8,128)(2,1)S(1)}, bf16[176,256]{1,0:T(8,128)(2,1)S(1)}, u32[]{:S(2)}, u32[]{:S(2)}) collective-permute-start(bf16[176,256]{1,0:T(8,128)(2,1)S(1)} %get-tuple-element.57.near), channel_id=1, source_target_pairs={{0,64},{16,80},{32,96},{48,112},{64,0},{80,16},{96,32},{112,48},{1... | collective-permute-start | bytes 270344 | tf_op jit(solution)/shard_map/ppermute | solution.py:23
  84.3 2.5 %shard_map.93.rest_0_ = bf16[8,144,1280]{2,1,0:T(8,128)(2,1)} custom-call(s32[4]{0:T(128)S(1)} %get-tuple-element.71.place, bf16[1152,256]{1,0:T(8,128)(2,1)S(1)} %shard_map.92.a, bf16[1280,256]{1,0:T(8,128)(2,1)S(1)} %bitcast.16, bf16[1280,256]{1,0:T(8,128)(2,1)S(1)} %collective-permute-done.13.wb), custom_call_target="tpu_custom_call" | custom-call | flops 754974720 | bytes 3500000 | tf_op jit(solution)/shard_map/pallas_call | solution.py:199
  86.8 1.4 %collective-permute-done.11.far = bf16[176,256]{1,0:T(8,128)(2,1)S(1)} collective-permute-done((bf16[176,256]{1,0:T(8,128)(2,1)S(1)}, bf16[176,256]{1,0:T(8,128)(2,1)S(1)}, u32[]{:S(2)}, u32[]{:S(2)}) %collective-permute-start.11) | collective-permute-done | bytes 90144 | tf_op jit(solution)/shard_map/ppermute | solution.py:23
  88.8 3.1 %collective-permute-start.15 = (bf16[336,256]{1,0:T(8,128)(2,1)S(1)}, bf16[336,256]{1,0:T(8,128)(2,1)S(1)}, u32[]{:S(2)}, u32[]{:S(2)}) collective-permute-start(bf16[336,256]{1,0:T(8,128)(2,1)S(1)} %get-tuple-element.63.e0), channel_id=1, source_target_pairs={{0,32},{16,48},{32,0},{48,16},{64,96},{80,112},{96,64},{112,80},{1... | collective-permute-start | bytes 516104 | tf_op jit(solution)/shard_map/ppermute | solution.py:23
  92.0 4.1 %collective-permute-start.17 = (bf16[336,256]{1,0:T(8,128)(2,1)S(1)}, bf16[336,256]{1,0:T(8,128)(2,1)S(1)}, u32[]{:S(2)}, u32[]{:S(2)}) collective-permute-start(bf16[336,256]{1,0:T(8,128)(2,1)S(1)} %get-tuple-element.63.e0), channel_id=1, source_target_pairs={{0,48},{16,32},{32,16},{48,0},{64,112},{80,96},{96,80},{112,64},{1... | collective-permute-start | bytes 516104 | tf_op jit(solution)/shard_map/ppermute | solution.py:23
  96.1 2.0 %collective-permute-start.14 = (bf16[336,256]{1,0:T(8,128)(2,1)S(1)}, bf16[336,256]{1,0:T(8,128)(2,1)S(1)}, u32[]{:S(2)}, u32[]{:S(2)}) collective-permute-start(bf16[336,256]{1,0:T(8,128)(2,1)S(1)} %get-tuple-element.63.e0), channel_id=1, source_target_pairs={{0,16},{16,0},{32,48},{48,32},{64,80},{80,64},{96,112},{112,96},{1... | collective-permute-start | bytes 516104 | tf_op jit(solution)/shard_map/ppermute | solution.py:23
  98.0 2.5 %shard_map.95 = bf16[8,144,1280]{2,1,0:T(8,128)(2,1)} custom-call(s32[4]{0:T(128)S(1)} %get-tuple-element.70.place, bf16[1152,256]{1,0:T(8,128)(2,1)S(1)} %collective-permute-done.16.a, bf16[1280,256]{1,0:T(8,128)(2,1)S(1)} %bitcast.17, bf16[1280,256]{1,0:T(8,128)(2,1)S(1)} %collective-permute-done.13.wb, ...), custom_call_target="tpu_custom_call", output_to_operand_aliasing={{}: (4, {})} | custom-call | flops 754974720 | bytes 3500000 | tf_op jit(solution)/shard_map/pallas_call | solution.py:199
  101.3 2.1 %collective-permute-done.14.e1 = bf16[336,256]{1,0:T(8,128)(2,1)S(1)} collective-permute-done((bf16[336,256]{1,0:T(8,128)(2,1)S(1)}, bf16[336,256]{1,0:T(8,128)(2,1)S(1)}, u32[]{:S(2)}, u32[]{:S(2)}) %collective-permute-start.14) | collective-permute-done | bytes 172064 | tf_op jit(solution)/shard_map/ppermute | solution.py:23
  103.4 1.4 %shard_map.96 = (bf16[8,4,40,256]{3,2,1,0:T(8,128)(2,1)}, f32[8,256]{1,0:T(8,128)S(1)}) custom-call(s32[5]{0:T(128)S(1)} %stack.23.ix, bf16[336,256]{1,0:T(8,128)(2,1)S(1)} %get-tuple-element.63.e0, bf16[336,256]{1,0:T(8,128)(2,1)S(1)} %collective-permute-done.14.e1, bf16[336,256]{1,0:T(8,128)(2,1)S(1)} %collective-permute-done.15.e2, ...), custom_call_target="tpu_custom_call" | custom-call | flops 500000000 | tf_op jit(solution)/shard_map/pallas_call | solution.py:31
  (36 shorter events, 5.5 us)
Async XLA Ops:
  0.7 1.1 %copy-start = (bf16[1,1280,256]{2,1,0:T(8,128)(2,1)S(1)}, bf16[1,1280,256]{2,1,0:T(8,128)(2,1)}, u32[]{:S(2)}) copy-start(bf16[1,1280,256]{2,1,0:T(8,128)(2,1)} %param.5) | copy-start | bytes 1966084
  1.8 1.1 %copy-start.2 = (bf16[1280,256]{1,0:T(8,128)(2,1)S(1)}, bf16[1280,256]{1,0:T(8,128)(2,1)}, u32[]{:S(2)}) copy-start(bf16[1280,256]{1,0:T(8,128)(2,1)} %param.6) | copy-start | bytes 1966084
  2.9 0.9 copy-start.3
  4.6 26.2 %collective-permute-start.5 = (bf16[304,256]{1,0:T(8,128)(2,1)S(1)}, bf16[304,256]{1,0:T(8,128)(2,1)S(1)}, u32[]{:S(2)}, u32[]{:S(2)}) collective-permute-start(bf16[304,256]{1,0:T(8,128)(2,1)S(1)} %get-tuple-element.46.a), channel_id=1, source_target_pairs={{0,8},{2,10},{4,12},{6,14},{8,0},{10,2},{12,4},{14,6},{1,9},{3,11}... | collective-permute-start | bytes 466952 | tf_op jit(solution)/shard_map/ppermute | solution.py:23
  20.4 13.0 %collective-permute-start = (bf16[320,256]{1,0:T(8,128)(2,1)S(1)}, bf16[320,256]{1,0:T(8,128)(2,1)S(1)}, u32[]{:S(2)}, u32[]{:S(2)}) collective-permute-start(bf16[320,256]{1,0:T(8,128)(2,1)S(1)} %get-tuple-element.39), channel_id=1, source_target_pairs={{0,16},{16,0},{32,48},{48,32},{64,80},{80,64},{96,112},{112,96},{1... | collective-permute-start | bytes 491528 | tf_op jit(solution)/shard_map/ppermute | solution.py:23
  23.0 10.3 %collective-permute-start.1 = (bf16[320,256]{1,0:T(8,128)(2,1)S(1)}, bf16[320,256]{1,0:T(8,128)(2,1)S(1)}, u32[]{:S(2)}, u32[]{:S(2)}) collective-permute-start(bf16[320,256]{1,0:T(8,128)(2,1)S(1)} %get-tuple-element.40), channel_id=1, source_target_pairs={{0,32},{16,48},{32,0},{48,16},{64,96},{80,112},{96,64},{112,80},{1... | collective-permute-start | bytes 491528 | tf_op jit(solution)/shard_map/ppermute | solution.py:23
  25.9 9.4 %collective-permute-start.2 = (bf16[320,256]{1,0:T(8,128)(2,1)S(1)}, bf16[320,256]{1,0:T(8,128)(2,1)S(1)}, u32[]{:S(2)}, u32[]{:S(2)}) collective-permute-start(bf16[320,256]{1,0:T(8,128)(2,1)S(1)} %get-tuple-element.41), channel_id=1, source_target_pairs={{0,48},{16,32},{32,16},{48,0},{64,112},{80,96},{96,80},{112,64},{1... | collective-permute-start | bytes 491528 | tf_op jit(solution)/shard_map/ppermute | solution.py:23
  31.4 22.4 %copy-start.4 = (f32[1,1,40,256]{3,2,1,0:T(8,128)S(1)}, f32[1,1,40,256]{3,2,1,0:T(8,128)}, u32[]{:S(2)}) copy-start(f32[1,1,40,256]{3,2,1,0:T(8,128)} %param.7) | copy-start | bytes 122884
  31.4 9.0 %collective-permute-start.6 = (bf16[304,256]{1,0:T(8,128)(2,1)S(1)}, bf16[304,256]{1,0:T(8,128)(2,1)S(1)}, u32[]{:S(2)}, u32[]{:S(2)}) collective-permute-start(bf16[304,256]{1,0:T(8,128)(2,1)S(1)} %get-tuple-element.49), channel_id=1, source_target_pairs={{0,1},{1,0},{2,3},{3,2},{4,5},{5,4},{6,7},{7,6},{8,9},{9,8},{10,11... | collective-permute-start | bytes 466952 | tf_op jit(solution)/shard_map/ppermute | solution.py:23
  36.1 26.6 %copy-start.1 = (bf16[1,1280,256]{2,1,0:T(8,128)(2,1)S(1)}, bf16[1,1280,256]{2,1,0:T(8,128)(2,1)}, u32[]{:S(2)}) copy-start(bf16[1,1280,256]{2,1,0:T(8,128)(2,1)} %param.5) | copy-start | bytes 1966084
  36.1 8.3 %collective-permute-start.3 = (bf16[160,256]{1,0:T(8,128)(2,1)S(1)}, bf16[160,256]{1,0:T(8,128)(2,1)S(1)}, u32[]{:S(2)}, u32[]{:S(2)}) collective-permute-start(bf16[160,256]{1,0:T(8,128)(2,1)S(1)} %get-tuple-element.43), channel_id=1, source_target_pairs={{0,64},{16,80},{32,96},{48,112},{64,0},{80,16},{96,32},{112,48},{1... | collective-permute-start | bytes 245768 | tf_op jit(solution)/shard_map/ppermute | solution.py:23
  41.0 6.1 %collective-permute-start.7 = (f32[8,128]{1,0:T(8,128)S(1)}, f32[8,128]{1,0:T(8,128)S(1)}, u32[]{:S(2)}, u32[]{:S(2)}) collective-permute-start(f32[8,128]{1,0:T(8,128)S(1)} %get-tuple-element.51), channel_id=1, source_target_pairs={{0,2},{2,0},{4,6},{6,4},{8,10},{10,8},{12,14},{14,12},{1,3},{3,1},... | collective-permute-start | bytes 12296 | tf_op jit(solution)/shard_map/ppermute | solution.py:23
  45.0 8.9 %collective-permute-start.4 = (bf16[80,256]{1,0:T(8,128)(2,1)S(1)}, bf16[80,256]{1,0:T(8,128)(2,1)S(1)}, u32[]{:S(2)}, u32[]{:S(2)}) collective-permute-start(bf16[80,256]{1,0:T(8,128)(2,1)S(1)} %get-tuple-element.45), channel_id=1, source_target_pairs={{0,128},{16,144},{32,160},{48,176},{64,192},{80,208},{96,224},{112... | collective-permute-start | bytes 122888 | tf_op jit(solution)/shard_map/ppermute | solution.py:23
  47.1 6.7 %collective-permute-start.8 = (f32[8,128]{1,0:T(8,128)S(1)}, f32[8,128]{1,0:T(8,128)S(1)}, u32[]{:S(2)}, u32[]{:S(2)}) collective-permute-start(f32[8,128]{1,0:T(8,128)S(1)} %max.3), channel_id=1, source_target_pairs={{0,6},{2,4},{4,2},{6,0},{8,14},{10,12},{12,10},{14,8},{1,7},{3,5},... | collective-permute-start | bytes 12296 | tf_op jit(solution)/shard_map/ppermute | solution.py:23
  54.4 12.4 %collective-permute-start.9 = (bf16[96,256]{1,0:T(8,128)(2,1)S(1)}, bf16[96,256]{1,0:T(8,128)(2,1)S(1)}, u32[]{:S(2)}, u32[]{:S(2)}) collective-permute-start(bf16[96,256]{1,0:T(8,128)(2,1)S(1)} %get-tuple-element.52.q), channel_id=1, source_target_pairs={{0,256},{16,272},{32,288},{48,304},{64,320},{80,336},{96,352},{112... | collective-permute-start | bytes 147464 | tf_op jit(solution)/shard_map/ppermute | solution.py:23
  62.7 21.6 %collective-permute-start.13 = (bf16[1280,256]{1,0:T(8,128)(2,1)S(1)}, bf16[1280,256]{1,0:T(8,128)(2,1)S(1)}, u32[]{:S(2)}, u32[]{:S(2)}) collective-permute-start(bf16[1280,256]{1,0:T(8,128)(2,1)S(1)} %bitcast.15), channel_id=1, source_target_pairs={{0,1},{1,0},{2,3},{3,2},{4,5},{5,4},{6,7},{7,6},{8,9},{9,8},{10,11... | collective-permute-start | bytes 1966088 | tf_op jit(solution)/shard_map/ppermute | solution.py:23
  64.6 11.3 %collective-permute-start.12 = (bf16[576,256]{1,0:T(8,128)(2,1)S(1)}, bf16[576,256]{1,0:T(8,128)(2,1)S(1)}, u32[]{:S(2)}, u32[]{:S(2)}) collective-permute-start(bf16[576,256]{1,0:T(8,128)(2,1)S(1)} %get-tuple-element.59.a), channel_id=1, source_target_pairs={{0,2},{2,0},{4,6},{6,4},{8,10},{10,8},{12,14},{14,12},{1,3},{3,1},... | collective-permute-start | bytes 884744 | tf_op jit(solution)/shard_map/ppermute | solution.py:23
  66.8 14.4 %copy-start.5 = (s32[8]{0:T(128)S(1)}, s32[8]{0:T(128)}, u32[]{:S(2)}) copy-start(s32[8]{0:T(128)} %constant.22.clone) | copy-start | bytes 100
  68.0 13.2 %collective-permute-start.10 = (bf16[96,256]{1,0:T(8,128)(2,1)S(1)}, bf16[96,256]{1,0:T(8,128)(2,1)S(1)}, u32[]{:S(2)}, u32[]{:S(2)}) collective-permute-start(bf16[96,256]{1,0:T(8,128)(2,1)S(1)} %get-tuple-element.55.a), channel_id=1, source_target_pairs={{0,128},{16,144},{32,160},{48,176},{64,192},{80,208},{96,224},{112... | collective-permute-start | bytes 147464 | tf_op jit(solution)/shard_map/ppermute | solution.py:23
  76.5 21.5 %collective-permute-start.16 = (bf16[1152,256]{1,0:T(8,128)(2,1)S(1)}, bf16[1152,256]{1,0:T(8,128)(2,1)S(1)}, u32[]{:S(2)}, u32[]{:S(2)}) collective-permute-start(bf16[1152,256]{1,0:T(8,128)(2,1)S(1)} %shard_map.92.a), channel_id=1, source_target_pairs={{0,6},{2,4},{4,2},{6,0},{8,14},{10,12},{12,10},{14,8},{1,7},{3,5},... | collective-permute-start | bytes 1769480 | tf_op jit(solution)/shard_map/ppermute | solution.py:23
  81.8 6.4 %collective-permute-start.11 = (bf16[176,256]{1,0:T(8,128)(2,1)S(1)}, bf16[176,256]{1,0:T(8,128)(2,1)S(1)}, u32[]{:S(2)}, u32[]{:S(2)}) collective-permute-start(bf16[176,256]{1,0:T(8,128)(2,1)S(1)} %get-tuple-element.57.near), channel_id=1, source_target_pairs={{0,64},{16,80},{32,96},{48,112},{64,0},{80,16},{96,32},{112,48},{1... | collective-permute-start | bytes 270344 | tf_op jit(solution)/shard_map/ppermute | solution.py:23
  88.8 11.8 %collective-permute-start.15 = (bf16[336,256]{1,0:T(8,128)(2,1)S(1)}, bf16[336,256]{1,0:T(8,128)(2,1)S(1)}, u32[]{:S(2)}, u32[]{:S(2)}) collective-permute-start(bf16[336,256]{1,0:T(8,128)(2,1)S(1)} %get-tuple-element.63.e0), channel_id=1, source_target_pairs={{0,32},{16,48},{32,0},{48,16},{64,96},{80,112},{96,64},{112,80},{1... | collective-permute-start | bytes 516104 | tf_op jit(solution)/shard_map/ppermute | solution.py:23
  92.0 9.3 %collective-permute-start.17 = (bf16[336,256]{1,0:T(8,128)(2,1)S(1)}, bf16[336,256]{1,0:T(8,128)(2,1)S(1)}, u32[]{:S(2)}, u32[]{:S(2)}) collective-permute-start(bf16[336,256]{1,0:T(8,128)(2,1)S(1)} %get-tuple-element.63.e0), channel_id=1, source_target_pairs={{0,48},{16,32},{32,16},{48,0},{64,112},{80,96},{96,80},{112,64},{1... | collective-permute-start | bytes 516104 | tf_op jit(solution)/shard_map/ppermute | solution.py:23
  96.1 7.3 %collective-permute-start.14 = (bf16[336,256]{1,0:T(8,128)(2,1)S(1)}, bf16[336,256]{1,0:T(8,128)(2,1)S(1)}, u32[]{:S(2)}, u32[]{:S(2)}) collective-permute-start(bf16[336,256]{1,0:T(8,128)(2,1)S(1)} %get-tuple-element.63.e0), channel_id=1, source_target_pairs={{0,16},{16,0},{32,48},{48,32},{64,80},{80,64},{96,112},{112,96},{1... | collective-permute-start | bytes 516104 | tf_op jit(solution)/shard_map/ppermute | solution.py:23

commit v4 on v3

--- a/solution.py
+++ b/solution.py
@@ -116,24 +116,15 @@
     mx2[...] = jnp.broadcast_to(m, TOP)
 
 
-def join_kernel(ix, a, b, mx, out, mx2):
-    n = b.shape[0] - TAIL
-    m = jnp.maximum(mx[0:1], untail(b, n))
-    out[0:n] = a[0:n]
-    out[n : 2 * n] = b[0:n]
-    out[2 * n :] = tail(m)
-    mx2[...] = jnp.broadcast_to(m, TOP)
-
-
-def eight_kernel(ix, near, far, mx, eight, mx2, s):
+def eight_kernel(ix, f0, f1, f2, f3, mx, eight, mx2, s):
     lo = ix[2]
-    for j, ref in enumerate((near, far)):
-        x = ref[0 : 4 * ROWS].astype(F32)
-        for k in range(2):
-            for b in range(2):
-                at = (2 * k + b) * ROWS
-                s[pl.ds((4 * b + (lo ^ (j + 2 * k))) * ROWS, ROWS)] = x[at : at + ROWS]
-    m = jnp.maximum(mx[0:1], untail(far, 4 * ROWS))
+    m = mx[0:1]
+    for d, ref in enumerate((f0, f1, f2, f3)):
+        x = ref[0 : 2 * ROWS].astype(F32)
+        for b in range(2):
+            s[pl.ds((4 * b + (lo ^ d)) * ROWS, ROWS)] = x[b * ROWS : (b + 1) * ROWS]
+        if d > 0:
+            m = jnp.maximum(m, untail(ref, 2 * ROWS))
     put(eight, s[...], m)
     mx2[...] = jnp.broadcast_to(m, TOP)
 
@@ -249,13 +240,12 @@
     g = swap(q, "replica", 16)
     kg_x = swap(tie(both, q), "fsdp", 1)
     fresh, mom_new, mx = call(hi_kernel, [bf(96), fl(40), top], (ix, q, p_own, mom, a_y, mx, g), [fl(80)], 6.0)
-    near, mx = call(join_kernel, [bf(176), top], (ix, fresh, swap(fresh, "replica", 8), mx))
-    far = swap(near, "replica", 4)
-    quad = call(quad_kernel, [bf(1152)], (ix, both, tie(kg_x, fresh)))[0]
+    f3, f2, f1 = (swap(fresh, "replica", 4 * d) for d in (3, 2, 1))
+    quad = call(quad_kernel, [bf(1152)], (ix, both, tie(kg_x, (f1, f2, f3))))[0]
     more = swap(quad, "fsdp", 3)
     place = jnp.array([0, 4, 1, 5, 3, 7, 2, 6], jnp.int32) ^ f
     prod = product(place[:4], quad, w, w_other)
-    eight, mx = call(eight_kernel, [bf(336), top], (ix, near, tie(far, prod), mx), [fl(320)])
+    eight, mx = call(eight_kernel, [bf(336), top], (ix, fresh, f1, f2, f3, mx), [fl(320)])
     e2, e1, e3 = (swap(eight, "replica", d) for d in (2, 1, 3))
     prod = product(place[4:], tie(more, eight), w, w_other, prod)
     new_weights, scale = call(out_kernel, [(four, BF16), top], (ix, eight, e1, tie(e2, prod), e3, mx))

time: 106 us -> 105 us (level)
  waiting for transfers between devices: 14 us -> 7.26 us
  starting transfers between devices: 73.3 us -> 78.8 us
    ppermute x18 -> x19, waiting for transfers between devices: 14 us -> 7.26 us  [swap(): return lax.ppermute(x, axis, [(i, i ^ bit) for i in range(n)])]
    ppermute x18 -> x19, starting transfers between devices: 73.3 us -> 78.8 us  [swap(): return lax.ppermute(x, axis, [(i, i ^ bit) for i in range(n)])]
    pallas_call x11 -> x10, Pallas kernels: 8.19 us -> 7.62 us  [call(): pl.pallas_call(kernel, out_shape=[jax.ShapeDtypeStruct(s, d) for s, d in...]
  transfers between devices with their start and end apart: 18 -> 19, of which waited for: 6 -> 4; matrix products, arithmetic and copies ran while one was open for 0% -> 0% of each run, Pallas kernels for 10% -> 9%
where the time goes in v4:
time: 105 us; the launch traced here: 103 us
  starting transfers between devices  78.8 us (75%)
  Pallas kernels  12.6 us (12%)
  waiting for transfers between devices  7.26 us (7%)
  local copies, waits for them, and re-layouts  3.77 us (4%)
    ppermute x19, starting transfers between devices, swap(): return lax.ppermute(x, axis, [(i, i ^ bit) for i in range(n)])  78.8 us
    pallas_call x10, Pallas kernels, call(): pl.pallas_call(kernel, out_shape=[jax.ShapeDtypeStruct(s, d) for s, d in...  7.62 us
    ppermute x19, waiting for transfers between devices, swap(): return lax.ppermute(x, axis, [(i, i ^ bit) for i in range(n)])  7.26 us
    pallas_call x2, Pallas kernels, product(): pl.pallas_call(product_kernel, in_specs=[SMEM, VMEM, VMEM, VMEM] + [pl.Bl...  5.02 us
    unnamed x12, local copies, waits for them, and re-layouts  3.1 us
  transfers between devices with their start and end apart: 19, of which 4 were waited for; matrix products, arithmetic and copies ran while one was open for 0% of the time, Pallas kernels for 9%

profile of v4, /device:TPU:24, one launch (start us, length us, event | category | flops | bytes accessed | tf_op | source)
XLA Modules:
  0.0 103.5 jit_solution(522141880036477400)
XLA Ops:
  0.7 1.1 %copy-done = bf16[1,1280,256]{2,1,0:T(8,128)(2,1)S(1)} copy-done((bf16[1,1280,256]{2,1,0:T(8,128)(2,1)S(1)}, bf16[1,1280,256]{2,1,0:T(8,128)(2,1)}, u32[]{:S(2)}) %copy-start) | copy-done | bytes 655384
  1.8 1.1 %copy-done.2 = bf16[1280,256]{1,0:T(8,128)(2,1)S(1)} copy-done((bf16[1280,256]{1,0:T(8,128)(2,1)S(1)}, bf16[1280,256]{1,0:T(8,128)(2,1)}, u32[]{:S(2)}) %copy-start.2) | copy-done | bytes 655384
  2.9 0.9 copy-done.3
  3.8 0.8 shard_map.84
  4.6 15.7 %collective-permute-start.5 = (bf16[304,256]{1,0:T(8,128)(2,1)S(1)}, bf16[304,256]{1,0:T(8,128)(2,1)S(1)}, u32[]{:S(2)}, u32[]{:S(2)}) collective-permute-start(bf16[304,256]{1,0:T(8,128)(2,1)S(1)} %get-tuple-element.43.a), channel_id=1, source_target_pairs={{0,8},{2,10},{4,12},{6,14},{8,0},{10,2},{12,4},{14,6},{1,9},{3,11}... | collective-permute-start | bytes 466952 | tf_op jit(solution)/shard_map/ppermute | solution.py:23
  20.4 2.7 %collective-permute-start = (bf16[320,256]{1,0:T(8,128)(2,1)S(1)}, bf16[320,256]{1,0:T(8,128)(2,1)S(1)}, u32[]{:S(2)}, u32[]{:S(2)}) collective-permute-start(bf16[320,256]{1,0:T(8,128)(2,1)S(1)} %get-tuple-element.36), channel_id=1, source_target_pairs={{0,16},{16,0},{32,48},{48,32},{64,80},{80,64},{96,112},{112,96},{1... | collective-permute-start | bytes 491528 | tf_op jit(solution)/shard_map/ppermute | solution.py:23
  23.0 2.8 %collective-permute-start.1 = (bf16[320,256]{1,0:T(8,128)(2,1)S(1)}, bf16[320,256]{1,0:T(8,128)(2,1)S(1)}, u32[]{:S(2)}, u32[]{:S(2)}) collective-permute-start(bf16[320,256]{1,0:T(8,128)(2,1)S(1)} %get-tuple-element.37), channel_id=1, source_target_pairs={{0,32},{16,48},{32,0},{48,16},{64,96},{80,112},{96,64},{112,80},{1... | collective-permute-start | bytes 491528 | tf_op jit(solution)/shard_map/ppermute | solution.py:23
  25.9 4.9 %collective-permute-start.2 = (bf16[320,256]{1,0:T(8,128)(2,1)S(1)}, bf16[320,256]{1,0:T(8,128)(2,1)S(1)}, u32[]{:S(2)}, u32[]{:S(2)}) collective-permute-start(bf16[320,256]{1,0:T(8,128)(2,1)S(1)} %get-tuple-element.38), channel_id=1, source_target_pairs={{0,48},{16,32},{32,16},{48,0},{64,112},{80,96},{96,80},{112,64},{1... | collective-permute-start | bytes 491528 | tf_op jit(solution)/shard_map/ppermute | solution.py:23
  31.4 1.9 %collective-permute-start.6 = (bf16[304,256]{1,0:T(8,128)(2,1)S(1)}, bf16[304,256]{1,0:T(8,128)(2,1)S(1)}, u32[]{:S(2)}, u32[]{:S(2)}) collective-permute-start(bf16[304,256]{1,0:T(8,128)(2,1)S(1)} %get-tuple-element.46), channel_id=1, source_target_pairs={{0,1},{1,0},{2,3},{3,2},{4,5},{5,4},{6,7},{7,6},{8,9},{9,8},{10,11... | collective-permute-start | bytes 466952 | tf_op jit(solution)/shard_map/ppermute | solution.py:23
  33.4 1.9 %collective-permute-done.2.g3 = bf16[320,256]{1,0:T(8,128)(2,1)S(1)} collective-permute-done((bf16[320,256]{1,0:T(8,128)(2,1)S(1)}, bf16[320,256]{1,0:T(8,128)(2,1)S(1)}, u32[]{:S(2)}, u32[]{:S(2)}) %collective-permute-start.2) | collective-permute-done | bytes 163872 | tf_op jit(solution)/shard_map/ppermute | solution.py:23
  35.3 0.7 shard_map.85
  36.1 4.3 %collective-permute-start.3 = (bf16[160,256]{1,0:T(8,128)(2,1)S(1)}, bf16[160,256]{1,0:T(8,128)(2,1)S(1)}, u32[]{:S(2)}, u32[]{:S(2)}) collective-permute-start(bf16[160,256]{1,0:T(8,128)(2,1)S(1)} %get-tuple-element.40), channel_id=1, source_target_pairs={{0,64},{16,80},{32,96},{48,112},{64,0},{80,16},{96,32},{112,48},{1... | collective-permute-start | bytes 245768 | tf_op jit(solution)/shard_map/ppermute | solution.py:23
  41.0 3.4 %collective-permute-start.7 = (f32[8,128]{1,0:T(8,128)S(1)}, f32[8,128]{1,0:T(8,128)S(1)}, u32[]{:S(2)}, u32[]{:S(2)}) collective-permute-start(f32[8,128]{1,0:T(8,128)S(1)} %get-tuple-element.48), channel_id=1, source_target_pairs={{0,2},{2,0},{4,6},{6,4},{8,10},{10,8},{12,14},{14,12},{1,3},{3,1},... | collective-permute-start | bytes 12296 | tf_op jit(solution)/shard_map/ppermute | solution.py:23
  45.0 2.1 %collective-permute-start.4 = (bf16[80,256]{1,0:T(8,128)(2,1)S(1)}, bf16[80,256]{1,0:T(8,128)(2,1)S(1)}, u32[]{:S(2)}, u32[]{:S(2)}) collective-permute-start(bf16[80,256]{1,0:T(8,128)(2,1)S(1)} %get-tuple-element.42), channel_id=1, source_target_pairs={{0,128},{16,144},{32,160},{48,176},{64,192},{80,208},{96,224},{112... | collective-permute-start | bytes 122888 | tf_op jit(solution)/shard_map/ppermute | solution.py:23
  47.1 4.1 %collective-permute-start.8 = (f32[8,128]{1,0:T(8,128)S(1)}, f32[8,128]{1,0:T(8,128)S(1)}, u32[]{:S(2)}, u32[]{:S(2)}) collective-permute-start(f32[8,128]{1,0:T(8,128)S(1)} %max.3), channel_id=1, source_target_pairs={{0,6},{2,4},{4,2},{6,0},{8,14},{10,12},{12,10},{14,8},{1,7},{3,5},... | collective-permute-start | bytes 12296 | tf_op jit(solution)/shard_map/ppermute | solution.py:23
  51.2 2.6 %collective-permute-done.8 = f32[8,128]{1,0:T(8,128)S(1)} collective-permute-done((f32[8,128]{1,0:T(8,128)S(1)}, f32[8,128]{1,0:T(8,128)S(1)}, u32[]{:S(2)}, u32[]{:S(2)}) %collective-permute-start.8) | collective-permute-done | bytes 4128 | tf_op jit(solution)/shard_map/ppermute | solution.py:23
  54.4 8.2 %collective-permute-start.9 = (bf16[96,256]{1,0:T(8,128)(2,1)S(1)}, bf16[96,256]{1,0:T(8,128)(2,1)S(1)}, u32[]{:S(2)}, u32[]{:S(2)}) collective-permute-start(bf16[96,256]{1,0:T(8,128)(2,1)S(1)} %get-tuple-element.49.q), channel_id=1, source_target_pairs={{0,256},{16,272},{32,288},{48,304},{64,320},{80,336},{96,352},{112... | collective-permute-start | bytes 147464 | tf_op jit(solution)/shard_map/ppermute | solution.py:23
  62.7 1.9 %collective-permute-start.17 = (bf16[1280,256]{1,0:T(8,128)(2,1)S(1)}, bf16[1280,256]{1,0:T(8,128)(2,1)S(1)}, u32[]{:S(2)}, u32[]{:S(2)}) collective-permute-start(bf16[1280,256]{1,0:T(8,128)(2,1)S(1)} %bitcast.15), channel_id=1, source_target_pairs={{0,1},{1,0},{2,3},{3,2},{4,5},{5,4},{6,7},{7,6},{8,9},{9,8},{10,11... | collective-permute-start | bytes 1966088 | tf_op jit(solution)/shard_map/ppermute | solution.py:23
  64.6 2.2 %collective-permute-start.15 = (bf16[576,256]{1,0:T(8,128)(2,1)S(1)}, bf16[576,256]{1,0:T(8,128)(2,1)S(1)}, u32[]{:S(2)}, u32[]{:S(2)}) collective-permute-start(bf16[576,256]{1,0:T(8,128)(2,1)S(1)} %get-tuple-element.56.a), channel_id=1, source_target_pairs={{0,2},{2,0},{4,6},{6,4},{8,10},{10,8},{12,14},{14,12},{1,3},{3,1},... | collective-permute-start | bytes 884744 | tf_op jit(solution)/shard_map/ppermute | solution.py:23
  66.8 1.2 %shard_map.90 = (bf16[96,256]{1,0:T(8,128)(2,1)S(1)}, f32[40,256]{1,0:T(8,128)}, f32[8,256]{1,0:T(8,128)S(1)}) custom-call(s32[5]{0:T(128)S(1)} %stack.23.ix, bf16[96,256]{1,0:T(8,128)(2,1)S(1)} %get-tuple-element.49.q, f32[40,256]{1,0:T(8,128)S(1)} %get-tuple-element.50.p_own, f32[40,256]{1,0:T(8,128)S(1)} %bitcast.21, ...), custom_call_target="tpu_custom_call" | custom-call | flops 6000000000 | tf_op jit(solution)/shard_map/pallas_call | solution.py:31
  68.0 2.8 %collective-permute-start.10 = (bf16[96,256]{1,0:T(8,128)(2,1)S(1)}, bf16[96,256]{1,0:T(8,128)(2,1)S(1)}, u32[]{:S(2)}, u32[]{:S(2)}) collective-permute-start(bf16[96,256]{1,0:T(8,128)(2,1)S(1)} %get-tuple-element.52.f0), channel_id=1, source_target_pairs={{0,64},{16,80},{32,96},{48,112},{64,0},{80,16},{96,32},{112,48},{1... | collective-permute-start | bytes 147464 | tf_op jit(solution)/shard_map/ppermute | solution.py:23
  70.9 2.1 %collective-permute-start.11 = (bf16[96,256]{1,0:T(8,128)(2,1)S(1)}, bf16[96,256]{1,0:T(8,128)(2,1)S(1)}, u32[]{:S(2)}, u32[]{:S(2)}) collective-permute-start(bf16[96,256]{1,0:T(8,128)(2,1)S(1)} %get-tuple-element.52.f0), channel_id=1, source_target_pairs={{0,128},{16,144},{32,160},{48,176},{64,192},{80,208},{96,224},{112... | collective-permute-start | bytes 147464 | tf_op jit(solution)/shard_map/ppermute | solution.py:23
  73.0 5.2 %collective-permute-start.12 = (bf16[96,256]{1,0:T(8,128)(2,1)S(1)}, bf16[96,256]{1,0:T(8,128)(2,1)S(1)}, u32[]{:S(2)}, u32[]{:S(2)}) collective-permute-start(bf16[96,256]{1,0:T(8,128)(2,1)S(1)} %get-tuple-element.52.f0), channel_id=1, source_target_pairs={{0,192},{16,208},{32,224},{48,240},{64,128},{80,144},{96,160},{112... | collective-permute-start | bytes 147464 | tf_op jit(solution)/shard_map/ppermute | solution.py:23
  78.7 2.1 %collective-permute-done.12.f3 = bf16[96,256]{1,0:T(8,128)(2,1)S(1)} collective-permute-done((bf16[96,256]{1,0:T(8,128)(2,1)S(1)}, bf16[96,256]{1,0:T(8,128)(2,1)S(1)}, u32[]{:S(2)}, u32[]{:S(2)}) %collective-permute-start.12) | collective-permute-done | bytes 49184 | tf_op jit(solution)/shard_map/ppermute | solution.py:23
  81.4 4.5 %collective-permute-start.16 = (bf16[1152,256]{1,0:T(8,128)(2,1)S(1)}, bf16[1152,256]{1,0:T(8,128)(2,1)S(1)}, u32[]{:S(2)}, u32[]{:S(2)}) collective-permute-start(bf16[1152,256]{1,0:T(8,128)(2,1)S(1)} %shard_map.92.a), channel_id=1, source_target_pairs={{0,6},{2,4},{4,2},{6,0},{8,14},{10,12},{12,10},{14,8},{1,7},{3,5},... | collective-permute-start | bytes 1769480 | tf_op jit(solution)/shard_map/ppermute | solution.py:23
  85.9 0.6 shard_map.91
  86.5 3.1 %collective-permute-start.14 = (bf16[336,256]{1,0:T(8,128)(2,1)S(1)}, bf16[336,256]{1,0:T(8,128)(2,1)S(1)}, u32[]{:S(2)}, u32[]{:S(2)}) collective-permute-start(bf16[336,256]{1,0:T(8,128)(2,1)S(1)} %get-tuple-element.54.e0), channel_id=1, source_target_pairs={{0,32},{16,48},{32,0},{48,16},{64,96},{80,112},{96,64},{112,80},{1... | collective-permute-start | bytes 516104 | tf_op jit(solution)/shard_map/ppermute | solution.py:23
  89.7 2.4 %collective-permute-start.13 = (bf16[336,256]{1,0:T(8,128)(2,1)S(1)}, bf16[336,256]{1,0:T(8,128)(2,1)S(1)}, u32[]{:S(2)}, u32[]{:S(2)}) collective-permute-start(bf16[336,256]{1,0:T(8,128)(2,1)S(1)} %get-tuple-element.54.e0), channel_id=1, source_target_pairs={{0,16},{16,0},{32,48},{48,32},{64,80},{80,64},{96,112},{112,96},{1... | collective-permute-start | bytes 516104 | tf_op jit(solution)/shard_map/ppermute | solution.py:23
  92.1 4.3 %collective-permute-start.18 = (bf16[336,256]{1,0:T(8,128)(2,1)S(1)}, bf16[336,256]{1,0:T(8,128)(2,1)S(1)}, u32[]{:S(2)}, u32[]{:S(2)}) collective-permute-start(bf16[336,256]{1,0:T(8,128)(2,1)S(1)} %get-tuple-element.54.e0), channel_id=1, source_target_pairs={{0,48},{16,32},{32,16},{48,0},{64,112},{80,96},{96,80},{112,64},{1... | collective-permute-start | bytes 516104 | tf_op jit(solution)/shard_map/ppermute | solution.py:23
  96.4 2.5 %shard_map.93.rest_0_ = bf16[8,144,1280]{2,1,0:T(8,128)(2,1)} custom-call(s32[4]{0:T(128)S(1)} %get-tuple-element.64.place, bf16[1152,256]{1,0:T(8,128)(2,1)S(1)} %shard_map.92.a, bf16[1280,256]{1,0:T(8,128)(2,1)S(1)} %bitcast.16, bf16[1280,256]{1,0:T(8,128)(2,1)S(1)} %collective-permute-done.17.wb), custom_call_target="tpu_custom_call" | custom-call | flops 754974720 | bytes 3500000 | tf_op jit(solution)/shard_map/pallas_call | solution.py:190
  99.0 2.5 %shard_map.94 = bf16[8,144,1280]{2,1,0:T(8,128)(2,1)} custom-call(s32[4]{0:T(128)S(1)} %get-tuple-element.65.place, bf16[1152,256]{1,0:T(8,128)(2,1)S(1)} %collective-permute-done.16.a, bf16[1280,256]{1,0:T(8,128)(2,1)S(1)} %bitcast.17, bf16[1280,256]{1,0:T(8,128)(2,1)S(1)} %collective-permute-done.17.wb, ...), custom_call_target="tpu_custom_call", output_to_operand_aliasing={{}: (4, {})} | custom-call | flops 754974720 | bytes 3500000 | tf_op jit(solution)/shard_map/pallas_call | solution.py:190
  101.5 1.4 %shard_map.95 = (bf16[8,4,40,256]{3,2,1,0:T(8,128)(2,1)}, f32[8,256]{1,0:T(8,128)S(1)}) custom-call(s32[5]{0:T(128)S(1)} %stack.23.ix, bf16[336,256]{1,0:T(8,128)(2,1)S(1)} %get-tuple-element.54.e0, bf16[336,256]{1,0:T(8,128)(2,1)S(1)} %collective-permute-done.13.e1, bf16[336,256]{1,0:T(8,128)(2,1)S(1)} %collective-permute-done.14.e2, ...), custom_call_target="tpu_custom_call" | custom-call | flops 500000000 | tf_op jit(solution)/shard_map/pallas_call | solution.py:31
  (37 shorter events, 4.2 us)
Async XLA Ops:
  0.7 1.1 %copy-start = (bf16[1,1280,256]{2,1,0:T(8,128)(2,1)S(1)}, bf16[1,1280,256]{2,1,0:T(8,128)(2,1)}, u32[]{:S(2)}) copy-start(bf16[1,1280,256]{2,1,0:T(8,128)(2,1)} %param.5) | copy-start | bytes 1966084
  1.8 1.1 %copy-start.2 = (bf16[1280,256]{1,0:T(8,128)(2,1)S(1)}, bf16[1280,256]{1,0:T(8,128)(2,1)}, u32[]{:S(2)}) copy-start(bf16[1280,256]{1,0:T(8,128)(2,1)} %param.6) | copy-start | bytes 1966084
  2.9 0.9 copy-start.3
  4.6 26.2 %collective-permute-start.5 = (bf16[304,256]{1,0:T(8,128)(2,1)S(1)}, bf16[304,256]{1,0:T(8,128)(2,1)S(1)}, u32[]{:S(2)}, u32[]{:S(2)}) collective-permute-start(bf16[304,256]{1,0:T(8,128)(2,1)S(1)} %get-tuple-element.43.a), channel_id=1, source_target_pairs={{0,8},{2,10},{4,12},{6,14},{8,0},{10,2},{12,4},{14,6},{1,9},{3,11}... | collective-permute-start | bytes 466952 | tf_op jit(solution)/shard_map/ppermute | solution.py:23
  20.4 13.0 %collective-permute-start = (bf16[320,256]{1,0:T(8,128)(2,1)S(1)}, bf16[320,256]{1,0:T(8,128)(2,1)S(1)}, u32[]{:S(2)}, u32[]{:S(2)}) collective-permute-start(bf16[320,256]{1,0:T(8,128)(2,1)S(1)} %get-tuple-element.36), channel_id=1, source_target_pairs={{0,16},{16,0},{32,48},{48,32},{64,80},{80,64},{96,112},{112,96},{1... | collective-permute-start | bytes 491528 | tf_op jit(solution)/shard_map/ppermute | solution.py:23
  23.0 10.3 %collective-permute-start.1 = (bf16[320,256]{1,0:T(8,128)(2,1)S(1)}, bf16[320,256]{1,0:T(8,128)(2,1)S(1)}, u32[]{:S(2)}, u32[]{:S(2)}) collective-permute-start(bf16[320,256]{1,0:T(8,128)(2,1)S(1)} %get-tuple-element.37), channel_id=1, source_target_pairs={{0,32},{16,48},{32,0},{48,16},{64,96},{80,112},{96,64},{112,80},{1... | collective-permute-start | bytes 491528 | tf_op jit(solution)/shard_map/ppermute | solution.py:23
  25.9 9.4 %collective-permute-start.2 = (bf16[320,256]{1,0:T(8,128)(2,1)S(1)}, bf16[320,256]{1,0:T(8,128)(2,1)S(1)}, u32[]{:S(2)}, u32[]{:S(2)}) collective-permute-start(bf16[320,256]{1,0:T(8,128)(2,1)S(1)} %get-tuple-element.38), channel_id=1, source_target_pairs={{0,48},{16,32},{32,16},{48,0},{64,112},{80,96},{96,80},{112,64},{1... | collective-permute-start | bytes 491528 | tf_op jit(solution)/shard_map/ppermute | solution.py:23
  31.4 22.4 %copy-start.4 = (f32[1,1,40,256]{3,2,1,0:T(8,128)S(1)}, f32[1,1,40,256]{3,2,1,0:T(8,128)}, u32[]{:S(2)}) copy-start(f32[1,1,40,256]{3,2,1,0:T(8,128)} %param.7) | copy-start | bytes 122884
  31.4 9.0 %collective-permute-start.6 = (bf16[304,256]{1,0:T(8,128)(2,1)S(1)}, bf16[304,256]{1,0:T(8,128)(2,1)S(1)}, u32[]{:S(2)}, u32[]{:S(2)}) collective-permute-start(bf16[304,256]{1,0:T(8,128)(2,1)S(1)} %get-tuple-element.46), channel_id=1, source_target_pairs={{0,1},{1,0},{2,3},{3,2},{4,5},{5,4},{6,7},{7,6},{8,9},{9,8},{10,11... | collective-permute-start | bytes 466952 | tf_op jit(solution)/shard_map/ppermute | solution.py:23
  36.1 26.6 %copy-start.1 = (bf16[1,1280,256]{2,1,0:T(8,128)(2,1)S(1)}, bf16[1,1280,256]{2,1,0:T(8,128)(2,1)}, u32[]{:S(2)}) copy-start(bf16[1,1280,256]{2,1,0:T(8,128)(2,1)} %param.5) | copy-start | bytes 1966084
  36.1 8.3 %collective-permute-start.3 = (bf16[160,256]{1,0:T(8,128)(2,1)S(1)}, bf16[160,256]{1,0:T(8,128)(2,1)S(1)}, u32[]{:S(2)}, u32[]{:S(2)}) collective-permute-start(bf16[160,256]{1,0:T(8,128)(2,1)S(1)} %get-tuple-element.40), channel_id=1, source_target_pairs={{0,64},{16,80},{32,96},{48,112},{64,0},{80,16},{96,32},{112,48},{1... | collective-permute-start | bytes 245768 | tf_op jit(solution)/shard_map/ppermute | solution.py:23
  41.0 6.1 %collective-permute-start.7 = (f32[8,128]{1,0:T(8,128)S(1)}, f32[8,128]{1,0:T(8,128)S(1)}, u32[]{:S(2)}, u32[]{:S(2)}) collective-permute-start(f32[8,128]{1,0:T(8,128)S(1)} %get-tuple-element.48), channel_id=1, source_target_pairs={{0,2},{2,0},{4,6},{6,4},{8,10},{10,8},{12,14},{14,12},{1,3},{3,1},... | collective-permute-start | bytes 12296 | tf_op jit(solution)/shard_map/ppermute | solution.py:23
  45.0 8.9 %collective-permute-start.4 = (bf16[80,256]{1,0:T(8,128)(2,1)S(1)}, bf16[80,256]{1,0:T(8,128)(2,1)S(1)}, u32[]{:S(2)}, u32[]{:S(2)}) collective-permute-start(bf16[80,256]{1,0:T(8,128)(2,1)S(1)} %get-tuple-element.42), channel_id=1, source_target_pairs={{0,128},{16,144},{32,160},{48,176},{64,192},{80,208},{96,224},{112... | collective-permute-start | bytes 122888 | tf_op jit(solution)/shard_map/ppermute | solution.py:23
  47.1 6.7 %collective-permute-start.8 = (f32[8,128]{1,0:T(8,128)S(1)}, f32[8,128]{1,0:T(8,128)S(1)}, u32[]{:S(2)}, u32[]{:S(2)}) collective-permute-start(f32[8,128]{1,0:T(8,128)S(1)} %max.3), channel_id=1, source_target_pairs={{0,6},{2,4},{4,2},{6,0},{8,14},{10,12},{12,10},{14,8},{1,7},{3,5},... | collective-permute-start | bytes 12296 | tf_op jit(solution)/shard_map/ppermute | solution.py:23
  54.4 12.4 %collective-permute-start.9 = (bf16[96,256]{1,0:T(8,128)(2,1)S(1)}, bf16[96,256]{1,0:T(8,128)(2,1)S(1)}, u32[]{:S(2)}, u32[]{:S(2)}) collective-permute-start(bf16[96,256]{1,0:T(8,128)(2,1)S(1)} %get-tuple-element.49.q), channel_id=1, source_target_pairs={{0,256},{16,272},{32,288},{48,304},{64,320},{80,336},{96,352},{112... | collective-permute-start | bytes 147464 | tf_op jit(solution)/shard_map/ppermute | solution.py:23
  62.7 33.8 %collective-permute-start.17 = (bf16[1280,256]{1,0:T(8,128)(2,1)S(1)}, bf16[1280,256]{1,0:T(8,128)(2,1)S(1)}, u32[]{:S(2)}, u32[]{:S(2)}) collective-permute-start(bf16[1280,256]{1,0:T(8,128)(2,1)S(1)} %bitcast.15), channel_id=1, source_target_pairs={{0,1},{1,0},{2,3},{3,2},{4,5},{5,4},{6,7},{7,6},{8,9},{9,8},{10,11... | collective-permute-start | bytes 1966088 | tf_op jit(solution)/shard_map/ppermute | solution.py:23
  64.6 16.2 %collective-permute-start.15 = (bf16[576,256]{1,0:T(8,128)(2,1)S(1)}, bf16[576,256]{1,0:T(8,128)(2,1)S(1)}, u32[]{:S(2)}, u32[]{:S(2)}) collective-permute-start(bf16[576,256]{1,0:T(8,128)(2,1)S(1)} %get-tuple-element.56.a), channel_id=1, source_target_pairs={{0,2},{2,0},{4,6},{6,4},{8,10},{10,8},{12,14},{14,12},{1,3},{3,1},... | collective-permute-start | bytes 884744 | tf_op jit(solution)/shard_map/ppermute | solution.py:23
  66.8 19.1 %copy-start.5 = (s32[8]{0:T(128)S(1)}, s32[8]{0:T(128)}, u32[]{:S(2)}) copy-start(s32[8]{0:T(128)} %constant.22.clone) | copy-start | bytes 100
  68.0 10.1 %collective-permute-start.10 = (bf16[96,256]{1,0:T(8,128)(2,1)S(1)}, bf16[96,256]{1,0:T(8,128)(2,1)S(1)}, u32[]{:S(2)}, u32[]{:S(2)}) collective-permute-start(bf16[96,256]{1,0:T(8,128)(2,1)S(1)} %get-tuple-element.52.f0), channel_id=1, source_target_pairs={{0,64},{16,80},{32,96},{48,112},{64,0},{80,16},{96,32},{112,48},{1... | collective-permute-start | bytes 147464 | tf_op jit(solution)/shard_map/ppermute | solution.py:23
  70.9 7.9 %collective-permute-start.11 = (bf16[96,256]{1,0:T(8,128)(2,1)S(1)}, bf16[96,256]{1,0:T(8,128)(2,1)S(1)}, u32[]{:S(2)}, u32[]{:S(2)}) collective-permute-start(bf16[96,256]{1,0:T(8,128)(2,1)S(1)} %get-tuple-element.52.f0), channel_id=1, source_target_pairs={{0,128},{16,144},{32,160},{48,176},{64,192},{80,208},{96,224},{112... | collective-permute-start | bytes 147464 | tf_op jit(solution)/shard_map/ppermute | solution.py:23
  73.0 7.8 %collective-permute-start.12 = (bf16[96,256]{1,0:T(8,128)(2,1)S(1)}, bf16[96,256]{1,0:T(8,128)(2,1)S(1)}, u32[]{:S(2)}, u32[]{:S(2)}) collective-permute-start(bf16[96,256]{1,0:T(8,128)(2,1)S(1)} %get-tuple-element.52.f0), channel_id=1, source_target_pairs={{0,192},{16,208},{32,224},{48,240},{64,128},{80,144},{96,160},{112... | collective-permute-start | bytes 147464 | tf_op jit(solution)/shard_map/ppermute | solution.py:23
  81.4 17.6 %collective-permute-start.16 = (bf16[1152,256]{1,0:T(8,128)(2,1)S(1)}, bf16[1152,256]{1,0:T(8,128)(2,1)S(1)}, u32[]{:S(2)}, u32[]{:S(2)}) collective-permute-start(bf16[1152,256]{1,0:T(8,128)(2,1)S(1)} %shard_map.92.a), channel_id=1, source_target_pairs={{0,6},{2,4},{4,2},{6,0},{8,14},{10,12},{12,10},{14,8},{1,7},{3,5},... | collective-permute-start | bytes 1769480 | tf_op jit(solution)/shard_map/ppermute | solution.py:23
  86.5 15.0 %collective-permute-start.14 = (bf16[336,256]{1,0:T(8,128)(2,1)S(1)}, bf16[336,256]{1,0:T(8,128)(2,1)S(1)}, u32[]{:S(2)}, u32[]{:S(2)}) collective-permute-start(bf16[336,256]{1,0:T(8,128)(2,1)S(1)} %get-tuple-element.54.e0), channel_id=1, source_target_pairs={{0,32},{16,48},{32,0},{48,16},{64,96},{80,112},{96,64},{112,80},{1... | collective-permute-start | bytes 516104 | tf_op jit(solution)/shard_map/ppermute | solution.py:23
  89.7 11.8 %collective-permute-start.13 = (bf16[336,256]{1,0:T(8,128)(2,1)S(1)}, bf16[336,256]{1,0:T(8,128)(2,1)S(1)}, u32[]{:S(2)}, u32[]{:S(2)}) collective-permute-start(bf16[336,256]{1,0:T(8,128)(2,1)S(1)} %get-tuple-element.54.e0), channel_id=1, source_target_pairs={{0,16},{16,0},{32,48},{48,32},{64,80},{80,64},{96,112},{112,96},{1... | collective-permute-start | bytes 516104 | tf_op jit(solution)/shard_map/ppermute | solution.py:23
  92.1 9.4 %collective-permute-start.18 = (bf16[336,256]{1,0:T(8,128)(2,1)S(1)}, bf16[336,256]{1,0:T(8,128)(2,1)S(1)}, u32[]{:S(2)}, u32[]{:S(2)}) collective-permute-start(bf16[336,256]{1,0:T(8,128)(2,1)S(1)} %get-tuple-element.54.e0), channel_id=1, source_target_pairs={{0,48},{16,32},{32,16},{48,0},{64,112},{80,96},{96,80},{112,64},{1... | collective-permute-start | bytes 516104 | tf_op jit(solution)/shard_map/ppermute | solution.py:23

commit v5 on v4

--- a/solution.py
+++ b/solution.py
@@ -137,7 +137,7 @@
         out[:, y ^ d] = e[0:n].astype(F32).reshape(8, ROWS, COLS).astype(BF16)
         if d > 0:
             m = jnp.maximum(m, untail(e, n))
-    scale[...] = jnp.broadcast_to(m, TOP) + EPSILON
+    scale[...] = m[:, 0:1] + EPSILON
 
 
 def pair_kernel(ix, a, b, mx, theirs, mine, mx2):
@@ -235,21 +235,21 @@
     both, ms = call(core_kernel, [bf(576), ((8, 128), F32)], (ix, kg_mine, kg_core, mx))
     ms = jnp.maximum(ms, swap(ms, "fsdp", 1))
     mr = swap(ms, "fsdp", 3)
+    kg_x = swap(tie(both, (h, ms)), "fsdp", 1)
     wide = [jnp.concatenate([m, m], axis=1) for m in (ms, mr)]
     q, p_own, mx = call(lo_kernel, [bf(96), fl(40), top], (ix, own2, mom, h, *wide), [fl(80)])
     g = swap(q, "replica", 16)
-    kg_x = swap(tie(both, q), "fsdp", 1)
-    fresh, mom_new, mx = call(hi_kernel, [bf(96), fl(40), top], (ix, q, p_own, mom, a_y, mx, g), [fl(80)], 6.0)
+    fresh, mom_new, mx = call(hi_kernel, [bf(96), fl(40), top], (ix, q, p_own, mom, a_y, mx, g), [fl(80)], 14.0)
     f3, f2, f1 = (swap(fresh, "replica", 4 * d) for d in (3, 2, 1))
-    quad = call(quad_kernel, [bf(1152)], (ix, both, tie(kg_x, (f1, f2, f3))))[0]
+    quad = call(quad_kernel, [bf(1152)], (ix, both, tie(kg_x, q)))[0]
     more = swap(quad, "fsdp", 3)
     place = jnp.array([0, 4, 1, 5, 3, 7, 2, 6], jnp.int32) ^ f
     prod = product(place[:4], quad, w, w_other)
-    eight, mx = call(eight_kernel, [bf(336), top], (ix, fresh, f1, f2, f3, mx), [fl(320)])
+    eight, mx = call(eight_kernel, [bf(336), top], (ix, fresh, f1, f2, tie(f3, prod), mx), [fl(320)])
     e2, e1, e3 = (swap(eight, "replica", d) for d in (2, 1, 3))
     prod = product(place[4:], tie(more, eight), w, w_other, prod)
-    new_weights, scale = call(out_kernel, [(four, BF16), top], (ix, eight, e1, tie(e2, prod), e3, mx))
-    return new_weights.reshape(anchor.shape), mom_new[None, None], prod[None], scale[0, :1]
+    new_weights, scale = call(out_kernel, [(four, BF16), ((1, 1), F32)], (ix, eight, e1, tie(e2, prod), e3, mx))
+    return new_weights.reshape(anchor.shape), mom_new[None, None], prod[None], scale.reshape(1)
 
 
 def solution(mesh):

time: 105 us -> 99.2 us (0.945)
  waiting for transfers between devices: 7.26 us -> 2.8 us
  Pallas kernels: 12.6 us -> 14.3 us
  local copies, waits for them, and re-layouts: 3.77 us -> 2.17 us
    ppermute x19, waiting for transfers between devices: 7.26 us -> 2.8 us  [swap(): return lax.ppermute(x, axis, [(i, i ^ bit) for i in range(n)])]
    pallas_call x2, Pallas kernels: 5.02 us -> 6.13 us  [product(): pl.pallas_call(product_kernel, in_specs=[SMEM, VMEM, VMEM, VMEM] + [pl.Bl...]
    unnamed x12 -> x8, local copies, waits for them, and re-layouts: 3.1 us -> 2.01 us
  transfers between devices with their start and end apart: 19 -> 19, of which waited for: 4 -> 2; matrix products, arithmetic and copies ran while one was open for 0% -> 0% of each run, Pallas kernels for 9% -> 12%
where the time goes in v5:
time: 99.2 us; the launch traced here: 98.3 us
  starting transfers between devices  78 us (79%)
  Pallas kernels  14.3 us (14%)
  waiting for transfers between devices  2.8 us (3%)
  local copies, waits for them, and re-layouts  2.17 us (2%)
  between operations  1.04 us (1%)
    ppermute x19, starting transfers between devices, swap(): return lax.ppermute(x, axis, [(i, i ^ bit) for i in range(n)])  78 us
    pallas_call x10, Pallas kernels, call(): pl.pallas_call(kernel, out_shape=[jax.ShapeDtypeStruct(s, d) for s, d in...  8.19 us
    pallas_call x2, Pallas kernels, product(): pl.pallas_call(product_kernel, in_specs=[SMEM, VMEM, VMEM, VMEM] + [pl.Bl...  6.13 us
    ppermute x19, waiting for transfers between devices, swap(): return lax.ppermute(x, axis, [(i, i ^ bit) for i in range(n)])  2.8 us
    unnamed x8, local copies, waits for them, and re-layouts  2.01 us
  transfers between devices with their start and end apart: 19, of which 2 were waited for; matrix products, arithmetic and copies ran while one was open for 0% of the time, Pallas kernels for 12%

profile of v5, /device:TPU:24, one launch (start us, length us, event | category | flops | bytes accessed | tf_op | source)
XLA Modules:
  0.0 98.3 jit_solution(13826213039495507537)
XLA Ops:
  0.7 1.1 %copy-done = bf16[1280,256]{1,0:T(8,128)(2,1)S(1)} copy-done((bf16[1280,256]{1,0:T(8,128)(2,1)S(1)}, bf16[1280,256]{1,0:T(8,128)(2,1)}, u32[]{:S(2)}) %copy-start) | copy-done | bytes 655384
  1.8 0.9 copy-done.1
  2.7 1.4 %shard_map.84 = (bf16[320,256]{1,0:T(8,128)(2,1)S(1)}, bf16[320,256]{1,0:T(8,128)(2,1)S(1)}, bf16[320,256]{1,0:T(8,128)(2,1)S(1)}, f32[320,256]{1,0:T(8,128)S(1)...) custom-call(s32[5]{0:T(128)S(1)} %stack.23.ix, bf16[8,4,40,256]{3,2,1,0:T(8,128)(2,1)} %bitcast.5.w, ...), custom_call_target="tpu_custom_call" | custom-call | flops 500000000 | tf_op jit(solution)/shard_map/pallas_call | solution.py:31
  4.1 15.7 %collective-permute-start.5 = (bf16[304,256]{1,0:T(8,128)(2,1)S(1)}, bf16[304,256]{1,0:T(8,128)(2,1)S(1)}, u32[]{:S(2)}, u32[]{:S(2)}) collective-permute-start(bf16[304,256]{1,0:T(8,128)(2,1)S(1)} %get-tuple-element.44.a), channel_id=1, source_target_pairs={{0,8},{2,10},{4,12},{6,14},{8,0},{10,2},{12,4},{14,6},{1,9},{3,11}... | collective-permute-start | bytes 466952 | tf_op jit(solution)/shard_map/ppermute | solution.py:23
  19.9 2.7 %collective-permute-start = (bf16[320,256]{1,0:T(8,128)(2,1)S(1)}, bf16[320,256]{1,0:T(8,128)(2,1)S(1)}, u32[]{:S(2)}, u32[]{:S(2)}) collective-permute-start(bf16[320,256]{1,0:T(8,128)(2,1)S(1)} %get-tuple-element.37), channel_id=1, source_target_pairs={{0,16},{16,0},{32,48},{48,32},{64,80},{80,64},{96,112},{112,96},{1... | collective-permute-start | bytes 491528 | tf_op jit(solution)/shard_map/ppermute | solution.py:23
  22.5 2.8 %collective-permute-start.1 = (bf16[320,256]{1,0:T(8,128)(2,1)S(1)}, bf16[320,256]{1,0:T(8,128)(2,1)S(1)}, u32[]{:S(2)}, u32[]{:S(2)}) collective-permute-start(bf16[320,256]{1,0:T(8,128)(2,1)S(1)} %get-tuple-element.38), channel_id=1, source_target_pairs={{0,32},{16,48},{32,0},{48,16},{64,96},{80,112},{96,64},{112,80},{1... | collective-permute-start | bytes 491528 | tf_op jit(solution)/shard_map/ppermute | solution.py:23
  25.4 4.9 %collective-permute-start.2 = (bf16[320,256]{1,0:T(8,128)(2,1)S(1)}, bf16[320,256]{1,0:T(8,128)(2,1)S(1)}, u32[]{:S(2)}, u32[]{:S(2)}) collective-permute-start(bf16[320,256]{1,0:T(8,128)(2,1)S(1)} %get-tuple-element.39), channel_id=1, source_target_pairs={{0,48},{16,32},{32,16},{48,0},{64,112},{80,96},{96,80},{112,64},{1... | collective-permute-start | bytes 491528 | tf_op jit(solution)/shard_map/ppermute | solution.py:23
  30.3 1.9 %collective-permute-start.14 = (bf16[1280,256]{1,0:T(8,128)(2,1)}, bf16[1280,256]{1,0:T(8,128)(2,1)S(1)}, u32[]{:S(2)}, u32[]{:S(2)}) collective-permute-start(bf16[1280,256]{1,0:T(8,128)(2,1)} %bitcast.9.wa), channel_id=1, source_target_pairs={{0,1},{1,0},{2,3},{3,2},{4,5},{5,4},{6,7},{7,6},{8,9},{9,8},{10,11... | collective-permute-start | bytes 1966088 | tf_op jit(solution)/shard_map/ppermute | solution.py:23
  32.2 0.6 shard_map.87
  32.8 2.4 %collective-permute-start.6 = (bf16[304,256]{1,0:T(8,128)(2,1)S(1)}, bf16[304,256]{1,0:T(8,128)(2,1)S(1)}, u32[]{:S(2)}, u32[]{:S(2)}) collective-permute-start(bf16[304,256]{1,0:T(8,128)(2,1)S(1)} %get-tuple-element.47), channel_id=1, source_target_pairs={{0,1},{1,0},{2,3},{3,2},{4,5},{5,4},{6,7},{7,6},{8,9},{9,8},{10,11... | collective-permute-start | bytes 466952 | tf_op jit(solution)/shard_map/ppermute | solution.py:23
  35.3 0.8 shard_map.85
  36.0 3.7 %collective-permute-start.3 = (bf16[160,256]{1,0:T(8,128)(2,1)S(1)}, bf16[160,256]{1,0:T(8,128)(2,1)S(1)}, u32[]{:S(2)}, u32[]{:S(2)}) collective-permute-start(bf16[160,256]{1,0:T(8,128)(2,1)S(1)} %get-tuple-element.41), channel_id=1, source_target_pairs={{0,64},{16,80},{32,96},{48,112},{64,0},{80,16},{96,32},{112,48},{1... | collective-permute-start | bytes 245768 | tf_op jit(solution)/shard_map/ppermute | solution.py:23
  40.4 3.4 %collective-permute-start.7 = (f32[8,128]{1,0:T(8,128)S(1)}, f32[8,128]{1,0:T(8,128)S(1)}, u32[]{:S(2)}, u32[]{:S(2)}) collective-permute-start(f32[8,128]{1,0:T(8,128)S(1)} %get-tuple-element.49), channel_id=1, source_target_pairs={{0,2},{2,0},{4,6},{6,4},{8,10},{10,8},{12,14},{14,12},{1,3},{3,1},... | collective-permute-start | bytes 12296 | tf_op jit(solution)/shard_map/ppermute | solution.py:23
  44.3 2.6 %collective-permute-start.4 = (bf16[80,256]{1,0:T(8,128)(2,1)S(1)}, bf16[80,256]{1,0:T(8,128)(2,1)S(1)}, u32[]{:S(2)}, u32[]{:S(2)}) collective-permute-start(bf16[80,256]{1,0:T(8,128)(2,1)S(1)} %get-tuple-element.43), channel_id=1, source_target_pairs={{0,128},{16,144},{32,160},{48,176},{64,192},{80,208},{96,224},{112... | collective-permute-start | bytes 122888 | tf_op jit(solution)/shard_map/ppermute | solution.py:23
  47.0 4.0 %collective-permute-start.8 = (f32[8,128]{1,0:T(8,128)S(1)}, f32[8,128]{1,0:T(8,128)S(1)}, u32[]{:S(2)}, u32[]{:S(2)}) collective-permute-start(f32[8,128]{1,0:T(8,128)S(1)} %max.3), channel_id=1, source_target_pairs={{0,6},{2,4},{4,2},{6,0},{8,14},{10,12},{12,10},{14,8},{1,7},{3,5},... | collective-permute-start | bytes 12296 | tf_op jit(solution)/shard_map/ppermute | solution.py:23
  51.6 2.4 %collective-permute-start.13 = (bf16[576,256]{1,0:T(8,128)(2,1)S(1)}, bf16[576,256]{1,0:T(8,128)(2,1)S(1)}, u32[]{:S(2)}, u32[]{:S(2)}) collective-permute-start(bf16[576,256]{1,0:T(8,128)(2,1)S(1)} %get-tuple-element.55.a), channel_id=1, source_target_pairs={{0,2},{2,0},{4,6},{6,4},{8,10},{10,8},{12,14},{14,12},{1,3},{3,1},... | collective-permute-start | bytes 884744 | tf_op jit(solution)/shard_map/ppermute | solution.py:23
  54.0 0.6 shard_map.89
  54.6 7.6 %collective-permute-start.9 = (bf16[96,256]{1,0:T(8,128)(2,1)S(1)}, bf16[96,256]{1,0:T(8,128)(2,1)S(1)}, u32[]{:S(2)}, u32[]{:S(2)}) collective-permute-start(bf16[96,256]{1,0:T(8,128)(2,1)S(1)} %get-tuple-element.50.q), channel_id=1, source_target_pairs={{0,256},{16,272},{32,288},{48,304},{64,320},{80,336},{96,352},{112... | collective-permute-start | bytes 147464 | tf_op jit(solution)/shard_map/ppermute | solution.py:23
  62.2 0.6 shard_map.91.a
  62.8 4.5 %collective-permute-start.17 = (bf16[1152,256]{1,0:T(8,128)(2,1)S(1)}, bf16[1152,256]{1,0:T(8,128)(2,1)S(1)}, u32[]{:S(2)}, u32[]{:S(2)}) collective-permute-start(bf16[1152,256]{1,0:T(8,128)(2,1)S(1)} %shard_map.91.a), channel_id=1, source_target_pairs={{0,6},{2,4},{4,2},{6,0},{8,14},{10,12},{12,10},{14,8},{1,7},{3,5},... | collective-permute-start | bytes 1769480 | tf_op jit(solution)/shard_map/ppermute | solution.py:23
  67.4 1.2 %shard_map.90 = (bf16[96,256]{1,0:T(8,128)(2,1)S(1)}, f32[40,256]{1,0:T(8,128)}, f32[8,256]{1,0:T(8,128)S(1)}) custom-call(s32[5]{0:T(128)S(1)} %stack.23.ix, bf16[96,256]{1,0:T(8,128)(2,1)S(1)} %get-tuple-element.50.q, f32[40,256]{1,0:T(8,128)S(1)} %get-tuple-element.51.p_own, f32[40,256]{1,0:T(8,128)S(1)} %bitcast.17, ...), custom_call_target="tpu_custom_call" | custom-call | flops 14000000000 | tf_op jit(solution)/shard_map/pallas_call | solution.py:31
  68.5 3.2 %collective-permute-start.12 = (bf16[96,256]{1,0:T(8,128)(2,1)S(1)}, bf16[96,256]{1,0:T(8,128)(2,1)S(1)}, u32[]{:S(2)}, u32[]{:S(2)}) collective-permute-start(bf16[96,256]{1,0:T(8,128)(2,1)S(1)} %get-tuple-element.53.f0), channel_id=1, source_target_pairs={{0,192},{16,208},{32,224},{48,240},{64,128},{80,144},{96,160},{112... | collective-permute-start | bytes 147464 | tf_op jit(solution)/shard_map/ppermute | solution.py:23
  71.7 2.7 %collective-permute-start.11 = (bf16[96,256]{1,0:T(8,128)(2,1)S(1)}, bf16[96,256]{1,0:T(8,128)(2,1)S(1)}, u32[]{:S(2)}, u32[]{:S(2)}) collective-permute-start(bf16[96,256]{1,0:T(8,128)(2,1)S(1)} %get-tuple-element.53.f0), channel_id=1, source_target_pairs={{0,128},{16,144},{32,160},{48,176},{64,192},{80,208},{96,224},{112... | collective-permute-start | bytes 147464 | tf_op jit(solution)/shard_map/ppermute | solution.py:23
  74.4 4.3 %collective-permute-start.10 = (bf16[96,256]{1,0:T(8,128)(2,1)S(1)}, bf16[96,256]{1,0:T(8,128)(2,1)S(1)}, u32[]{:S(2)}, u32[]{:S(2)}) collective-permute-start(bf16[96,256]{1,0:T(8,128)(2,1)S(1)} %get-tuple-element.53.f0), channel_id=1, source_target_pairs={{0,64},{16,80},{32,96},{48,112},{64,0},{80,16},{96,32},{112,48},{1... | collective-permute-start | bytes 147464 | tf_op jit(solution)/shard_map/ppermute | solution.py:23
  78.7 3.1 %shard_map.92.rest_0_ = bf16[8,144,1280]{2,1,0:T(8,128)(2,1)} custom-call(s32[4]{0:T(128)S(1)} %get-tuple-element.67.place, bf16[1152,256]{1,0:T(8,128)(2,1)S(1)} %shard_map.91.a, bf16[1280,256]{1,0:T(8,128)(2,1)} %bitcast.9.wa, bf16[1280,256]{1,0:T(8,128)(2,1)S(1)} %collective-permute-done.14.wb), custom_call_target="tpu_custom_call" | custom-call | flops 754974720 | bytes 3500000 | tf_op jit(solution)/shard_map/pallas_call | solution.py:190
  81.8 0.6 shard_map.93
  82.4 3.1 %collective-permute-start.16 = (bf16[336,256]{1,0:T(8,128)(2,1)S(1)}, bf16[336,256]{1,0:T(8,128)(2,1)S(1)}, u32[]{:S(2)}, u32[]{:S(2)}) collective-permute-start(bf16[336,256]{1,0:T(8,128)(2,1)S(1)} %get-tuple-element.59.e0), channel_id=1, source_target_pairs={{0,32},{16,48},{32,0},{48,16},{64,96},{80,112},{96,64},{112,80},{1... | collective-permute-start | bytes 516104 | tf_op jit(solution)/shard_map/ppermute | solution.py:23
  85.5 4.1 %collective-permute-start.18 = (bf16[336,256]{1,0:T(8,128)(2,1)S(1)}, bf16[336,256]{1,0:T(8,128)(2,1)S(1)}, u32[]{:S(2)}, u32[]{:S(2)}) collective-permute-start(bf16[336,256]{1,0:T(8,128)(2,1)S(1)} %get-tuple-element.59.e0), channel_id=1, source_target_pairs={{0,48},{16,32},{32,16},{48,0},{64,112},{80,96},{96,80},{112,64},{1... | collective-permute-start | bytes 516104 | tf_op jit(solution)/shard_map/ppermute | solution.py:23
  89.6 2.0 %collective-permute-start.15 = (bf16[336,256]{1,0:T(8,128)(2,1)S(1)}, bf16[336,256]{1,0:T(8,128)(2,1)S(1)}, u32[]{:S(2)}, u32[]{:S(2)}) collective-permute-start(bf16[336,256]{1,0:T(8,128)(2,1)S(1)} %get-tuple-element.59.e0), channel_id=1, source_target_pairs={{0,16},{16,0},{32,48},{48,32},{64,80},{80,64},{96,112},{112,96},{1... | collective-permute-start | bytes 516104 | tf_op jit(solution)/shard_map/ppermute | solution.py:23
  91.6 3.1 %shard_map.94 = bf16[8,144,1280]{2,1,0:T(8,128)(2,1)} custom-call(s32[4]{0:T(128)S(1)} %get-tuple-element.66.place, bf16[1152,256]{1,0:T(8,128)(2,1)S(1)} %collective-permute-done.17.a, bf16[1280,256]{1,0:T(8,128)(2,1)} %bitcast.9.wa, bf16[1280,256]{1,0:T(8,128)(2,1)S(1)} %collective-permute-done.14.wb, ...), custom_call_target="tpu_custom_call", output_to_operand_aliasing={{}: (4, {})} | custom-call | flops 754974720 | bytes 3500000 | tf_op jit(solution)/shard_map/pallas_call | solution.py:190
  94.7 2.2 %collective-permute-done.15.e1 = bf16[336,256]{1,0:T(8,128)(2,1)S(1)} collective-permute-done((bf16[336,256]{1,0:T(8,128)(2,1)S(1)}, bf16[336,256]{1,0:T(8,128)(2,1)S(1)}, u32[]{:S(2)}, u32[]{:S(2)}) %collective-permute-start.15) | collective-permute-done | bytes 172064 | tf_op jit(solution)/shard_map/ppermute | solution.py:23
  96.9 1.4 %shard_map.95 = (bf16[8,4,40,256]{3,2,1,0:T(8,128)(2,1)}, f32[1,1]{1,0:T(1,128)}) custom-call(s32[5]{0:T(128)S(1)} %stack.23.ix, bf16[336,256]{1,0:T(8,128)(2,1)S(1)} %get-tuple-element.59.e0, bf16[336,256]{1,0:T(8,128)(2,1)S(1)} %collective-permute-done.15.e1, bf16[336,256]{1,0:T(8,128)(2,1)S(1)} %collective-permute-done.16.e2, ...), custom_call_target="tpu_custom_call" | custom-call | flops 500000000 | tf_op jit(solution)/shard_map/pallas_call | solution.py:31
  (32 shorter events, 1.9 us)
Async XLA Ops:
  0.6 39.1 %copy-start.3 = (s32[8]{0:T(128)S(1)}, s32[8]{0:T(128)}, u32[]{:S(2)}) copy-start(s32[8]{0:T(128)} %constant.22.clone) | copy-start | bytes 100
  0.7 1.1 %copy-start = (bf16[1280,256]{1,0:T(8,128)(2,1)S(1)}, bf16[1280,256]{1,0:T(8,128)(2,1)}, u32[]{:S(2)}) copy-start(bf16[1280,256]{1,0:T(8,128)(2,1)} %param.6) | copy-start | bytes 1966084
  1.8 0.9 copy-start.1
  4.1 28.1 %collective-permute-start.5 = (bf16[304,256]{1,0:T(8,128)(2,1)S(1)}, bf16[304,256]{1,0:T(8,128)(2,1)S(1)}, u32[]{:S(2)}, u32[]{:S(2)}) collective-permute-start(bf16[304,256]{1,0:T(8,128)(2,1)S(1)} %get-tuple-element.44.a), channel_id=1, source_target_pairs={{0,8},{2,10},{4,12},{6,14},{8,0},{10,2},{12,4},{14,6},{1,9},{3,11}... | collective-permute-start | bytes 466952 | tf_op jit(solution)/shard_map/ppermute | solution.py:23
  19.9 15.4 %collective-permute-start = (bf16[320,256]{1,0:T(8,128)(2,1)S(1)}, bf16[320,256]{1,0:T(8,128)(2,1)S(1)}, u32[]{:S(2)}, u32[]{:S(2)}) collective-permute-start(bf16[320,256]{1,0:T(8,128)(2,1)S(1)} %get-tuple-element.37), channel_id=1, source_target_pairs={{0,16},{16,0},{32,48},{48,32},{64,80},{80,64},{96,112},{112,96},{1... | collective-permute-start | bytes 491528 | tf_op jit(solution)/shard_map/ppermute | solution.py:23
  22.5 12.7 %collective-permute-start.1 = (bf16[320,256]{1,0:T(8,128)(2,1)S(1)}, bf16[320,256]{1,0:T(8,128)(2,1)S(1)}, u32[]{:S(2)}, u32[]{:S(2)}) collective-permute-start(bf16[320,256]{1,0:T(8,128)(2,1)S(1)} %get-tuple-element.38), channel_id=1, source_target_pairs={{0,32},{16,48},{32,0},{48,16},{64,96},{80,112},{96,64},{112,80},{1... | collective-permute-start | bytes 491528 | tf_op jit(solution)/shard_map/ppermute | solution.py:23
  25.4 9.9 %collective-permute-start.2 = (bf16[320,256]{1,0:T(8,128)(2,1)S(1)}, bf16[320,256]{1,0:T(8,128)(2,1)S(1)}, u32[]{:S(2)}, u32[]{:S(2)}) collective-permute-start(bf16[320,256]{1,0:T(8,128)(2,1)S(1)} %get-tuple-element.39), channel_id=1, source_target_pairs={{0,48},{16,32},{32,16},{48,0},{64,112},{80,96},{96,80},{112,64},{1... | collective-permute-start | bytes 491528 | tf_op jit(solution)/shard_map/ppermute | solution.py:23
  30.3 48.4 %collective-permute-start.14 = (bf16[1280,256]{1,0:T(8,128)(2,1)}, bf16[1280,256]{1,0:T(8,128)(2,1)S(1)}, u32[]{:S(2)}, u32[]{:S(2)}) collective-permute-start(bf16[1280,256]{1,0:T(8,128)(2,1)} %bitcast.9.wa), channel_id=1, source_target_pairs={{0,1},{1,0},{2,3},{3,2},{4,5},{5,4},{6,7},{7,6},{8,9},{9,8},{10,11... | collective-permute-start | bytes 1966088 | tf_op jit(solution)/shard_map/ppermute | solution.py:23
  32.8 21.2 %copy-start.2 = (f32[1,1,40,256]{3,2,1,0:T(8,128)S(1)}, f32[1,1,40,256]{3,2,1,0:T(8,128)}, u32[]{:S(2)}) copy-start(f32[1,1,40,256]{3,2,1,0:T(8,128)} %param.7) | copy-start | bytes 122884
  32.8 6.9 %collective-permute-start.6 = (bf16[304,256]{1,0:T(8,128)(2,1)S(1)}, bf16[304,256]{1,0:T(8,128)(2,1)S(1)}, u32[]{:S(2)}, u32[]{:S(2)}) collective-permute-start(bf16[304,256]{1,0:T(8,128)(2,1)S(1)} %get-tuple-element.47), channel_id=1, source_target_pairs={{0,1},{1,0},{2,3},{3,2},{4,5},{5,4},{6,7},{7,6},{8,9},{9,8},{10,11... | collective-permute-start | bytes 466952 | tf_op jit(solution)/shard_map/ppermute | solution.py:23
  36.0 7.7 %collective-permute-start.3 = (bf16[160,256]{1,0:T(8,128)(2,1)S(1)}, bf16[160,256]{1,0:T(8,128)(2,1)S(1)}, u32[]{:S(2)}, u32[]{:S(2)}) collective-permute-start(bf16[160,256]{1,0:T(8,128)(2,1)S(1)} %get-tuple-element.41), channel_id=1, source_target_pairs={{0,64},{16,80},{32,96},{48,112},{64,0},{80,16},{96,32},{112,48},{1... | collective-permute-start | bytes 245768 | tf_op jit(solution)/shard_map/ppermute | solution.py:23
  40.4 6.6 %collective-permute-start.7 = (f32[8,128]{1,0:T(8,128)S(1)}, f32[8,128]{1,0:T(8,128)S(1)}, u32[]{:S(2)}, u32[]{:S(2)}) collective-permute-start(f32[8,128]{1,0:T(8,128)S(1)} %get-tuple-element.49), channel_id=1, source_target_pairs={{0,2},{2,0},{4,6},{6,4},{8,10},{10,8},{12,14},{14,12},{1,3},{3,1},... | collective-permute-start | bytes 12296 | tf_op jit(solution)/shard_map/ppermute | solution.py:23
  44.3 7.2 %collective-permute-start.4 = (bf16[80,256]{1,0:T(8,128)(2,1)S(1)}, bf16[80,256]{1,0:T(8,128)(2,1)S(1)}, u32[]{:S(2)}, u32[]{:S(2)}) collective-permute-start(bf16[80,256]{1,0:T(8,128)(2,1)S(1)} %get-tuple-element.43), channel_id=1, source_target_pairs={{0,128},{16,144},{32,160},{48,176},{64,192},{80,208},{96,224},{112... | collective-permute-start | bytes 122888 | tf_op jit(solution)/shard_map/ppermute | solution.py:23
  47.0 7.0 %collective-permute-start.8 = (f32[8,128]{1,0:T(8,128)S(1)}, f32[8,128]{1,0:T(8,128)S(1)}, u32[]{:S(2)}, u32[]{:S(2)}) collective-permute-start(f32[8,128]{1,0:T(8,128)S(1)} %max.3), channel_id=1, source_target_pairs={{0,6},{2,4},{4,2},{6,0},{8,14},{10,12},{12,10},{14,8},{1,7},{3,5},... | collective-permute-start | bytes 12296 | tf_op jit(solution)/shard_map/ppermute | solution.py:23
  51.6 10.7 %collective-permute-start.13 = (bf16[576,256]{1,0:T(8,128)(2,1)S(1)}, bf16[576,256]{1,0:T(8,128)(2,1)S(1)}, u32[]{:S(2)}, u32[]{:S(2)}) collective-permute-start(bf16[576,256]{1,0:T(8,128)(2,1)S(1)} %get-tuple-element.55.a), channel_id=1, source_target_pairs={{0,2},{2,0},{4,6},{6,4},{8,10},{10,8},{12,14},{14,12},{1,3},{3,1},... | collective-permute-start | bytes 884744 | tf_op jit(solution)/shard_map/ppermute | solution.py:23
  54.6 12.8 %collective-permute-start.9 = (bf16[96,256]{1,0:T(8,128)(2,1)S(1)}, bf16[96,256]{1,0:T(8,128)(2,1)S(1)}, u32[]{:S(2)}, u32[]{:S(2)}) collective-permute-start(bf16[96,256]{1,0:T(8,128)(2,1)S(1)} %get-tuple-element.50.q), channel_id=1, source_target_pairs={{0,256},{16,272},{32,288},{48,304},{64,320},{80,336},{96,352},{112... | collective-permute-start | bytes 147464 | tf_op jit(solution)/shard_map/ppermute | solution.py:23
  62.8 28.8 %collective-permute-start.17 = (bf16[1152,256]{1,0:T(8,128)(2,1)S(1)}, bf16[1152,256]{1,0:T(8,128)(2,1)S(1)}, u32[]{:S(2)}, u32[]{:S(2)}) collective-permute-start(bf16[1152,256]{1,0:T(8,128)(2,1)S(1)} %shard_map.91.a), channel_id=1, source_target_pairs={{0,6},{2,4},{4,2},{6,0},{8,14},{10,12},{12,10},{14,8},{1,7},{3,5},... | collective-permute-start | bytes 1769480 | tf_op jit(solution)/shard_map/ppermute | solution.py:23
  68.5 13.2 %collective-permute-start.12 = (bf16[96,256]{1,0:T(8,128)(2,1)S(1)}, bf16[96,256]{1,0:T(8,128)(2,1)S(1)}, u32[]{:S(2)}, u32[]{:S(2)}) collective-permute-start(bf16[96,256]{1,0:T(8,128)(2,1)S(1)} %get-tuple-element.53.f0), channel_id=1, source_target_pairs={{0,192},{16,208},{32,224},{48,240},{64,128},{80,144},{96,160},{112... | collective-permute-start | bytes 147464 | tf_op jit(solution)/shard_map/ppermute | solution.py:23
  71.7 10.0 %collective-permute-start.11 = (bf16[96,256]{1,0:T(8,128)(2,1)S(1)}, bf16[96,256]{1,0:T(8,128)(2,1)S(1)}, u32[]{:S(2)}, u32[]{:S(2)}) collective-permute-start(bf16[96,256]{1,0:T(8,128)(2,1)S(1)} %get-tuple-element.53.f0), channel_id=1, source_target_pairs={{0,128},{16,144},{32,160},{48,176},{64,192},{80,208},{96,224},{112... | collective-permute-start | bytes 147464 | tf_op jit(solution)/shard_map/ppermute | solution.py:23
  74.4 7.4 %collective-permute-start.10 = (bf16[96,256]{1,0:T(8,128)(2,1)S(1)}, bf16[96,256]{1,0:T(8,128)(2,1)S(1)}, u32[]{:S(2)}, u32[]{:S(2)}) collective-permute-start(bf16[96,256]{1,0:T(8,128)(2,1)S(1)} %get-tuple-element.53.f0), channel_id=1, source_target_pairs={{0,64},{16,80},{32,96},{48,112},{64,0},{80,16},{96,32},{112,48},{1... | collective-permute-start | bytes 147464 | tf_op jit(solution)/shard_map/ppermute | solution.py:23
  82.4 12.3 %collective-permute-start.16 = (bf16[336,256]{1,0:T(8,128)(2,1)S(1)}, bf16[336,256]{1,0:T(8,128)(2,1)S(1)}, u32[]{:S(2)}, u32[]{:S(2)}) collective-permute-start(bf16[336,256]{1,0:T(8,128)(2,1)S(1)} %get-tuple-element.59.e0), channel_id=1, source_target_pairs={{0,32},{16,48},{32,0},{48,16},{64,96},{80,112},{96,64},{112,80},{1... | collective-permute-start | bytes 516104 | tf_op jit(solution)/shard_map/ppermute | solution.py:23
  85.5 9.2 %collective-permute-start.18 = (bf16[336,256]{1,0:T(8,128)(2,1)S(1)}, bf16[336,256]{1,0:T(8,128)(2,1)S(1)}, u32[]{:S(2)}, u32[]{:S(2)}) collective-permute-start(bf16[336,256]{1,0:T(8,128)(2,1)S(1)} %get-tuple-element.59.e0), channel_id=1, source_target_pairs={{0,48},{16,32},{32,16},{48,0},{64,112},{80,96},{96,80},{112,64},{1... | collective-permute-start | bytes 516104 | tf_op jit(solution)/shard_map/ppermute | solution.py:23
  89.6 7.3 %collective-permute-start.15 = (bf16[336,256]{1,0:T(8,128)(2,1)S(1)}, bf16[336,256]{1,0:T(8,128)(2,1)S(1)}, u32[]{:S(2)}, u32[]{:S(2)}) collective-permute-start(bf16[336,256]{1,0:T(8,128)(2,1)S(1)} %get-tuple-element.59.e0), channel_id=1, source_target_pairs={{0,16},{16,0},{32,48},{48,32},{64,80},{80,64},{96,112},{112,96},{1... | collective-permute-start | bytes 516104 | tf_op jit(solution)/shard_map/ppermute | solution.py:23

commit v6 on v5

--- a/solution.py
+++ b/solution.py
@@ -248,7 +248,7 @@
     eight, mx = call(eight_kernel, [bf(336), top], (ix, fresh, f1, f2, tie(f3, prod), mx), [fl(320)])
     e2, e1, e3 = (swap(eight, "replica", d) for d in (2, 1, 3))
     prod = product(place[4:], tie(more, eight), w, w_other, prod)
-    new_weights, scale = call(out_kernel, [(four, BF16), ((1, 1), F32)], (ix, eight, e1, tie(e2, prod), e3, mx))
+    new_weights, scale = call(out_kernel, [(four, BF16), ((1, 1), F32)], (ix, eight, e1, e2, tie(e3, prod), mx))
     return new_weights.reshape(anchor.shape), mom_new[None, None], prod[None], scale.reshape(1)
 
 

time: 99.2 us -> 99.1 us (level)
  waiting for transfers between devices: 2.8 us -> 1.58 us
    ppermute x19, waiting for transfers between devices: 2.8 us -> 1.58 us  [swap(): return lax.ppermute(x, axis, [(i, i ^ bit) for i in range(n)])]
where the time goes in v6:
time: 99.1 us; the launch traced here: 97.7 us
  starting transfers between devices  78.6 us (79%)
  Pallas kernels  14.3 us (14%)
  local copies, waits for them, and re-layouts  2.17 us (2%)
  waiting for transfers between devices  1.58 us (2%)
  between operations  1.04 us (1%)
    ppermute x19, starting transfers between devices, swap(): return lax.ppermute(x, axis, [(i, i ^ bit) for i in range(n)])  78.6 us
    pallas_call x10, Pallas kernels, call(): pl.pallas_call(kernel, out_shape=[jax.ShapeDtypeStruct(s, d) for s, d in...  8.19 us
    pallas_call x2, Pallas kernels, product(): pl.pallas_call(product_kernel, in_specs=[SMEM, VMEM, VMEM, VMEM] + [pl.Bl...  6.13 us
    unnamed x8, local copies, waits for them, and re-layouts  2.01 us
  transfers between devices with their start and end apart: 19, of which 2 were waited for; matrix products, arithmetic and copies ran while one was open for 0% of the time, Pallas kernels for 12%

profile of v6, /device:TPU:24, one launch (start us, length us, event | category | flops | bytes accessed | tf_op | source)
XLA Modules:
  0.0 97.7 jit_solution(9756997789808194151)
XLA Ops:
  0.7 1.1 %copy-done = bf16[1280,256]{1,0:T(8,128)(2,1)S(1)} copy-done((bf16[1280,256]{1,0:T(8,128)(2,1)S(1)}, bf16[1280,256]{1,0:T(8,128)(2,1)}, u32[]{:S(2)}) %copy-start) | copy-done | bytes 655384
  1.8 0.9 copy-done.1
  2.7 1.4 %shard_map.84 = (bf16[320,256]{1,0:T(8,128)(2,1)S(1)}, bf16[320,256]{1,0:T(8,128)(2,1)S(1)}, bf16[320,256]{1,0:T(8,128)(2,1)S(1)}, f32[320,256]{1,0:T(8,128)S(1)...) custom-call(s32[5]{0:T(128)S(1)} %stack.23.ix, bf16[8,4,40,256]{3,2,1,0:T(8,128)(2,1)} %bitcast.5.w, ...), custom_call_target="tpu_custom_call" | custom-call | flops 500000000 | tf_op jit(solution)/shard_map/pallas_call | solution.py:31
  4.1 15.7 %collective-permute-start.5 = (bf16[304,256]{1,0:T(8,128)(2,1)S(1)}, bf16[304,256]{1,0:T(8,128)(2,1)S(1)}, u32[]{:S(2)}, u32[]{:S(2)}) collective-permute-start(bf16[304,256]{1,0:T(8,128)(2,1)S(1)} %get-tuple-element.44.a), channel_id=1, source_target_pairs={{0,8},{2,10},{4,12},{6,14},{8,0},{10,2},{12,4},{14,6},{1,9},{3,11}... | collective-permute-start | bytes 466952 | tf_op jit(solution)/shard_map/ppermute | solution.py:23
  19.9 2.7 %collective-permute-start = (bf16[320,256]{1,0:T(8,128)(2,1)S(1)}, bf16[320,256]{1,0:T(8,128)(2,1)S(1)}, u32[]{:S(2)}, u32[]{:S(2)}) collective-permute-start(bf16[320,256]{1,0:T(8,128)(2,1)S(1)} %get-tuple-element.37), channel_id=1, source_target_pairs={{0,16},{16,0},{32,48},{48,32},{64,80},{80,64},{96,112},{112,96},{1... | collective-permute-start | bytes 491528 | tf_op jit(solution)/shard_map/ppermute | solution.py:23
  22.5 2.8 %collective-permute-start.1 = (bf16[320,256]{1,0:T(8,128)(2,1)S(1)}, bf16[320,256]{1,0:T(8,128)(2,1)S(1)}, u32[]{:S(2)}, u32[]{:S(2)}) collective-permute-start(bf16[320,256]{1,0:T(8,128)(2,1)S(1)} %get-tuple-element.38), channel_id=1, source_target_pairs={{0,32},{16,48},{32,0},{48,16},{64,96},{80,112},{96,64},{112,80},{1... | collective-permute-start | bytes 491528 | tf_op jit(solution)/shard_map/ppermute | solution.py:23
  25.4 4.9 %collective-permute-start.2 = (bf16[320,256]{1,0:T(8,128)(2,1)S(1)}, bf16[320,256]{1,0:T(8,128)(2,1)S(1)}, u32[]{:S(2)}, u32[]{:S(2)}) collective-permute-start(bf16[320,256]{1,0:T(8,128)(2,1)S(1)} %get-tuple-element.39), channel_id=1, source_target_pairs={{0,48},{16,32},{32,16},{48,0},{64,112},{80,96},{96,80},{112,64},{1... | collective-permute-start | bytes 491528 | tf_op jit(solution)/shard_map/ppermute | solution.py:23
  30.3 1.9 %collective-permute-start.14 = (bf16[1280,256]{1,0:T(8,128)(2,1)}, bf16[1280,256]{1,0:T(8,128)(2,1)S(1)}, u32[]{:S(2)}, u32[]{:S(2)}) collective-permute-start(bf16[1280,256]{1,0:T(8,128)(2,1)} %bitcast.9.wa), channel_id=1, source_target_pairs={{0,1},{1,0},{2,3},{3,2},{4,5},{5,4},{6,7},{7,6},{8,9},{9,8},{10,11... | collective-permute-start | bytes 1966088 | tf_op jit(solution)/shard_map/ppermute | solution.py:23
  32.2 0.6 shard_map.87
  32.8 2.4 %collective-permute-start.6 = (bf16[304,256]{1,0:T(8,128)(2,1)S(1)}, bf16[304,256]{1,0:T(8,128)(2,1)S(1)}, u32[]{:S(2)}, u32[]{:S(2)}) collective-permute-start(bf16[304,256]{1,0:T(8,128)(2,1)S(1)} %get-tuple-element.47), channel_id=1, source_target_pairs={{0,1},{1,0},{2,3},{3,2},{4,5},{5,4},{6,7},{7,6},{8,9},{9,8},{10,11... | collective-permute-start | bytes 466952 | tf_op jit(solution)/shard_map/ppermute | solution.py:23
  35.3 0.8 shard_map.85
  36.0 3.7 %collective-permute-start.3 = (bf16[160,256]{1,0:T(8,128)(2,1)S(1)}, bf16[160,256]{1,0:T(8,128)(2,1)S(1)}, u32[]{:S(2)}, u32[]{:S(2)}) collective-permute-start(bf16[160,256]{1,0:T(8,128)(2,1)S(1)} %get-tuple-element.41), channel_id=1, source_target_pairs={{0,64},{16,80},{32,96},{48,112},{64,0},{80,16},{96,32},{112,48},{1... | collective-permute-start | bytes 245768 | tf_op jit(solution)/shard_map/ppermute | solution.py:23
  40.4 3.4 %collective-permute-start.7 = (f32[8,128]{1,0:T(8,128)S(1)}, f32[8,128]{1,0:T(8,128)S(1)}, u32[]{:S(2)}, u32[]{:S(2)}) collective-permute-start(f32[8,128]{1,0:T(8,128)S(1)} %get-tuple-element.49), channel_id=1, source_target_pairs={{0,2},{2,0},{4,6},{6,4},{8,10},{10,8},{12,14},{14,12},{1,3},{3,1},... | collective-permute-start | bytes 12296 | tf_op jit(solution)/shard_map/ppermute | solution.py:23
  44.3 2.6 %collective-permute-start.4 = (bf16[80,256]{1,0:T(8,128)(2,1)S(1)}, bf16[80,256]{1,0:T(8,128)(2,1)S(1)}, u32[]{:S(2)}, u32[]{:S(2)}) collective-permute-start(bf16[80,256]{1,0:T(8,128)(2,1)S(1)} %get-tuple-element.43), channel_id=1, source_target_pairs={{0,128},{16,144},{32,160},{48,176},{64,192},{80,208},{96,224},{112... | collective-permute-start | bytes 122888 | tf_op jit(solution)/shard_map/ppermute | solution.py:23
  47.0 4.0 %collective-permute-start.8 = (f32[8,128]{1,0:T(8,128)S(1)}, f32[8,128]{1,0:T(8,128)S(1)}, u32[]{:S(2)}, u32[]{:S(2)}) collective-permute-start(f32[8,128]{1,0:T(8,128)S(1)} %max.3), channel_id=1, source_target_pairs={{0,6},{2,4},{4,2},{6,0},{8,14},{10,12},{12,10},{14,8},{1,7},{3,5},... | collective-permute-start | bytes 12296 | tf_op jit(solution)/shard_map/ppermute | solution.py:23
  51.6 2.4 %collective-permute-start.13 = (bf16[576,256]{1,0:T(8,128)(2,1)S(1)}, bf16[576,256]{1,0:T(8,128)(2,1)S(1)}, u32[]{:S(2)}, u32[]{:S(2)}) collective-permute-start(bf16[576,256]{1,0:T(8,128)(2,1)S(1)} %get-tuple-element.55.a), channel_id=1, source_target_pairs={{0,2},{2,0},{4,6},{6,4},{8,10},{10,8},{12,14},{14,12},{1,3},{3,1},... | collective-permute-start | bytes 884744 | tf_op jit(solution)/shard_map/ppermute | solution.py:23
  54.0 0.6 shard_map.89
  54.6 7.6 %collective-permute-start.9 = (bf16[96,256]{1,0:T(8,128)(2,1)S(1)}, bf16[96,256]{1,0:T(8,128)(2,1)S(1)}, u32[]{:S(2)}, u32[]{:S(2)}) collective-permute-start(bf16[96,256]{1,0:T(8,128)(2,1)S(1)} %get-tuple-element.50.q), channel_id=1, source_target_pairs={{0,256},{16,272},{32,288},{48,304},{64,320},{80,336},{96,352},{112... | collective-permute-start | bytes 147464 | tf_op jit(solution)/shard_map/ppermute | solution.py:23
  62.2 0.6 shard_map.91.a
  62.8 4.5 %collective-permute-start.18 = (bf16[1152,256]{1,0:T(8,128)(2,1)S(1)}, bf16[1152,256]{1,0:T(8,128)(2,1)S(1)}, u32[]{:S(2)}, u32[]{:S(2)}) collective-permute-start(bf16[1152,256]{1,0:T(8,128)(2,1)S(1)} %shard_map.91.a), channel_id=1, source_target_pairs={{0,6},{2,4},{4,2},{6,0},{8,14},{10,12},{12,10},{14,8},{1,7},{3,5},... | collective-permute-start | bytes 1769480 | tf_op jit(solution)/shard_map/ppermute | solution.py:23
  67.4 1.2 %shard_map.90 = (bf16[96,256]{1,0:T(8,128)(2,1)S(1)}, f32[40,256]{1,0:T(8,128)}, f32[8,256]{1,0:T(8,128)S(1)}) custom-call(s32[5]{0:T(128)S(1)} %stack.23.ix, bf16[96,256]{1,0:T(8,128)(2,1)S(1)} %get-tuple-element.50.q, f32[40,256]{1,0:T(8,128)S(1)} %get-tuple-element.51.p_own, f32[40,256]{1,0:T(8,128)S(1)} %bitcast.17, ...), custom_call_target="tpu_custom_call" | custom-call | flops 14000000000 | tf_op jit(solution)/shard_map/pallas_call | solution.py:31
  68.5 3.2 %collective-permute-start.12 = (bf16[96,256]{1,0:T(8,128)(2,1)S(1)}, bf16[96,256]{1,0:T(8,128)(2,1)S(1)}, u32[]{:S(2)}, u32[]{:S(2)}) collective-permute-start(bf16[96,256]{1,0:T(8,128)(2,1)S(1)} %get-tuple-element.53.f0), channel_id=1, source_target_pairs={{0,192},{16,208},{32,224},{48,240},{64,128},{80,144},{96,160},{112... | collective-permute-start | bytes 147464 | tf_op jit(solution)/shard_map/ppermute | solution.py:23
  71.7 2.7 %collective-permute-start.11 = (bf16[96,256]{1,0:T(8,128)(2,1)S(1)}, bf16[96,256]{1,0:T(8,128)(2,1)S(1)}, u32[]{:S(2)}, u32[]{:S(2)}) collective-permute-start(bf16[96,256]{1,0:T(8,128)(2,1)S(1)} %get-tuple-element.53.f0), channel_id=1, source_target_pairs={{0,128},{16,144},{32,160},{48,176},{64,192},{80,208},{96,224},{112... | collective-permute-start | bytes 147464 | tf_op jit(solution)/shard_map/ppermute | solution.py:23
  74.4 4.3 %collective-permute-start.10 = (bf16[96,256]{1,0:T(8,128)(2,1)S(1)}, bf16[96,256]{1,0:T(8,128)(2,1)S(1)}, u32[]{:S(2)}, u32[]{:S(2)}) collective-permute-start(bf16[96,256]{1,0:T(8,128)(2,1)S(1)} %get-tuple-element.53.f0), channel_id=1, source_target_pairs={{0,64},{16,80},{32,96},{48,112},{64,0},{80,16},{96,32},{112,48},{1... | collective-permute-start | bytes 147464 | tf_op jit(solution)/shard_map/ppermute | solution.py:23
  78.7 3.1 %shard_map.92.rest_0_ = bf16[8,144,1280]{2,1,0:T(8,128)(2,1)} custom-call(s32[4]{0:T(128)S(1)} %get-tuple-element.67.place, bf16[1152,256]{1,0:T(8,128)(2,1)S(1)} %shard_map.91.a, bf16[1280,256]{1,0:T(8,128)(2,1)} %bitcast.9.wa, bf16[1280,256]{1,0:T(8,128)(2,1)S(1)} %collective-permute-done.14.wb), custom_call_target="tpu_custom_call" | custom-call | flops 754974720 | bytes 3500000 | tf_op jit(solution)/shard_map/pallas_call | solution.py:190
  81.8 0.6 shard_map.93
  82.4 2.1 %collective-permute-start.17 = (bf16[336,256]{1,0:T(8,128)(2,1)S(1)}, bf16[336,256]{1,0:T(8,128)(2,1)S(1)}, u32[]{:S(2)}, u32[]{:S(2)}) collective-permute-start(bf16[336,256]{1,0:T(8,128)(2,1)S(1)} %get-tuple-element.59.e0), channel_id=1, source_target_pairs={{0,48},{16,32},{32,16},{48,0},{64,112},{80,96},{96,80},{112,64},{1... | collective-permute-start | bytes 516104 | tf_op jit(solution)/shard_map/ppermute | solution.py:23
  84.5 4.5 %collective-permute-start.16 = (bf16[336,256]{1,0:T(8,128)(2,1)S(1)}, bf16[336,256]{1,0:T(8,128)(2,1)S(1)}, u32[]{:S(2)}, u32[]{:S(2)}) collective-permute-start(bf16[336,256]{1,0:T(8,128)(2,1)S(1)} %get-tuple-element.59.e0), channel_id=1, source_target_pairs={{0,32},{16,48},{32,0},{48,16},{64,96},{80,112},{96,64},{112,80},{1... | collective-permute-start | bytes 516104 | tf_op jit(solution)/shard_map/ppermute | solution.py:23
  89.0 3.2 %collective-permute-start.15 = (bf16[336,256]{1,0:T(8,128)(2,1)S(1)}, bf16[336,256]{1,0:T(8,128)(2,1)S(1)}, u32[]{:S(2)}, u32[]{:S(2)}) collective-permute-start(bf16[336,256]{1,0:T(8,128)(2,1)S(1)} %get-tuple-element.59.e0), channel_id=1, source_target_pairs={{0,16},{16,0},{32,48},{48,32},{64,80},{80,64},{96,112},{112,96},{1... | collective-permute-start | bytes 516104 | tf_op jit(solution)/shard_map/ppermute | solution.py:23
  92.2 3.1 %shard_map.94 = bf16[8,144,1280]{2,1,0:T(8,128)(2,1)} custom-call(s32[4]{0:T(128)S(1)} %get-tuple-element.66.place, bf16[1152,256]{1,0:T(8,128)(2,1)S(1)} %collective-permute-done.18.a, bf16[1280,256]{1,0:T(8,128)(2,1)} %bitcast.9.wa, bf16[1280,256]{1,0:T(8,128)(2,1)S(1)} %collective-permute-done.14.wb, ...), custom_call_target="tpu_custom_call", output_to_operand_aliasing={{}: (4, {})} | custom-call | flops 754974720 | bytes 3500000 | tf_op jit(solution)/shard_map/pallas_call | solution.py:190
  95.3 1.0 %collective-permute-done.15.e1 = bf16[336,256]{1,0:T(8,128)(2,1)S(1)} collective-permute-done((bf16[336,256]{1,0:T(8,128)(2,1)S(1)}, bf16[336,256]{1,0:T(8,128)(2,1)S(1)}, u32[]{:S(2)}, u32[]{:S(2)}) %collective-permute-start.15) | collective-permute-done | bytes 172064 | tf_op jit(solution)/shard_map/ppermute | solution.py:23
  96.3 1.4 %shard_map.95 = (bf16[8,4,40,256]{3,2,1,0:T(8,128)(2,1)}, f32[1,1]{1,0:T(1,128)}) custom-call(s32[5]{0:T(128)S(1)} %stack.23.ix, bf16[336,256]{1,0:T(8,128)(2,1)S(1)} %get-tuple-element.59.e0, bf16[336,256]{1,0:T(8,128)(2,1)S(1)} %collective-permute-done.15.e1, bf16[336,256]{1,0:T(8,128)(2,1)S(1)} %collective-permute-done.16.e2, ...), custom_call_target="tpu_custom_call" | custom-call | flops 500000000 | tf_op jit(solution)/shard_map/pallas_call | solution.py:31
  (32 shorter events, 1.9 us)
Async XLA Ops:
  0.6 39.1 %copy-start.3 = (s32[8]{0:T(128)S(1)}, s32[8]{0:T(128)}, u32[]{:S(2)}) copy-start(s32[8]{0:T(128)} %constant.22.clone) | copy-start | bytes 100
  0.7 1.1 %copy-start = (bf16[1280,256]{1,0:T(8,128)(2,1)S(1)}, bf16[1280,256]{1,0:T(8,128)(2,1)}, u32[]{:S(2)}) copy-start(bf16[1280,256]{1,0:T(8,128)(2,1)} %param.6) | copy-start | bytes 1966084
  1.8 0.9 copy-start.1
  4.1 28.1 %collective-permute-start.5 = (bf16[304,256]{1,0:T(8,128)(2,1)S(1)}, bf16[304,256]{1,0:T(8,128)(2,1)S(1)}, u32[]{:S(2)}, u32[]{:S(2)}) collective-permute-start(bf16[304,256]{1,0:T(8,128)(2,1)S(1)} %get-tuple-element.44.a), channel_id=1, source_target_pairs={{0,8},{2,10},{4,12},{6,14},{8,0},{10,2},{12,4},{14,6},{1,9},{3,11}... | collective-permute-start | bytes 466952 | tf_op jit(solution)/shard_map/ppermute | solution.py:23
  19.9 15.4 %collective-permute-start = (bf16[320,256]{1,0:T(8,128)(2,1)S(1)}, bf16[320,256]{1,0:T(8,128)(2,1)S(1)}, u32[]{:S(2)}, u32[]{:S(2)}) collective-permute-start(bf16[320,256]{1,0:T(8,128)(2,1)S(1)} %get-tuple-element.37), channel_id=1, source_target_pairs={{0,16},{16,0},{32,48},{48,32},{64,80},{80,64},{96,112},{112,96},{1... | collective-permute-start | bytes 491528 | tf_op jit(solution)/shard_map/ppermute | solution.py:23
  22.5 12.7 %collective-permute-start.1 = (bf16[320,256]{1,0:T(8,128)(2,1)S(1)}, bf16[320,256]{1,0:T(8,128)(2,1)S(1)}, u32[]{:S(2)}, u32[]{:S(2)}) collective-permute-start(bf16[320,256]{1,0:T(8,128)(2,1)S(1)} %get-tuple-element.38), channel_id=1, source_target_pairs={{0,32},{16,48},{32,0},{48,16},{64,96},{80,112},{96,64},{112,80},{1... | collective-permute-start | bytes 491528 | tf_op jit(solution)/shard_map/ppermute | solution.py:23
  25.4 9.9 %collective-permute-start.2 = (bf16[320,256]{1,0:T(8,128)(2,1)S(1)}, bf16[320,256]{1,0:T(8,128)(2,1)S(1)}, u32[]{:S(2)}, u32[]{:S(2)}) collective-permute-start(bf16[320,256]{1,0:T(8,128)(2,1)S(1)} %get-tuple-element.39), channel_id=1, source_target_pairs={{0,48},{16,32},{32,16},{48,0},{64,112},{80,96},{96,80},{112,64},{1... | collective-permute-start | bytes 491528 | tf_op jit(solution)/shard_map/ppermute | solution.py:23
  30.3 48.4 %collective-permute-start.14 = (bf16[1280,256]{1,0:T(8,128)(2,1)}, bf16[1280,256]{1,0:T(8,128)(2,1)S(1)}, u32[]{:S(2)}, u32[]{:S(2)}) collective-permute-start(bf16[1280,256]{1,0:T(8,128)(2,1)} %bitcast.9.wa), channel_id=1, source_target_pairs={{0,1},{1,0},{2,3},{3,2},{4,5},{5,4},{6,7},{7,6},{8,9},{9,8},{10,11... | collective-permute-start | bytes 1966088 | tf_op jit(solution)/shard_map/ppermute | solution.py:23
  32.8 21.2 %copy-start.2 = (f32[1,1,40,256]{3,2,1,0:T(8,128)S(1)}, f32[1,1,40,256]{3,2,1,0:T(8,128)}, u32[]{:S(2)}) copy-start(f32[1,1,40,256]{3,2,1,0:T(8,128)} %param.7) | copy-start | bytes 122884
  32.8 6.9 %collective-permute-start.6 = (bf16[304,256]{1,0:T(8,128)(2,1)S(1)}, bf16[304,256]{1,0:T(8,128)(2,1)S(1)}, u32[]{:S(2)}, u32[]{:S(2)}) collective-permute-start(bf16[304,256]{1,0:T(8,128)(2,1)S(1)} %get-tuple-element.47), channel_id=1, source_target_pairs={{0,1},{1,0},{2,3},{3,2},{4,5},{5,4},{6,7},{7,6},{8,9},{9,8},{10,11... | collective-permute-start | bytes 466952 | tf_op jit(solution)/shard_map/ppermute | solution.py:23
  36.0 7.7 %collective-permute-start.3 = (bf16[160,256]{1,0:T(8,128)(2,1)S(1)}, bf16[160,256]{1,0:T(8,128)(2,1)S(1)}, u32[]{:S(2)}, u32[]{:S(2)}) collective-permute-start(bf16[160,256]{1,0:T(8,128)(2,1)S(1)} %get-tuple-element.41), channel_id=1, source_target_pairs={{0,64},{16,80},{32,96},{48,112},{64,0},{80,16},{96,32},{112,48},{1... | collective-permute-start | bytes 245768 | tf_op jit(solution)/shard_map/ppermute | solution.py:23
  40.4 6.6 %collective-permute-start.7 = (f32[8,128]{1,0:T(8,128)S(1)}, f32[8,128]{1,0:T(8,128)S(1)}, u32[]{:S(2)}, u32[]{:S(2)}) collective-permute-start(f32[8,128]{1,0:T(8,128)S(1)} %get-tuple-element.49), channel_id=1, source_target_pairs={{0,2},{2,0},{4,6},{6,4},{8,10},{10,8},{12,14},{14,12},{1,3},{3,1},... | collective-permute-start | bytes 12296 | tf_op jit(solution)/shard_map/ppermute | solution.py:23
  44.3 7.2 %collective-permute-start.4 = (bf16[80,256]{1,0:T(8,128)(2,1)S(1)}, bf16[80,256]{1,0:T(8,128)(2,1)S(1)}, u32[]{:S(2)}, u32[]{:S(2)}) collective-permute-start(bf16[80,256]{1,0:T(8,128)(2,1)S(1)} %get-tuple-element.43), channel_id=1, source_target_pairs={{0,128},{16,144},{32,160},{48,176},{64,192},{80,208},{96,224},{112... | collective-permute-start | bytes 122888 | tf_op jit(solution)/shard_map/ppermute | solution.py:23
  47.0 7.0 %collective-permute-start.8 = (f32[8,128]{1,0:T(8,128)S(1)}, f32[8,128]{1,0:T(8,128)S(1)}, u32[]{:S(2)}, u32[]{:S(2)}) collective-permute-start(f32[8,128]{1,0:T(8,128)S(1)} %max.3), channel_id=1, source_target_pairs={{0,6},{2,4},{4,2},{6,0},{8,14},{10,12},{12,10},{14,8},{1,7},{3,5},... | collective-permute-start | bytes 12296 | tf_op jit(solution)/shard_map/ppermute | solution.py:23
  51.6 10.7 %collective-permute-start.13 = (bf16[576,256]{1,0:T(8,128)(2,1)S(1)}, bf16[576,256]{1,0:T(8,128)(2,1)S(1)}, u32[]{:S(2)}, u32[]{:S(2)}) collective-permute-start(bf16[576,256]{1,0:T(8,128)(2,1)S(1)} %get-tuple-element.55.a), channel_id=1, source_target_pairs={{0,2},{2,0},{4,6},{6,4},{8,10},{10,8},{12,14},{14,12},{1,3},{3,1},... | collective-permute-start | bytes 884744 | tf_op jit(solution)/shard_map/ppermute | solution.py:23
  54.6 12.8 %collective-permute-start.9 = (bf16[96,256]{1,0:T(8,128)(2,1)S(1)}, bf16[96,256]{1,0:T(8,128)(2,1)S(1)}, u32[]{:S(2)}, u32[]{:S(2)}) collective-permute-start(bf16[96,256]{1,0:T(8,128)(2,1)S(1)} %get-tuple-element.50.q), channel_id=1, source_target_pairs={{0,256},{16,272},{32,288},{48,304},{64,320},{80,336},{96,352},{112... | collective-permute-start | bytes 147464 | tf_op jit(solution)/shard_map/ppermute | solution.py:23
  62.8 29.4 %collective-permute-start.18 = (bf16[1152,256]{1,0:T(8,128)(2,1)S(1)}, bf16[1152,256]{1,0:T(8,128)(2,1)S(1)}, u32[]{:S(2)}, u32[]{:S(2)}) collective-permute-start(bf16[1152,256]{1,0:T(8,128)(2,1)S(1)} %shard_map.91.a), channel_id=1, source_target_pairs={{0,6},{2,4},{4,2},{6,0},{8,14},{10,12},{12,10},{14,8},{1,7},{3,5},... | collective-permute-start | bytes 1769480 | tf_op jit(solution)/shard_map/ppermute | solution.py:23
  68.5 13.2 %collective-permute-start.12 = (bf16[96,256]{1,0:T(8,128)(2,1)S(1)}, bf16[96,256]{1,0:T(8,128)(2,1)S(1)}, u32[]{:S(2)}, u32[]{:S(2)}) collective-permute-start(bf16[96,256]{1,0:T(8,128)(2,1)S(1)} %get-tuple-element.53.f0), channel_id=1, source_target_pairs={{0,192},{16,208},{32,224},{48,240},{64,128},{80,144},{96,160},{112... | collective-permute-start | bytes 147464 | tf_op jit(solution)/shard_map/ppermute | solution.py:23
  71.7 10.0 %collective-permute-start.11 = (bf16[96,256]{1,0:T(8,128)(2,1)S(1)}, bf16[96,256]{1,0:T(8,128)(2,1)S(1)}, u32[]{:S(2)}, u32[]{:S(2)}) collective-permute-start(bf16[96,256]{1,0:T(8,128)(2,1)S(1)} %get-tuple-element.53.f0), channel_id=1, source_target_pairs={{0,128},{16,144},{32,160},{48,176},{64,192},{80,208},{96,224},{112... | collective-permute-start | bytes 147464 | tf_op jit(solution)/shard_map/ppermute | solution.py:23
  74.4 7.4 %collective-permute-start.10 = (bf16[96,256]{1,0:T(8,128)(2,1)S(1)}, bf16[96,256]{1,0:T(8,128)(2,1)S(1)}, u32[]{:S(2)}, u32[]{:S(2)}) collective-permute-start(bf16[96,256]{1,0:T(8,128)(2,1)S(1)} %get-tuple-element.53.f0), channel_id=1, source_target_pairs={{0,64},{16,80},{32,96},{48,112},{64,0},{80,16},{96,32},{112,48},{1... | collective-permute-start | bytes 147464 | tf_op jit(solution)/shard_map/ppermute | solution.py:23
  82.4 12.9 %collective-permute-start.17 = (bf16[336,256]{1,0:T(8,128)(2,1)S(1)}, bf16[336,256]{1,0:T(8,128)(2,1)S(1)}, u32[]{:S(2)}, u32[]{:S(2)}) collective-permute-start(bf16[336,256]{1,0:T(8,128)(2,1)S(1)} %get-tuple-element.59.e0), channel_id=1, source_target_pairs={{0,48},{16,32},{32,16},{48,0},{64,112},{80,96},{96,80},{112,64},{1... | collective-permute-start | bytes 516104 | tf_op jit(solution)/shard_map/ppermute | solution.py:23
  84.5 10.8 %collective-permute-start.16 = (bf16[336,256]{1,0:T(8,128)(2,1)S(1)}, bf16[336,256]{1,0:T(8,128)(2,1)S(1)}, u32[]{:S(2)}, u32[]{:S(2)}) collective-permute-start(bf16[336,256]{1,0:T(8,128)(2,1)S(1)} %get-tuple-element.59.e0), channel_id=1, source_target_pairs={{0,32},{16,48},{32,0},{48,16},{64,96},{80,112},{96,64},{112,80},{1... | collective-permute-start | bytes 516104 | tf_op jit(solution)/shard_map/ppermute | solution.py:23
  89.0 7.3 %collective-permute-start.15 = (bf16[336,256]{1,0:T(8,128)(2,1)S(1)}, bf16[336,256]{1,0:T(8,128)(2,1)S(1)}, u32[]{:S(2)}, u32[]{:S(2)}) collective-permute-start(bf16[336,256]{1,0:T(8,128)(2,1)S(1)} %get-tuple-element.59.e0), channel_id=1, source_target_pairs={{0,16},{16,0},{32,48},{48,32},{64,80},{80,64},{96,112},{112,96},{1... | collective-permute-start | bytes 516104 | tf_op jit(solution)/shard_map/ppermute | solution.py:23

commit v7 on v6

--- a/solution.py
+++ b/solution.py
@@ -165,14 +165,20 @@
 
 
 def product_kernel(place, a, wa, wb, *rest):
-    out, buf, sem = rest[-3:]
+    out, buf, w, sem, w_sem = rest[-5:]
     dims = (((1,), (1,)), ((), ()))
     n = 4 * TOK
     copies = []
+    loads = []
     for j in range(wa.shape[0] // COLS):
+        rows = pl.ds(j * COLS, COLS)
+        loads.append(pltpu.make_async_copy(wa.at[rows], w.at[rows], w_sem.at[j]))
+        loads[-1].start()
+    for j, load in enumerate(loads):
         at = slice(j * COLS, (j + 1) * COLS)
-        x = lax.dot_general(a[0:n], wa[at], dims, preferred_element_type=F32)
-        x += lax.dot_general(a[n:], wb[at], dims, preferred_element_type=F32)
+        x = lax.dot_general(a[n:], wb[at], dims, preferred_element_type=F32)
+        load.wait()
+        x += lax.dot_general(a[0:n], w[at], dims, preferred_element_type=F32)
         buf[j] = x.astype(BF16)
         for i in range(4):
             src = buf.at[j, pl.ds(i * TOK, TOK)]
@@ -189,12 +195,14 @@
     args = [place, rows, w, w_other] + ([] if prod is None else [prod])
     return pl.pallas_call(
         product_kernel,
-        in_specs=[SMEM, VMEM, VMEM, VMEM] + [pl.BlockSpec(memory_space=pl.ANY)] * (len(args) - 4),
+        in_specs=[SMEM, VMEM, pl.BlockSpec(memory_space=pl.ANY), VMEM] + [pl.BlockSpec(memory_space=pl.ANY)] * (len(args) - 4),
         out_specs=pl.BlockSpec(memory_space=pl.ANY),
         out_shape=jax.ShapeDtypeStruct((8, TOK, width), BF16),
         scratch_shapes=[
             pltpu.VMEM((blocks, 4 * TOK, COLS), BF16),
+            pltpu.VMEM((width, COLS), BF16),
             pltpu.SemaphoreType.DMA((blocks, 4)),
+            pltpu.SemaphoreType.DMA((blocks,)),
         ],
         input_output_aliases={} if prod is None else {4: 0},
         compiler_params=pltpu.CompilerParams(vmem_limit_bytes=24 * 1024 * 1024),

time: 99.1 us -> 101 us (1.019)
  Pallas kernels: 14.3 us -> 17.7 us
    pallas_call x2, Pallas kernels: 6.13 us -> 9.55 us  [product(): pl.pallas_call(product_kernel, in_specs=[SMEM, VMEM, pl.BlockSpec(memory_...]
  transfers between devices with their start and end apart: 19 -> 19, of which waited for: 2 -> 1; matrix products, arithmetic and copies ran while one was open for 0% -> 0% of each run, Pallas kernels for 12% -> 15%
where the time goes in v7:
time: 101 us; the launch traced here: 100 us
  starting transfers between devices  78.6 us (78%)
  Pallas kernels  17.7 us (18%)
  local copies, waits for them, and re-layouts  2.17 us (2%)
  between operations  1.05 us (1%)
    ppermute x19, starting transfers between devices, swap(): return lax.ppermute(x, axis, [(i, i ^ bit) for i in range(n)])  78.6 us
    pallas_call x2, Pallas kernels, product(): pl.pallas_call(product_kernel, in_specs=[SMEM, VMEM, pl.BlockSpec(memory_...  9.55 us
    pallas_call x10, Pallas kernels, call(): pl.pallas_call(kernel, out_shape=[jax.ShapeDtypeStruct(s, d) for s, d in...  8.19 us
  transfers between devices with their start and end apart: 19, of which 1 were waited for; matrix products, arithmetic and copies ran while one was open for 0% of the time, Pallas kernels for 15%

profile of v7, /device:TPU:24, one launch (start us, length us, event | category | flops | bytes accessed | tf_op | source)
XLA Modules:
  0.0 100.2 jit_solution(9671886475689814842)
XLA Ops:
  0.7 1.1 %copy-done = bf16[1280,256]{1,0:T(8,128)(2,1)S(1)} copy-done((bf16[1280,256]{1,0:T(8,128)(2,1)S(1)}, bf16[1280,256]{1,0:T(8,128)(2,1)}, u32[]{:S(2)}) %copy-start) | copy-done | bytes 655384
  1.8 0.9 copy-done.1
  2.7 1.4 %shard_map.84 = (bf16[320,256]{1,0:T(8,128)(2,1)S(1)}, bf16[320,256]{1,0:T(8,128)(2,1)S(1)}, bf16[320,256]{1,0:T(8,128)(2,1)S(1)}, f32[320,256]{1,0:T(8,128)S(1)...) custom-call(s32[5]{0:T(128)S(1)} %stack.23.ix, bf16[8,4,40,256]{3,2,1,0:T(8,128)(2,1)} %bitcast.5.w, ...), custom_call_target="tpu_custom_call" | custom-call | flops 500000000 | tf_op jit(solution)/shard_map/pallas_call | solution.py:31
  4.1 15.7 %collective-permute-start.5 = (bf16[304,256]{1,0:T(8,128)(2,1)S(1)}, bf16[304,256]{1,0:T(8,128)(2,1)S(1)}, u32[]{:S(2)}, u32[]{:S(2)}) collective-permute-start(bf16[304,256]{1,0:T(8,128)(2,1)S(1)} %get-tuple-element.44.a), channel_id=1, source_target_pairs={{0,8},{2,10},{4,12},{6,14},{8,0},{10,2},{12,4},{14,6},{1,9},{3,11}... | collective-permute-start | bytes 466952 | tf_op jit(solution)/shard_map/ppermute | solution.py:23
  19.9 2.7 %collective-permute-start = (bf16[320,256]{1,0:T(8,128)(2,1)S(1)}, bf16[320,256]{1,0:T(8,128)(2,1)S(1)}, u32[]{:S(2)}, u32[]{:S(2)}) collective-permute-start(bf16[320,256]{1,0:T(8,128)(2,1)S(1)} %get-tuple-element.37), channel_id=1, source_target_pairs={{0,16},{16,0},{32,48},{48,32},{64,80},{80,64},{96,112},{112,96},{1... | collective-permute-start | bytes 491528 | tf_op jit(solution)/shard_map/ppermute | solution.py:23
  22.5 2.8 %collective-permute-start.1 = (bf16[320,256]{1,0:T(8,128)(2,1)S(1)}, bf16[320,256]{1,0:T(8,128)(2,1)S(1)}, u32[]{:S(2)}, u32[]{:S(2)}) collective-permute-start(bf16[320,256]{1,0:T(8,128)(2,1)S(1)} %get-tuple-element.38), channel_id=1, source_target_pairs={{0,32},{16,48},{32,0},{48,16},{64,96},{80,112},{96,64},{112,80},{1... | collective-permute-start | bytes 491528 | tf_op jit(solution)/shard_map/ppermute | solution.py:23
  25.4 4.9 %collective-permute-start.2 = (bf16[320,256]{1,0:T(8,128)(2,1)S(1)}, bf16[320,256]{1,0:T(8,128)(2,1)S(1)}, u32[]{:S(2)}, u32[]{:S(2)}) collective-permute-start(bf16[320,256]{1,0:T(8,128)(2,1)S(1)} %get-tuple-element.39), channel_id=1, source_target_pairs={{0,48},{16,32},{32,16},{48,0},{64,112},{80,96},{96,80},{112,64},{1... | collective-permute-start | bytes 491528 | tf_op jit(solution)/shard_map/ppermute | solution.py:23
  30.3 1.9 %collective-permute-start.14 = (bf16[1280,256]{1,0:T(8,128)(2,1)}, bf16[1280,256]{1,0:T(8,128)(2,1)S(1)}, u32[]{:S(2)}, u32[]{:S(2)}) collective-permute-start(bf16[1280,256]{1,0:T(8,128)(2,1)} %bitcast.9.wa), channel_id=1, source_target_pairs={{0,1},{1,0},{2,3},{3,2},{4,5},{5,4},{6,7},{7,6},{8,9},{9,8},{10,11... | collective-permute-start | bytes 1966088 | tf_op jit(solution)/shard_map/ppermute | solution.py:23
  32.2 0.6 shard_map.87
  32.8 2.4 %collective-permute-start.6 = (bf16[304,256]{1,0:T(8,128)(2,1)S(1)}, bf16[304,256]{1,0:T(8,128)(2,1)S(1)}, u32[]{:S(2)}, u32[]{:S(2)}) collective-permute-start(bf16[304,256]{1,0:T(8,128)(2,1)S(1)} %get-tuple-element.47), channel_id=1, source_target_pairs={{0,1},{1,0},{2,3},{3,2},{4,5},{5,4},{6,7},{7,6},{8,9},{9,8},{10,11... | collective-permute-start | bytes 466952 | tf_op jit(solution)/shard_map/ppermute | solution.py:23
  35.3 0.8 shard_map.85
  36.0 3.7 %collective-permute-start.3 = (bf16[160,256]{1,0:T(8,128)(2,1)S(1)}, bf16[160,256]{1,0:T(8,128)(2,1)S(1)}, u32[]{:S(2)}, u32[]{:S(2)}) collective-permute-start(bf16[160,256]{1,0:T(8,128)(2,1)S(1)} %get-tuple-element.41), channel_id=1, source_target_pairs={{0,64},{16,80},{32,96},{48,112},{64,0},{80,16},{96,32},{112,48},{1... | collective-permute-start | bytes 245768 | tf_op jit(solution)/shard_map/ppermute | solution.py:23
  39.8 0.6 shard_map.88
  40.4 3.4 %collective-permute-start.7 = (f32[8,128]{1,0:T(8,128)S(1)}, f32[8,128]{1,0:T(8,128)S(1)}, u32[]{:S(2)}, u32[]{:S(2)}) collective-permute-start(f32[8,128]{1,0:T(8,128)S(1)} %get-tuple-element.49), channel_id=1, source_target_pairs={{0,2},{2,0},{4,6},{6,4},{8,10},{10,8},{12,14},{14,12},{1,3},{3,1},... | collective-permute-start | bytes 12296 | tf_op jit(solution)/shard_map/ppermute | solution.py:23
  44.3 2.6 %collective-permute-start.4 = (bf16[80,256]{1,0:T(8,128)(2,1)S(1)}, bf16[80,256]{1,0:T(8,128)(2,1)S(1)}, u32[]{:S(2)}, u32[]{:S(2)}) collective-permute-start(bf16[80,256]{1,0:T(8,128)(2,1)S(1)} %get-tuple-element.43), channel_id=1, source_target_pairs={{0,128},{16,144},{32,160},{48,176},{64,192},{80,208},{96,224},{112... | collective-permute-start | bytes 122888 | tf_op jit(solution)/shard_map/ppermute | solution.py:23
  47.0 4.0 %collective-permute-start.8 = (f32[8,128]{1,0:T(8,128)S(1)}, f32[8,128]{1,0:T(8,128)S(1)}, u32[]{:S(2)}, u32[]{:S(2)}) collective-permute-start(f32[8,128]{1,0:T(8,128)S(1)} %max.3), channel_id=1, source_target_pairs={{0,6},{2,4},{4,2},{6,0},{8,14},{10,12},{12,10},{14,8},{1,7},{3,5},... | collective-permute-start | bytes 12296 | tf_op jit(solution)/shard_map/ppermute | solution.py:23
  51.6 2.4 %collective-permute-start.13 = (bf16[576,256]{1,0:T(8,128)(2,1)S(1)}, bf16[576,256]{1,0:T(8,128)(2,1)S(1)}, u32[]{:S(2)}, u32[]{:S(2)}) collective-permute-start(bf16[576,256]{1,0:T(8,128)(2,1)S(1)} %get-tuple-element.55.a), channel_id=1, source_target_pairs={{0,2},{2,0},{4,6},{6,4},{8,10},{10,8},{12,14},{14,12},{1,3},{3,1},... | collective-permute-start | bytes 884744 | tf_op jit(solution)/shard_map/ppermute | solution.py:23
  54.0 0.6 shard_map.89
  54.6 7.6 %collective-permute-start.9 = (bf16[96,256]{1,0:T(8,128)(2,1)S(1)}, bf16[96,256]{1,0:T(8,128)(2,1)S(1)}, u32[]{:S(2)}, u32[]{:S(2)}) collective-permute-start(bf16[96,256]{1,0:T(8,128)(2,1)S(1)} %get-tuple-element.50.q), channel_id=1, source_target_pairs={{0,256},{16,272},{32,288},{48,304},{64,320},{80,336},{96,352},{112... | collective-permute-start | bytes 147464 | tf_op jit(solution)/shard_map/ppermute | solution.py:23
  62.2 0.6 shard_map.91.a
  62.8 4.5 %collective-permute-start.18 = (bf16[1152,256]{1,0:T(8,128)(2,1)S(1)}, bf16[1152,256]{1,0:T(8,128)(2,1)S(1)}, u32[]{:S(2)}, u32[]{:S(2)}) collective-permute-start(bf16[1152,256]{1,0:T(8,128)(2,1)S(1)} %shard_map.91.a), channel_id=1, source_target_pairs={{0,6},{2,4},{4,2},{6,0},{8,14},{10,12},{12,10},{14,8},{1,7},{3,5},... | collective-permute-start | bytes 1769480 | tf_op jit(solution)/shard_map/ppermute | solution.py:23
  67.4 1.2 %shard_map.90 = (bf16[96,256]{1,0:T(8,128)(2,1)S(1)}, f32[40,256]{1,0:T(8,128)}, f32[8,256]{1,0:T(8,128)S(1)}) custom-call(s32[5]{0:T(128)S(1)} %stack.23.ix, bf16[96,256]{1,0:T(8,128)(2,1)S(1)} %get-tuple-element.50.q, f32[40,256]{1,0:T(8,128)S(1)} %get-tuple-element.51.p_own, f32[40,256]{1,0:T(8,128)S(1)} %bitcast.17, ...), custom_call_target="tpu_custom_call" | custom-call | flops 14000000000 | tf_op jit(solution)/shard_map/pallas_call | solution.py:31
  68.5 3.2 %collective-permute-start.12 = (bf16[96,256]{1,0:T(8,128)(2,1)S(1)}, bf16[96,256]{1,0:T(8,128)(2,1)S(1)}, u32[]{:S(2)}, u32[]{:S(2)}) collective-permute-start(bf16[96,256]{1,0:T(8,128)(2,1)S(1)} %get-tuple-element.53.f0), channel_id=1, source_target_pairs={{0,192},{16,208},{32,224},{48,240},{64,128},{80,144},{96,160},{112... | collective-permute-start | bytes 147464 | tf_op jit(solution)/shard_map/ppermute | solution.py:23
  71.7 2.7 %collective-permute-start.11 = (bf16[96,256]{1,0:T(8,128)(2,1)S(1)}, bf16[96,256]{1,0:T(8,128)(2,1)S(1)}, u32[]{:S(2)}, u32[]{:S(2)}) collective-permute-start(bf16[96,256]{1,0:T(8,128)(2,1)S(1)} %get-tuple-element.53.f0), channel_id=1, source_target_pairs={{0,128},{16,144},{32,160},{48,176},{64,192},{80,208},{96,224},{112... | collective-permute-start | bytes 147464 | tf_op jit(solution)/shard_map/ppermute | solution.py:23
  74.4 4.3 %collective-permute-start.10 = (bf16[96,256]{1,0:T(8,128)(2,1)S(1)}, bf16[96,256]{1,0:T(8,128)(2,1)S(1)}, u32[]{:S(2)}, u32[]{:S(2)}) collective-permute-start(bf16[96,256]{1,0:T(8,128)(2,1)S(1)} %get-tuple-element.53.f0), channel_id=1, source_target_pairs={{0,64},{16,80},{32,96},{48,112},{64,0},{80,16},{96,32},{112,48},{1... | collective-permute-start | bytes 147464 | tf_op jit(solution)/shard_map/ppermute | solution.py:23
  78.7 4.8 %shard_map.92.rest_0_ = bf16[8,144,1280]{2,1,0:T(8,128)(2,1)} custom-call(s32[4]{0:T(128)S(1)} %get-tuple-element.67.place, bf16[1152,256]{1,0:T(8,128)(2,1)S(1)} %shard_map.91.a, bf16[1280,256]{1,0:T(8,128)(2,1)} %bitcast.9.wa, bf16[1280,256]{1,0:T(8,128)(2,1)S(1)} %collective-permute-done.14.wb), custom_call_target="tpu_custom_call" | custom-call | flops 754974720 | bytes 3500000 | tf_op jit(solution)/shard_map/pallas_call | solution.py:196
  83.5 0.6 shard_map.93
  84.1 2.1 %collective-permute-start.17 = (bf16[336,256]{1,0:T(8,128)(2,1)S(1)}, bf16[336,256]{1,0:T(8,128)(2,1)S(1)}, u32[]{:S(2)}, u32[]{:S(2)}) collective-permute-start(bf16[336,256]{1,0:T(8,128)(2,1)S(1)} %get-tuple-element.59.e0), channel_id=1, source_target_pairs={{0,48},{16,32},{32,16},{48,0},{64,112},{80,96},{96,80},{112,64},{1... | collective-permute-start | bytes 516104 | tf_op jit(solution)/shard_map/ppermute | solution.py:23
  86.2 4.5 %collective-permute-start.16 = (bf16[336,256]{1,0:T(8,128)(2,1)S(1)}, bf16[336,256]{1,0:T(8,128)(2,1)S(1)}, u32[]{:S(2)}, u32[]{:S(2)}) collective-permute-start(bf16[336,256]{1,0:T(8,128)(2,1)S(1)} %get-tuple-element.59.e0), channel_id=1, source_target_pairs={{0,32},{16,48},{32,0},{48,16},{64,96},{80,112},{96,64},{112,80},{1... | collective-permute-start | bytes 516104 | tf_op jit(solution)/shard_map/ppermute | solution.py:23
  90.7 3.2 %collective-permute-start.15 = (bf16[336,256]{1,0:T(8,128)(2,1)S(1)}, bf16[336,256]{1,0:T(8,128)(2,1)S(1)}, u32[]{:S(2)}, u32[]{:S(2)}) collective-permute-start(bf16[336,256]{1,0:T(8,128)(2,1)S(1)} %get-tuple-element.59.e0), channel_id=1, source_target_pairs={{0,16},{16,0},{32,48},{48,32},{64,80},{80,64},{96,112},{112,96},{1... | collective-permute-start | bytes 516104 | tf_op jit(solution)/shard_map/ppermute | solution.py:23
  93.9 4.8 %shard_map.94 = bf16[8,144,1280]{2,1,0:T(8,128)(2,1)} custom-call(s32[4]{0:T(128)S(1)} %get-tuple-element.66.place, bf16[1152,256]{1,0:T(8,128)(2,1)S(1)} %collective-permute-done.18.a, bf16[1280,256]{1,0:T(8,128)(2,1)} %bitcast.9.wa, bf16[1280,256]{1,0:T(8,128)(2,1)S(1)} %collective-permute-done.14.wb, ...), custom_call_target="tpu_custom_call", output_to_operand_aliasing={{}: (4, {})} | custom-call | flops 754974720 | bytes 3500000 | tf_op jit(solution)/shard_map/pallas_call | solution.py:196
  98.8 1.4 %shard_map.95 = (bf16[8,4,40,256]{3,2,1,0:T(8,128)(2,1)}, f32[1,1]{1,0:T(1,128)}) custom-call(s32[5]{0:T(128)S(1)} %stack.23.ix, bf16[336,256]{1,0:T(8,128)(2,1)S(1)} %get-tuple-element.59.e0, bf16[336,256]{1,0:T(8,128)(2,1)S(1)} %collective-permute-done.15.e1, bf16[336,256]{1,0:T(8,128)(2,1)S(1)} %collective-permute-done.16.e2, ...), custom_call_target="tpu_custom_call" | custom-call | flops 500000000 | tf_op jit(solution)/shard_map/pallas_call | solution.py:31
  (32 shorter events, 1.3 us)
Async XLA Ops:
  0.6 39.1 %copy-start.3 = (s32[8]{0:T(128)S(1)}, s32[8]{0:T(128)}, u32[]{:S(2)}) copy-start(s32[8]{0:T(128)} %constant.22.clone) | copy-start | bytes 100
  0.7 1.1 %copy-start = (bf16[1280,256]{1,0:T(8,128)(2,1)S(1)}, bf16[1280,256]{1,0:T(8,128)(2,1)}, u32[]{:S(2)}) copy-start(bf16[1280,256]{1,0:T(8,128)(2,1)} %param.6) | copy-start | bytes 1966084
  1.8 0.9 copy-start.1
  4.1 28.1 %collective-permute-start.5 = (bf16[304,256]{1,0:T(8,128)(2,1)S(1)}, bf16[304,256]{1,0:T(8,128)(2,1)S(1)}, u32[]{:S(2)}, u32[]{:S(2)}) collective-permute-start(bf16[304,256]{1,0:T(8,128)(2,1)S(1)} %get-tuple-element.44.a), channel_id=1, source_target_pairs={{0,8},{2,10},{4,12},{6,14},{8,0},{10,2},{12,4},{14,6},{1,9},{3,11}... | collective-permute-start | bytes 466952 | tf_op jit(solution)/shard_map/ppermute | solution.py:23
  19.9 15.4 %collective-permute-start = (bf16[320,256]{1,0:T(8,128)(2,1)S(1)}, bf16[320,256]{1,0:T(8,128)(2,1)S(1)}, u32[]{:S(2)}, u32[]{:S(2)}) collective-permute-start(bf16[320,256]{1,0:T(8,128)(2,1)S(1)} %get-tuple-element.37), channel_id=1, source_target_pairs={{0,16},{16,0},{32,48},{48,32},{64,80},{80,64},{96,112},{112,96},{1... | collective-permute-start | bytes 491528 | tf_op jit(solution)/shard_map/ppermute | solution.py:23
  22.5 12.7 %collective-permute-start.1 = (bf16[320,256]{1,0:T(8,128)(2,1)S(1)}, bf16[320,256]{1,0:T(8,128)(2,1)S(1)}, u32[]{:S(2)}, u32[]{:S(2)}) collective-permute-start(bf16[320,256]{1,0:T(8,128)(2,1)S(1)} %get-tuple-element.38), channel_id=1, source_target_pairs={{0,32},{16,48},{32,0},{48,16},{64,96},{80,112},{96,64},{112,80},{1... | collective-permute-start | bytes 491528 | tf_op jit(solution)/shard_map/ppermute | solution.py:23
  25.4 9.9 %collective-permute-start.2 = (bf16[320,256]{1,0:T(8,128)(2,1)S(1)}, bf16[320,256]{1,0:T(8,128)(2,1)S(1)}, u32[]{:S(2)}, u32[]{:S(2)}) collective-permute-start(bf16[320,256]{1,0:T(8,128)(2,1)S(1)} %get-tuple-element.39), channel_id=1, source_target_pairs={{0,48},{16,32},{32,16},{48,0},{64,112},{80,96},{96,80},{112,64},{1... | collective-permute-start | bytes 491528 | tf_op jit(solution)/shard_map/ppermute | solution.py:23
  30.3 48.4 %collective-permute-start.14 = (bf16[1280,256]{1,0:T(8,128)(2,1)}, bf16[1280,256]{1,0:T(8,128)(2,1)S(1)}, u32[]{:S(2)}, u32[]{:S(2)}) collective-permute-start(bf16[1280,256]{1,0:T(8,128)(2,1)} %bitcast.9.wa), channel_id=1, source_target_pairs={{0,1},{1,0},{2,3},{3,2},{4,5},{5,4},{6,7},{7,6},{8,9},{9,8},{10,11... | collective-permute-start | bytes 1966088 | tf_op jit(solution)/shard_map/ppermute | solution.py:23
  32.8 21.2 %copy-start.2 = (f32[1,1,40,256]{3,2,1,0:T(8,128)S(1)}, f32[1,1,40,256]{3,2,1,0:T(8,128)}, u32[]{:S(2)}) copy-start(f32[1,1,40,256]{3,2,1,0:T(8,128)} %param.7) | copy-start | bytes 122884
  32.8 6.9 %collective-permute-start.6 = (bf16[304,256]{1,0:T(8,128)(2,1)S(1)}, bf16[304,256]{1,0:T(8,128)(2,1)S(1)}, u32[]{:S(2)}, u32[]{:S(2)}) collective-permute-start(bf16[304,256]{1,0:T(8,128)(2,1)S(1)} %get-tuple-element.47), channel_id=1, source_target_pairs={{0,1},{1,0},{2,3},{3,2},{4,5},{5,4},{6,7},{7,6},{8,9},{9,8},{10,11... | collective-permute-start | bytes 466952 | tf_op jit(solution)/shard_map/ppermute | solution.py:23
  36.0 7.7 %collective-permute-start.3 = (bf16[160,256]{1,0:T(8,128)(2,1)S(1)}, bf16[160,256]{1,0:T(8,128)(2,1)S(1)}, u32[]{:S(2)}, u32[]{:S(2)}) collective-permute-start(bf16[160,256]{1,0:T(8,128)(2,1)S(1)} %get-tuple-element.41), channel_id=1, source_target_pairs={{0,64},{16,80},{32,96},{48,112},{64,0},{80,16},{96,32},{112,48},{1... | collective-permute-start | bytes 245768 | tf_op jit(solution)/shard_map/ppermute | solution.py:23
  40.4 6.6 %collective-permute-start.7 = (f32[8,128]{1,0:T(8,128)S(1)}, f32[8,128]{1,0:T(8,128)S(1)}, u32[]{:S(2)}, u32[]{:S(2)}) collective-permute-start(f32[8,128]{1,0:T(8,128)S(1)} %get-tuple-element.49), channel_id=1, source_target_pairs={{0,2},{2,0},{4,6},{6,4},{8,10},{10,8},{12,14},{14,12},{1,3},{3,1},... | collective-permute-start | bytes 12296 | tf_op jit(solution)/shard_map/ppermute | solution.py:23
  44.3 7.2 %collective-permute-start.4 = (bf16[80,256]{1,0:T(8,128)(2,1)S(1)}, bf16[80,256]{1,0:T(8,128)(2,1)S(1)}, u32[]{:S(2)}, u32[]{:S(2)}) collective-permute-start(bf16[80,256]{1,0:T(8,128)(2,1)S(1)} %get-tuple-element.43), channel_id=1, source_target_pairs={{0,128},{16,144},{32,160},{48,176},{64,192},{80,208},{96,224},{112... | collective-permute-start | bytes 122888 | tf_op jit(solution)/shard_map/ppermute | solution.py:23
  47.0 7.0 %collective-permute-start.8 = (f32[8,128]{1,0:T(8,128)S(1)}, f32[8,128]{1,0:T(8,128)S(1)}, u32[]{:S(2)}, u32[]{:S(2)}) collective-permute-start(f32[8,128]{1,0:T(8,128)S(1)} %max.3), channel_id=1, source_target_pairs={{0,6},{2,4},{4,2},{6,0},{8,14},{10,12},{12,10},{14,8},{1,7},{3,5},... | collective-permute-start | bytes 12296 | tf_op jit(solution)/shard_map/ppermute | solution.py:23
  51.6 10.7 %collective-permute-start.13 = (bf16[576,256]{1,0:T(8,128)(2,1)S(1)}, bf16[576,256]{1,0:T(8,128)(2,1)S(1)}, u32[]{:S(2)}, u32[]{:S(2)}) collective-permute-start(bf16[576,256]{1,0:T(8,128)(2,1)S(1)} %get-tuple-element.55.a), channel_id=1, source_target_pairs={{0,2},{2,0},{4,6},{6,4},{8,10},{10,8},{12,14},{14,12},{1,3},{3,1},... | collective-permute-start | bytes 884744 | tf_op jit(solution)/shard_map/ppermute | solution.py:23
  54.6 12.8 %collective-permute-start.9 = (bf16[96,256]{1,0:T(8,128)(2,1)S(1)}, bf16[96,256]{1,0:T(8,128)(2,1)S(1)}, u32[]{:S(2)}, u32[]{:S(2)}) collective-permute-start(bf16[96,256]{1,0:T(8,128)(2,1)S(1)} %get-tuple-element.50.q), channel_id=1, source_target_pairs={{0,256},{16,272},{32,288},{48,304},{64,320},{80,336},{96,352},{112... | collective-permute-start | bytes 147464 | tf_op jit(solution)/shard_map/ppermute | solution.py:23
  62.8 31.1 %collective-permute-start.18 = (bf16[1152,256]{1,0:T(8,128)(2,1)S(1)}, bf16[1152,256]{1,0:T(8,128)(2,1)S(1)}, u32[]{:S(2)}, u32[]{:S(2)}) collective-permute-start(bf16[1152,256]{1,0:T(8,128)(2,1)S(1)} %shard_map.91.a), channel_id=1, source_target_pairs={{0,6},{2,4},{4,2},{6,0},{8,14},{10,12},{12,10},{14,8},{1,7},{3,5},... | collective-permute-start | bytes 1769480 | tf_op jit(solution)/shard_map/ppermute | solution.py:23
  68.5 14.9 %collective-permute-start.12 = (bf16[96,256]{1,0:T(8,128)(2,1)S(1)}, bf16[96,256]{1,0:T(8,128)(2,1)S(1)}, u32[]{:S(2)}, u32[]{:S(2)}) collective-permute-start(bf16[96,256]{1,0:T(8,128)(2,1)S(1)} %get-tuple-element.53.f0), channel_id=1, source_target_pairs={{0,192},{16,208},{32,224},{48,240},{64,128},{80,144},{96,160},{112... | collective-permute-start | bytes 147464 | tf_op jit(solution)/shard_map/ppermute | solution.py:23
  71.7 11.7 %collective-permute-start.11 = (bf16[96,256]{1,0:T(8,128)(2,1)S(1)}, bf16[96,256]{1,0:T(8,128)(2,1)S(1)}, u32[]{:S(2)}, u32[]{:S(2)}) collective-permute-start(bf16[96,256]{1,0:T(8,128)(2,1)S(1)} %get-tuple-element.53.f0), channel_id=1, source_target_pairs={{0,128},{16,144},{32,160},{48,176},{64,192},{80,208},{96,224},{112... | collective-permute-start | bytes 147464 | tf_op jit(solution)/shard_map/ppermute | solution.py:23
  74.4 9.1 %collective-permute-start.10 = (bf16[96,256]{1,0:T(8,128)(2,1)S(1)}, bf16[96,256]{1,0:T(8,128)(2,1)S(1)}, u32[]{:S(2)}, u32[]{:S(2)}) collective-permute-start(bf16[96,256]{1,0:T(8,128)(2,1)S(1)} %get-tuple-element.53.f0), channel_id=1, source_target_pairs={{0,64},{16,80},{32,96},{48,112},{64,0},{80,16},{96,32},{112,48},{1... | collective-permute-start | bytes 147464 | tf_op jit(solution)/shard_map/ppermute | solution.py:23
  84.1 14.6 %collective-permute-start.17 = (bf16[336,256]{1,0:T(8,128)(2,1)S(1)}, bf16[336,256]{1,0:T(8,128)(2,1)S(1)}, u32[]{:S(2)}, u32[]{:S(2)}) collective-permute-start(bf16[336,256]{1,0:T(8,128)(2,1)S(1)} %get-tuple-element.59.e0), channel_id=1, source_target_pairs={{0,48},{16,32},{32,16},{48,0},{64,112},{80,96},{96,80},{112,64},{1... | collective-permute-start | bytes 516104 | tf_op jit(solution)/shard_map/ppermute | solution.py:23
  86.2 12.5 %collective-permute-start.16 = (bf16[336,256]{1,0:T(8,128)(2,1)S(1)}, bf16[336,256]{1,0:T(8,128)(2,1)S(1)}, u32[]{:S(2)}, u32[]{:S(2)}) collective-permute-start(bf16[336,256]{1,0:T(8,128)(2,1)S(1)} %get-tuple-element.59.e0), channel_id=1, source_target_pairs={{0,32},{16,48},{32,0},{48,16},{64,96},{80,112},{96,64},{112,80},{1... | collective-permute-start | bytes 516104 | tf_op jit(solution)/shard_map/ppermute | solution.py:23
  90.7 8.0 %collective-permute-start.15 = (bf16[336,256]{1,0:T(8,128)(2,1)S(1)}, bf16[336,256]{1,0:T(8,128)(2,1)S(1)}, u32[]{:S(2)}, u32[]{:S(2)}) collective-permute-start(bf16[336,256]{1,0:T(8,128)(2,1)S(1)} %get-tuple-element.59.e0), channel_id=1, source_target_pairs={{0,16},{16,0},{32,48},{48,32},{64,80},{80,64},{96,112},{112,96},{1... | collective-permute-start | bytes 516104 | tf_op jit(solution)/shard_map/ppermute | solution.py:23
